TPU v7x, 32 devices: a whole 2x2x4 slice. The times are simulated.
32 devices in a mesh: rows: 8 (over z, y), imgs: 4 (over x, core).
Axes of the slice: x: 2, y: 2, z: 4, core: 2. Of those that a mesh axis runs over, the one named last changes fastest.
Arguments:
- image_in: bfloat16 [16, 32, 32, 384], P('imgs', 'rows'), may hold values from -34 to 34
- condition: bfloat16 [16, 148], P('imgs'), may hold values from -5 to 5
- group_counts: int32 [4], replicated, may hold values from 1 to 4, as said below
- out_cotangent: bfloat16 [16, 64, 64, 192], P('imgs', 'rows'), may hold values from -6 to 6
- power_vectors: float32 [3, 192], replicated, may hold values from -5 to 5
- conv1_weight: float32 [3456, 192], P('rows'), may hold values from -0.109375 to 0.109375
- conv2_weight: float32 [1728, 192], P('rows'), may hold values from -0.15625 to 0.15625
- skip_weight: float32 [384, 192], P('rows'), may hold values from -0.3125 to 0.3125
- cond_weight: float32 [148, 1152], P(None, 'rows'), may hold values from -0.25 to 0.25
- out_bias: float32 [192], P('rows'), may hold values from -1.5 to 1.5
- conv1_first: float32 [3456, 192], P('rows'), may hold values from -1024 to 1024
- conv2_first: float32 [1728, 192], P('rows'), may hold values from -1024 to 1024
- skip_first: float32 [384, 192], P('rows'), may hold values from -1024 to 1024
- cond_first: float32 [148, 1152], P(None, 'rows'), may hold values from -1024 to 1024
- bias_first: float32 [192], P('rows'), may hold values from -1024 to 1024
- conv1_second: float32 [3456, 192], P('rows'), may hold values from 0 to 65536, as said below
- conv2_second: float32 [1728, 192], P('rows'), may hold values from 0 to 65536, as said below
- skip_second: float32 [384, 192], P('rows'), may hold values from 0 to 65536, as said below
- cond_second: float32 [148, 1152], P(None, 'rows'), may hold values from 0 to 65536, as said below
- bias_second: float32 [192], P('rows'), may hold values from 0 to 65536, as said below
Outputs:
- out_image: bfloat16 [16, 64, 64, 192], P('imgs', 'rows')
- image_grad: float32 [16, 32, 32, 384], P('imgs', 'rows')
- conv1_new: float32 [3456, 192], P('rows')
- conv1_moment: float32 [3456, 192], P('rows')
- conv1_square: float32 [3456, 192], P('rows')
- conv2_new: float32 [1728, 192], P('rows')
- conv2_moment: float32 [1728, 192], P('rows')
- conv2_square: float32 [1728, 192], P('rows')
- skip_new: float32 [384, 192], P('rows')
- skip_moment: float32 [384, 192], P('rows')
- skip_square: float32 [384, 192], P('rows')
- cond_new: float32 [148, 1152], P(None, 'rows')
- cond_moment: float32 [148, 1152], P(None, 'rows')
- cond_square: float32 [148, 1152], P(None, 'rows')
- bias_new: float32 [192], P('rows')
- bias_moment: float32 [192], P('rows')
- bias_square: float32 [192], P('rows')
Inputs may be any that keep to these rules, and one draw needn't show every extreme that they name: Image group g holds live images in its first group_counts[g] slots; some group is full and some has the fewest. `conv1_second`: Positive. `conv2_second`: Positive. `skip_second`: Positive. `cond_second`: Positive. `bias_second`: Positive.
All inputs are finite; a program needn't handle non-finite values.
Results may differ from a plain program's by a relative error of at most 0.0015.
The roundings to bfloat16 on the way count: a program that leaves them out, or rounds other values in their place, can miss the bound.
Values may be sent and summed in bfloat16 or wider, within the bound.
No kernel may reach another device: no remote copies, remote signals or barrier semaphores. Data moves between devices by JAX's collectives and lax.ppermute only.
A program may use at most 128 MiB of HBM per device.

v0:
```python
import jax
import jax.numpy as jnp
from jax import lax
from jax.sharding import PartitionSpec as P

STEP = 10


precise = lax.Precision.HIGHEST
NORM_EPS = 1e-05
BETA_ONE = 0.9
BETA_TWO = 0.999
ADAM_EPS = 1e-08
DECAY_RATE = 0.01
LEARN_RATES = (0.02, 0.02, 0.05, 0.03, 0.15)


def with_halo(array, sides, width):
    for axis, dim in sides:
        devices, length = (lax.axis_size(axis), array.shape[dim])
        up = [(i, (i + 1) % devices) for i in range(devices - 1)]
        down = [(j, i) for i, j in up]
        last = lax.slice_in_dim(array, length - width, length, axis=dim)
        initial = lax.slice_in_dim(array, 0, width, axis=dim)
        before = lax.ppermute(last, axis, up)
        after = lax.ppermute(initial, axis, down)
        array = jnp.concatenate([before, array, after], axis=dim)
    return array


def upsample(values):
    return jnp.repeat(jnp.repeat(values, 2, axis=1), 2, axis=2)


def pool_pairs(values):
    shape = values.shape
    return jnp.sum(
        values.reshape(shape[0], shape[1] // 2, 2, shape[2] // 2, 2, shape[3]), axis=(2, 4)
    )


def conv_rows(halo_in, kernel):
    return lax.conv_general_dilated(
        halo_in,
        kernel,
        (1, 1),
        ((0, 0), (1, 1)),
        dimension_numbers=("NHWC", "HWIO", "NHWC"),
        preferred_element_type=jnp.float32,
    )


def flipped(kernel):
    return jnp.transpose(jnp.flip(kernel, (0, 1)), (0, 1, 3, 2))


def silu_slope(values):
    sigmoid_val = jax.nn.sigmoid(values)
    return sigmoid_val * (1.0 + values * (1.0 - sigmoid_val))


def tap_grads(halo_in, grad_out):
    padded = jnp.pad(halo_in, ((0, 0), (0, 0), (1, 1), (0, 0)))
    height = grad_out.shape[1]
    width_out = grad_out.shape[2]
    tap_parts = [
        jnp.einsum(
            "irwc,irwo->co",
            padded[:, tap_row : tap_row + height, tap_col : tap_col + width_out],
            grad_out,
            preferred_element_type=jnp.float32,
        )
        for tap_row in range(3)
        for tap_col in range(3)
    ]
    return jnp.concatenate(tap_parts, axis=0)


def power_pair(weight_low, vector):
    weight_full = weight_low.astype(jnp.float32)
    column = jnp.dot(weight_full, vector, precision=precise)
    left_vec = column * lax.rsqrt(jnp.sum(column * column))
    row_vec = jnp.dot(left_vec, weight_full, precision=precise)
    right_vec = row_vec * lax.rsqrt(jnp.sum(row_vec * row_vec))
    sigma = jnp.sum(weight_full * jnp.outer(left_vec, right_vec))
    return (left_vec, right_vec, sigma)


def finish_norm(values, sum_val, square_sum, count_all, scales, shifts):
    mean_val = sum_val / count_all
    square_val = square_sum / count_all
    rstd_val = lax.rsqrt(square_val - mean_val * mean_val + NORM_EPS)
    normed = (values - mean_val) * rstd_val
    return (normed, rstd_val, scales[:, None, None, :] * normed + shifts[:, None, None, :])


def adamw(weight, first_old, second, gradient, learn_rate):
    first_new = BETA_ONE * first_old + (1.0 - BETA_ONE) * gradient
    second_new = BETA_TWO * second + (1.0 - BETA_TWO) * gradient * gradient
    first_hat = first_new / (1.0 - BETA_ONE**STEP)
    second_hat = second_new / (1.0 - BETA_TWO**STEP)
    weight_new = weight - learn_rate * (
        first_hat / (jnp.sqrt(second_hat) + ADAM_EPS) + DECAY_RATE * weight
    )
    return (weight_new, first_new, second_new)


def own_rows(whole_vals, row_pos, size, axis_dim):
    return lax.dynamic_slice_in_dim(whole_vals, row_pos * size, size, axis_dim)


def body(
    image_in,
    condition,
    group_counts,
    out_cotangent,
    power_vectors,
    conv1_weight,
    conv2_weight,
    skip_weight,
    cond_weight,
    out_bias,
    conv1_first,
    conv2_first,
    skip_first,
    cond_first,
    bias_first,
    conv1_second,
    conv2_second,
    skip_second,
    cond_second,
    bias_second,
):
    low_one, low_two, low_skip, low_cond, low_bias = (
        lax.all_gather(conv1_weight.astype(jnp.bfloat16), "rows", axis=0, tiled=True),
        lax.all_gather(conv2_weight.astype(jnp.bfloat16), "rows", axis=0, tiled=True),
        lax.all_gather(skip_weight.astype(jnp.bfloat16), "rows", axis=0, tiled=True),
        lax.all_gather(cond_weight.astype(jnp.bfloat16), "rows", axis=1, tiled=True),
        lax.all_gather(out_bias.astype(jnp.bfloat16), "rows", axis=0, tiled=True),
    )
    chan_in = image_in.shape[3]
    chan_out = out_cotangent.shape[3]
    left_one, right_one, sigma_one = power_pair(low_one, power_vectors[0])
    left_two, right_two, sigma_two = power_pair(low_two, power_vectors[1])
    left_skip, right_skip, sigma_skip = power_pair(low_skip, power_vectors[2])
    inv_one = 1.0 / sigma_one
    inv_two = 1.0 / sigma_two
    inv_skip = 1.0 / sigma_skip
    groups = group_counts.shape[0]
    group_pos = lax.axis_index("imgs")
    own_count = jnp.sum(jnp.where(jnp.arange(groups) == group_pos, group_counts, 0))
    live_mask = (jnp.arange(image_in.shape[0]) < own_count).astype(jnp.float32)[:, None, None, None]
    total_live = jnp.sum(group_counts).astype(jnp.float32)
    width_in = image_in.shape[2]
    width_out = 2 * width_in
    count_low = total_live * (width_in * width_in)
    count_high = total_live * (width_out * width_out)
    projected = jnp.dot(condition, low_cond, preferred_element_type=jnp.float32)
    gain_one = 1.0 + projected[:, :chan_in]
    shift_one = projected[:, chan_in : 2 * chan_in]
    gain_two = 1.0 + projected[:, 2 * chan_in : 2 * chan_in + chan_out]
    shift_two = projected[:, 2 * chan_in + chan_out :]
    images = image_in.astype(jnp.float32)
    sum_one, square_one = lax.psum(
        (
            jnp.sum(live_mask * images, axis=(0, 1, 2)),
            jnp.sum(live_mask * images * images, axis=(0, 1, 2)),
        ),
        ("rows", "imgs"),
    )
    normed_one, rstd_one, pre_one = finish_norm(
        images, sum_one, square_one, count_low, gain_one, shift_one
    )
    act_one = jax.nn.silu(pre_one).astype(jnp.bfloat16)
    up_halo = with_halo(upsample(act_one), (("rows", 1),), 1)
    kernel_one = low_one.reshape(3, 3, chan_in, chan_out)
    hidden_raw = conv_rows(up_halo, kernel_one)
    hidden = hidden_raw * inv_one
    sum_two, square_two = lax.psum(
        (
            jnp.sum(live_mask * hidden, axis=(0, 1, 2)),
            jnp.sum(live_mask * hidden * hidden, axis=(0, 1, 2)),
        ),
        ("rows", "imgs"),
    )
    normed_two, rstd_two, pre_two = finish_norm(
        hidden, sum_two, square_two, count_high, gain_two, shift_two
    )
    act_two = jax.nn.silu(pre_two).astype(jnp.bfloat16)
    act_extended = with_halo(act_two, (("rows", 1),), 1)
    kernel_two = low_two.reshape(3, 3, chan_out, chan_out)
    branch_raw = conv_rows(act_extended, kernel_two)
    skip_raw = jnp.einsum("irwc,co->irwo", image_in, low_skip, preferred_element_type=jnp.float32)
    out_image = (
        branch_raw * inv_two + upsample(skip_raw * inv_skip) + low_bias.astype(jnp.float32)
    ).astype(jnp.bfloat16)
    cotangent = out_cotangent.astype(jnp.float32) * live_mask
    pooled = pool_pairs(cotangent)
    grad_bias = jnp.sum(cotangent, axis=(0, 1, 2))
    grad_branch = (cotangent * inv_two).astype(jnp.bfloat16)
    grad_skip = (pooled * inv_skip).astype(jnp.bfloat16)
    scale_two = jnp.sum(cotangent * branch_raw)
    scale_skip = jnp.sum(pooled * skip_raw)
    branch_extended = with_halo(grad_branch, (("rows", 1),), 1)
    actgrad_two = conv_rows(branch_extended, flipped(kernel_two))
    pregrad_two = actgrad_two * silu_slope(pre_two)
    normgrad_two = gain_two[:, None, None, :] * pregrad_two
    total_two, cross_two, scale_two_all, scale_skip_all = lax.psum(
        (
            jnp.sum(normgrad_two, axis=(0, 1, 2)),
            jnp.sum(normgrad_two * normed_two, axis=(0, 1, 2)),
            scale_two,
            scale_skip,
        ),
        ("rows", "imgs"),
    )
    hidden_grad = (
        live_mask
        * rstd_two
        * (normgrad_two - total_two / count_high - normed_two * (cross_two / count_high))
    )
    hidgrad_raw = (hidden_grad * inv_one).astype(jnp.bfloat16)
    scale_one = jnp.sum(hidden_grad * hidden_raw)
    hidden_extended = with_halo(hidgrad_raw, (("rows", 1),), 1)
    actgrad_one = pool_pairs(conv_rows(hidden_extended, flipped(kernel_one)))
    pregrad_one = actgrad_one * silu_slope(pre_one)
    normgrad_one = gain_one[:, None, None, :] * pregrad_one
    total_one, cross_one, scale_one_all = lax.psum(
        (
            jnp.sum(normgrad_one, axis=(0, 1, 2)),
            jnp.sum(normgrad_one * normed_one, axis=(0, 1, 2)),
            scale_one,
        ),
        ("rows", "imgs"),
    )
    image_grad = live_mask * rstd_one * (
        normgrad_one - total_one / count_low - normed_one * (cross_one / count_low)
    ) + jnp.einsum("irwo,co->irwc", grad_skip, low_skip, preferred_element_type=jnp.float32)
    image_terms = jnp.concatenate(
        [
            jnp.sum(pregrad_one * normed_one, axis=(1, 2)),
            jnp.sum(pregrad_one, axis=(1, 2)),
            jnp.sum(pregrad_two * normed_two, axis=(1, 2)),
            jnp.sum(pregrad_two, axis=(1, 2)),
        ],
        axis=1,
    )
    grad_cond = jnp.dot(condition.astype(jnp.float32).T, image_terms, precision=precise)
    grad_one = tap_grads(up_halo, hidgrad_raw)
    grad_two = tap_grads(act_extended, grad_branch)
    grad_skip_w = jnp.einsum(
        "irwc,irwo->co", image_in, grad_skip, preferred_element_type=jnp.float32
    )
    row_pos = lax.axis_index("rows")
    rows_one = conv1_weight.shape[0]
    rows_two = conv2_weight.shape[0]
    rows_skip = skip_weight.shape[0]
    shards = (
        lax.psum_scatter(grad_one, "rows", scatter_dimension=0, tiled=True),
        lax.psum_scatter(grad_two, "rows", scatter_dimension=0, tiled=True),
        lax.psum_scatter(grad_skip_w, "rows", scatter_dimension=0, tiled=True),
        lax.psum_scatter(grad_cond, "rows", scatter_dimension=1, tiled=True),
        lax.psum_scatter(grad_bias, "rows", scatter_dimension=0, tiled=True),
    )
    totals = lax.psum((shards[0], shards[1], shards[2], shards[3], shards[4]), "imgs")
    fixed_one = totals[0] - scale_one_all * inv_one * inv_one * jnp.outer(
        own_rows(left_one, row_pos, rows_one, 0), right_one
    )
    fixed_two = totals[1] - scale_two_all * inv_two * inv_two * jnp.outer(
        own_rows(left_two, row_pos, rows_two, 0), right_two
    )
    fixed_skip = totals[2] - scale_skip_all * inv_skip * inv_skip * jnp.outer(
        own_rows(left_skip, row_pos, rows_skip, 0), right_skip
    )
    one_new = adamw(conv1_weight, conv1_first, conv1_second, fixed_one, LEARN_RATES[0])
    two_new = adamw(conv2_weight, conv2_first, conv2_second, fixed_two, LEARN_RATES[1])
    skip_new = adamw(skip_weight, skip_first, skip_second, fixed_skip, LEARN_RATES[2])
    cond_new = adamw(cond_weight, cond_first, cond_second, totals[3], LEARN_RATES[3])
    bias_new = adamw(out_bias, bias_first, bias_second, totals[4], LEARN_RATES[4])
    return (
        out_image,
        image_grad,
        one_new[0],
        one_new[1],
        one_new[2],
        two_new[0],
        two_new[1],
        two_new[2],
        skip_new[0],
        skip_new[1],
        skip_new[2],
        cond_new[0],
        cond_new[1],
        cond_new[2],
        bias_new[0],
        bias_new[1],
        bias_new[2],
    )


def solution(mesh):
    return jax.shard_map(
        body,
        mesh=mesh,
        in_specs=(
            P("imgs", "rows", None, None),
            P("imgs", None),
            P(),
            P("imgs", "rows", None, None),
            P(),
            P("rows", None),
            P("rows", None),
            P("rows", None),
            P(None, "rows"),
            P("rows"),
            P("rows", None),
            P("rows", None),
            P("rows", None),
            P(None, "rows"),
            P("rows"),
            P("rows", None),
            P("rows", None),
            P("rows", None),
            P(None, "rows"),
            P("rows"),
        ),
        out_specs=(
            P("imgs", "rows", None, None),
            P("imgs", "rows", None, None),
            P("rows", None),
            P("rows", None),
            P("rows", None),
            P("rows", None),
            P("rows", None),
            P("rows", None),
            P("rows", None),
            P("rows", None),
            P("rows", None),
            P(None, "rows"),
            P(None, "rows"),
            P(None, "rows"),
            P("rows"),
            P("rows"),
            P("rows"),
        ),
        check_vma=False,
    )
```

profile of v0, /device:TPU:0, one launch (start us, length us, event | category | flops | bytes accessed | tf_op | source)
XLA Modules:
  0.0 665.2 jit_solution(4582389037853264306)
XLA Ops:
  12.0 33.7 %all_gather.15 = bf16[148,1152]{0,1:T(8,128)(2,1)S(1)} all-gather(bf16[148,144]{0,1:T(8,128)(2,1)S(1)} %convert_element_type.64), channel_id=1, replica_groups=mesh['rows'=8,'imgs'=4] {'rows'}, dimensions={1}, use_global_device_ids=true | all-gather | bytes 383616 | tf_op jit(solution)/shard_map/all_gather | solution.py:138
  47.5 40.2 %all-reduce.7 = (f32[384]{0:T(512)S(1)}, f32[384]{0:T(512)S(1)}) all-reduce(f32[384]{0:T(512)S(1)} %get-tuple-element.96, f32[384]{0:T(512)S(1)} %get-tuple-element.95), channel_id=1, replica_groups=mesh['rows'=8,'imgs'=4] {'rows','imgs'}, use_global_device_ids=true, to_apply=%region_5.0 | all-reduce | flops 768 | bytes 6144 | tf_op jit(solution)/shard_map/psum | solution.py:164
  91.7 4.9 collective-permute-start
  98.8 32.8 %all-gather.1 = bf16[8,216,192]{1,2,0:T(8,128)(2,1)S(1)} all-gather(bf16[1,216,192]{1,2,0:T(8,128)(2,1)S(1)} %convert_bitcast_fusion.1), channel_id=1, replica_groups=mesh['rows'=8,'imgs'=4] {'rows'}, dimensions={0}, use_global_device_ids=true | all-gather | bytes 746496 | tf_op jit(solution)/shard_map/all_gather | solution.py:136
  138.7 30.6 %all_gather.18 = bf16[384,192]{1,0:T(8,128)(2,1)S(1)} all-gather(bf16[48,192]{1,0:T(8,128)(2,1)S(1)} %convert_element_type.74), channel_id=1, replica_groups=mesh['rows'=8,'imgs'=4] {'rows'}, dimensions={0}, use_global_device_ids=true | all-gather | bytes 165888 | tf_op jit(solution)/shard_map/all_gather | solution.py:137
  202.0 8.0 %select_reduce_fusion.3 = (f32[192]{0:T(256)S(1)}, f32[192]{0:T(256)S(1)}, f32[8,32,9,192]{3,1,2,0:T(8,128)S(1)}) fusion(f32[8,32,9,192]{3,0,2,1:T(8,128)S(1)} %bitcast.284, f32[]{:T(128)S(6)} %div.128, pred[32,9]{0,1:T(8,128)(4,1)S(1)} %copy-done.84, bf16[3,3,384,192]{3,2,1,0:T(8,128)(2,1)S(1)} %bitcast.285, bf16[10,4,8,11,384]{4,1,3,2,0:T(4,128)(2,1)} %fusion.4), kind=kOutput, calls=%fused_computation.23 | convolution fusion | flops 3061186048 | bytes 7571236 | tf_op jit(solution)/shard_map/conv_general_dilated | solution.py:43
  210.1 37.6 %all-reduce.6 = (f32[192]{0:T(256)S(1)}, f32[192]{0:T(256)S(1)}) all-reduce(f32[192]{0:T(256)S(1)} %get-tuple-element.86, f32[192]{0:T(256)S(1)} %get-tuple-element.85), channel_id=1, replica_groups=mesh['rows'=8,'imgs'=4] {'rows','imgs'}, use_global_device_ids=true, to_apply=%region_10.11 | all-reduce | flops 384 | bytes 3072 | tf_op jit(solution)/shard_map/psum | solution.py:179
  248.3 3.6 multiply_convert_fusion.1
  254.7 4.8 collective-permute-start.2
  266.5 3.8 broadcast_multiply_fusion
  283.2 6.2 collective-permute-start.4
  304.9 6.9 %select_reduce_fusion.2 = (f32[192]{0:T(256)S(1)}, f32[192]{0:T(256)S(1)}, f32[8,32,9,192]{3,1,2,0:T(8,128)}, f32[8,32,9,192]{3,1,2,0:T(8,128)}, f32[8,32,9,192]{3,1,2,0:T(8,128)}) fusion(pred[32,9]{0,1:T(8,128)(4,1)S(1)} %copy-done.85, f32[192]{0:T(256)S(1)} %copy-done.72, f32[192]{0:T(256)S(1)} %copy-done.83, f32[]{:T(128)S(6)} %div.128, ...), kind=kOutput, calls=%fused_computation.19 | convolution fusion | flops 1537670656 | bytes 12635428 | tf_op jit(solution)/shard_map/conv_general_dilated | solution.py:43
  311.8 41.8 %all-reduce.5 = (f32[192]{0:T(256)S(1)}, f32[192]{0:T(256)S(1)}) all-reduce(f32[192]{0:T(256)S(1)} %get-tuple-element.88, f32[192]{0:T(256)S(1)} %get-tuple-element.87), channel_id=1, replica_groups=mesh['rows'=8,'imgs'=4] {'rows','imgs'}, use_global_device_ids=true, to_apply=%region_22.23 | all-reduce | flops 384 | bytes 3072 | tf_op jit(solution)/shard_map/psum | solution.py:208
  360.3 5.3 collective-permute-start.6
  375.1 5.8 fusion.27
  384.8 4.0 reshape.130
  388.8 4.4 reduce_sum.278
  427.2 4.8 copy.248
  445.9 20.2 %all-reduce.3 = f32[192]{0:T(256)S(1)} all-reduce(f32[192]{0:T(256)S(1)} %copy-done.88), channel_id=6, replica_groups=mesh['rows'=8,'imgs'=4] {'rows'}, use_global_device_ids=true, to_apply=%region_48.49.clone | all-reduce | flops 192 | bytes 1536
  466.2 37.8 %all-reduce.4 = (f32[384]{0:T(512)S(1)}, f32[384]{0:T(512)S(1)}, f32[]{:T(128)}, f32[]{:T(128)}, f32[]{:T(128)}) all-reduce(f32[384]{0:T(512)S(1)} %copy-done.86, f32[384]{0:T(512)S(1)} %copy-done.87, f32[]{:T(128)} %get-tuple-element.136, f32[]{:T(128)} %get-tuple-element.92, ...), channel_id=1, replica_groups=mesh['rows'=8,'imgs'=4] {'rows','imgs'}, use_global_device_ids=true, to_apply=%region_27.28 | all-reduce | flops 771 | bytes 6168 | tf_op jit(solution)/shard_map/psum | solution.py:228
  508.4 11.2 %all-reduce.8 = (f32[48,192]{1,0:T(8,128)S(1)}, f32[24]{0:T(128)S(1)}) all-reduce(f32[48,192]{1,0:T(8,128)} %reduce-scatter.17.cloned.1.call-done, f32[24]{0:T(128)S(1)} %dynamic-slice.2), channel_id=1, replica_groups=mesh['rows'=8,'imgs'=4] {'imgs'}, use_global_device_ids=true, to_apply=%region_38.39 | all-reduce | flops 9240 | bytes 73920 | tf_op jit(solution)/shard_map/psum | solution.py:265
  520.3 21.6 %all-reduce.2 = bf16[192]{0:T(256)(128)(2,1)S(1)} all-reduce(bf16[192]{0:T(256)(128)(2,1)S(1)} %dynamic-update-slice), channel_id=1, replica_groups=mesh['rows'=8,'imgs'=4] {'rows'}, use_global_device_ids=true, to_apply=%add.2 | all-reduce | flops 192 | bytes 768
  545.4 68.2 %reduce-scatter.13.cloned.1.call-done = f32[432,192]{1,0:T(8,128)} async-done(((f32[3456,192]{1,0:T(8,128)}), f32[432,192]{1,0:T(8,128)}) %reduce-scatter.13.cloned.1.call-update) | async-done | bytes 331792
  619.6 31.3 %all-reduce.12.cloned.1.call-done = (f32[432,192]{0,1:T(8,128)}, f32[216,192]{0,1:T(8,128)}, f32[148,144]{1,0:T(8,128)}) async-done(((f32[432,192]{0,1:T(8,128)}, f32[216,192]{0,1:T(8,128)}, f32[148,144]{1,0:T(8,128)}), (f32[432,192]{0,1:T(8,128)}, f32[216,192]{0,1:T(8,128)}, f32[148,144]{1,0:T(8,128)})) %all-reduce.12.cloned.1.call-update) | async-done | bytes 582928 | tf_op jit(solution)/shard_map/psum | solution.py:265
  (380 shorter events, 169.4 us)
Async XLA Ops:
  7.2 40.0 %copy-start.1 = (bf16[4,4,32,384]{3,2,1,0:T(8,128)(2,1)S(1)}, bf16[4,4,32,384]{3,2,1,0:T(8,128)(2,1)}, u32[]{:S(2)}) copy-start(bf16[4,4,32,384]{3,2,1,0:T(8,128)(2,1)} %param.20) | copy-start | bytes 1179652
  7.2 179.7 %all-gather.4.cloned.1.call-start = ((), (), s32[]{:S(2)}) async-start(), calls=%async_computation.4 | async-start | bytes 1769472 | tf_op jit(solution)/shard_map/all_gather | solution.py:135
  9.0 499.3 %reduce-scatter.17.cloned.1.call-start = ((), (), s32[]{:S(2)}) async-start(), calls=%async_computation.7 | async-start | bytes 442368 | tf_op jit(solution)/shard_map/reduce_scatter | solution.py:261
  11.0 77.7 %copy-start.73 = (f32[4]{0:T(128)}, f32[4]{0:T(128)S(1)}, u32[]{:S(2)}) copy-start(f32[4]{0:T(128)S(1)} %compare_convert_fusion) | copy-start | bytes 52
  46.6 42.2 %copy-start.63 = (f32[4,384]{1,0:T(4,128)}, f32[4,384]{1,0:T(4,128)S(1)}, u32[]{:S(2)}) copy-start(f32[4,384]{1,0:T(4,128)S(1)} %get-tuple-element.156) | copy-start | bytes 18436
  90.8 87.6 %copy-start.4 = (bf16[4,8,64,384]{3,2,1,0:T(8,128)(2,1)}, bf16[4,8,64,384]{3,2,1,0:T(8,128)(2,1)S(1)}, u32[]{:S(2)}) copy-start(bf16[4,8,64,384]{3,2,1,0:T(8,128)(2,1)S(1)} %reshape.125) | copy-start | bytes 4718596
  91.7 85.8 %collective-permute-start = (bf16[4,1,64,384]{3,2,1,0:T(8,128)(2,1)}, bf16[4,1,64,384]{3,2,1,0:T(8,128)(2,1)}, u32[]{:S(2)}, u32[]{:S(2)}) collective-permute-start(bf16[4,1,64,384]{3,2,1,0:T(8,128)(2,1)} %get-tuple-element.140), channel_id=1, source_target_pairs={{0,4},{4,8},{8,12},{12,16},{16,20},{20,24},{24,28},{1,5},{5,9},{9,... | collective-permute-start | bytes 589832 | tf_op jit(solution)/shard_map/ppermute | solution.py:25
  96.6 82.2 %collective-permute-start.1 = (bf16[4,1,64,384]{3,2,1,0:T(8,128)(2,1)}, bf16[4,1,64,384]{3,2,1,0:T(8,128)(2,1)}, u32[]{:S(2)}, u32[]{:S(2)}) collective-permute-start(bf16[4,1,64,384]{3,2,1,0:T(8,128)(2,1)} %get-tuple-element.139), channel_id=1, source_target_pairs={{4,0},{8,4},{12,8},{16,12},{20,16},{24,20},{28,24},{5,1},{9,5},{13... | collective-permute-start | bytes 589832 | tf_op jit(solution)/shard_map/ppermute | solution.py:26
  136.7 42.1 %copy-start.62 = (f32[1728]{0:T(1024)}, f32[1728]{0:T(1024)S(1)}, u32[]{:S(2)}) copy-start(f32[1728]{0:T(1024)S(1)} %broadcast_multiply_fusion.3) | copy-start | bytes 20740
  253.2 9.3 %collective-permute-start.3 = (bf16[4,1,64,192]{3,2,1,0:T(8,128)(2,1)S(1)}, bf16[4,1,64,192]{3,2,1,0:T(8,128)(2,1)S(1)}, u32[]{:S(2)}, u32[]{:S(2)}) collective-permute-start(bf16[4,1,64,192]{3,2,1,0:T(8,128)(2,1)S(1)} %slice_bitcast_fusion.5), channel_id=1, source_target_pairs={{4,0},{8,4},{12,8},{16,12},{20,16},{24,20},{28,24},{5,1},{9,5},{13... | collective-permute-start | bytes 294920 | tf_op jit(solution)/shard_map/ppermute | solution.py:26
  254.7 8.5 %collective-permute-start.2 = (bf16[4,1,64,192]{3,2,1,0:T(8,128)(2,1)S(1)}, bf16[4,1,64,192]{3,2,1,0:T(8,128)(2,1)S(1)}, u32[]{:S(2)}, u32[]{:S(2)}) collective-permute-start(bf16[4,1,64,192]{3,2,1,0:T(8,128)(2,1)S(1)} %slice_bitcast_fusion.6), channel_id=1, source_target_pairs={{0,4},{4,8},{8,12},{12,16},{16,20},{20,24},{24,28},{1,5},{5,9},{9,... | collective-permute-start | bytes 294920 | tf_op jit(solution)/shard_map/ppermute | solution.py:25
  282.0 14.2 %collective-permute-start.5 = (bf16[4,1,64,192]{3,1,2,0:T(2,128)(2,1)}, bf16[4,1,64,192]{3,1,2,0:T(2,128)(2,1)S(1)}, u32[]{:S(2)}, u32[]{:S(2)}) collective-permute-start(bf16[4,1,64,192]{3,1,2,0:T(2,128)(2,1)} %get-tuple-element.150), channel_id=1, source_target_pairs={{4,0},{8,4},{12,8},{16,12},{20,16},{24,20},{28,24},{5,1},{9,5},{13... | collective-permute-start | bytes 294920 | tf_op jit(solution)/shard_map/ppermute | solution.py:26
  283.2 15.3 %collective-permute-start.4 = (bf16[4,1,64,192]{3,1,2,0:T(2,128)(2,1)}, bf16[4,1,64,192]{3,1,2,0:T(2,128)(2,1)}, u32[]{:S(2)}, u32[]{:S(2)}) collective-permute-start(bf16[4,1,64,192]{3,1,2,0:T(2,128)(2,1)} %get-tuple-element.149), channel_id=1, source_target_pairs={{0,4},{4,8},{8,12},{12,16},{16,20},{20,24},{24,28},{1,5},{5,9},{9,... | collective-permute-start | bytes 294920 | tf_op jit(solution)/shard_map/ppermute | solution.py:25
  295.9 246.1 %reduce-scatter.19.cloned.1.call-start = ((), (), s32[]{:S(2)}) async-start(), calls=%async_computation.8 | async-start | bytes 1327104
  304.9 48.7 %copy-start.70 = (f32[4,192]{1,0:T(4,128)S(1)}, f32[4,192]{1,0:T(4,128)}, u32[]{:S(2)}) copy-start(f32[4,192]{1,0:T(4,128)} %broadcast_multiply_fusion.5) | copy-start | bytes 9220
  358.8 12.1 %collective-permute-start.7 = (bf16[4,1,64,192]{3,2,1,0:T(8,128)(2,1)S(1)}, bf16[4,1,64,192]{3,2,1,0:T(8,128)(2,1)S(1)}, u32[]{:S(2)}, u32[]{:S(2)}) collective-permute-start(bf16[4,1,64,192]{3,2,1,0:T(8,128)(2,1)S(1)} %slice_bitcast_fusion.3), channel_id=1, source_target_pairs={{4,0},{8,4},{12,8},{16,12},{20,16},{24,20},{28,24},{5,1},{9,5},{13... | collective-permute-start | bytes 294920 | tf_op jit(solution)/shard_map/ppermute | solution.py:26
  360.3 10.6 %collective-permute-start.6 = (bf16[4,1,64,192]{3,2,1,0:T(8,128)(2,1)S(1)}, bf16[4,1,64,192]{3,2,1,0:T(8,128)(2,1)S(1)}, u32[]{:S(2)}, u32[]{:S(2)}) collective-permute-start(bf16[4,1,64,192]{3,2,1,0:T(8,128)(2,1)S(1)} %slice_bitcast_fusion.4), channel_id=1, source_target_pairs={{0,4},{4,8},{8,12},{12,16},{16,20},{20,24},{24,28},{1,5},{5,9},{9,... | collective-permute-start | bytes 294920 | tf_op jit(solution)/shard_map/ppermute | solution.py:25
  399.3 144.3 %reduce-scatter.15.cloned.1.call-start = ((), (), s32[]{:S(2)}) async-start(), calls=%async_computation.6 | async-start | bytes 1990656
  410.5 203.1 %reduce-scatter.13.cloned.1.call-start = ((), (), s32[]{:S(2)}) async-start(), calls=%async_computation.5 | async-start | bytes 3981312
  432.1 218.8 %all-reduce.12.cloned.1.call-start = ((), (), s32[]{:S(2)}) async-start(), calls=%async_computation.9 | async-start | bytes 1490944 | tf_op jit(solution)/shard_map/psum | solution.py:265
  442.8 63.1 %copy-start.68 = (f32[384]{0:T(512)S(1)}, f32[384]{0:T(512)}, u32[]{:S(2)}) copy-start(f32[384]{0:T(512)} %copy-done.67) | copy-start | bytes 4612
  445.8 73.7 %copy-start.90 = (f32[24]{0:T(128)S(1)}, f32[24]{0:T(128)}, u32[]{:S(2)}) copy-start(f32[24]{0:T(128)} %param.29) | copy-start | bytes 292
  445.8 73.7 %copy-start.91 = (f32[24]{0:T(128)S(1)}, f32[24]{0:T(128)}, u32[]{:S(2)}) copy-start(f32[24]{0:T(128)} %param.34) | copy-start | bytes 292
  445.9 73.7 %copy-start.92 = (f32[24]{0:T(128)S(1)}, f32[24]{0:T(128)}, u32[]{:S(2)}) copy-start(f32[24]{0:T(128)} %param.39) | copy-start | bytes 292
  (83 other events, 586.7 us)
Sparse Core Ops, SparseCore 0:
  10.8 47.9 all-gather.3
  296.0 62.8 reduce-scatter.16
  399.4 63.5 reduce-scatter.18
  466.4 65.1 reduce-scatter.14
  535.5 78.0 reduce-scatter.12
  616.7 34.0 all-reduce.11
where the time goes:
time: 675 us; the launch traced here: 665 us
  blocking collectives  308 us (46%)
  waiting for transfers between devices  103 us (15%)
  local copies, waits for them, and re-layouts  89.9 us (13%)
  matrix products  60.1 us (9%)
  other arithmetic  51.6 us (8%)
  starting transfers between devices  27 us (4%)
  between operations  26.3 us (4%)
    unnamed x9, waiting for transfers between devices  68.4 us
    unnamed x214, local copies, waits for them, and re-layouts  44.6 us
    psum x1, blocking collectives, body(): lax.psum((jnp.sum(normgrad_two, axis=(0, 1, 2)), jnp.sum(normgrad_two * n...  41.8 us
    unnamed x2, blocking collectives  41.8 us
    psum x1, blocking collectives, body(): lax.psum((jnp.sum(live_mask * images, axis=(0, 1, 2)), jnp.sum(live_mask...  40.2 us
    psum x1, blocking collectives, body(): lax.psum((jnp.sum(normgrad_one, axis=(0, 1, 2)), jnp.sum(normgrad_one * n...  37.8 us
    psum x1, blocking collectives, body(): lax.psum((jnp.sum(live_mask * hidden, axis=(0, 1, 2)), jnp.sum(live_mask...  37.6 us
    all_gather x1, blocking collectives, body(): lax.all_gather(cond_weight.astype(jnp.bfloat16), 'rows', axis=1, tiled=True)  33.7 us
  transfers between devices with their start and end apart: 14, of which 4 were waited for; matrix products, arithmetic and copies ran while one was open for 20% of the time, Pallas kernels for 0%

commit v1 on v0

v1 whole, which is shorter than its diff:
```python
import functools

import jax
import jax.numpy as jnp
import numpy as np
from jax import lax
from jax.experimental import pallas as pl
from jax.experimental.pallas import tpu as pltpu
from jax.sharding import Mesh
from jax.sharding import PartitionSpec as P

STEP = 10
precise = lax.Precision.HIGHEST
NORM_EPS = 1e-05
BETA_ONE = 0.9
BETA_TWO = 0.999
ADAM_EPS = 1e-08
DECAY_RATE = 0.01
LEARN_RATES = (0.02, 0.02, 0.05, 0.03, 0.15)
ALL = ("rows", "x", "core")
F32, BF16 = jnp.float32, jnp.bfloat16
LANES = 128
VMEM_LIMIT = 40 * 2**20


def shape(dims, kind=F32):
    return jax.ShapeDtypeStruct(tuple(dims), kind)


def run(kernel, outs, args, scratch=(), scalars=1, flops=0, limit=VMEM_LIMIT):
    spec = pl.BlockSpec(memory_space=pltpu.VMEM)
    specs = [pl.BlockSpec(memory_space=pltpu.SMEM)] * scalars + [spec] * (len(args) - scalars)
    moved = sum(a.size * a.dtype.itemsize for a in args)
    moved += sum(np.prod(o.shape) * np.dtype(o.dtype).itemsize for o in outs)
    return pl.pallas_call(
        kernel,
        out_shape=tuple(outs),
        in_specs=specs,
        out_specs=tuple(spec for _ in outs),
        scratch_shapes=scratch,
        cost_estimate=pl.CostEstimate(
            flops=int(flops), bytes_accessed=int(moved), transcendentals=0
        ),
        compiler_params=pltpu.CompilerParams(vmem_limit_bytes=limit),
    )(*args)


def round_up(value, step):
    return -(-value // step) * step


class Sizes:
    def __init__(self, image, cot, condition, masters, rows_n, groups_n):
        self.images, self.rows, self.width, self.chan = image
        self.out = cot[3]
        self.slot = round_up(self.out, LANES)
        self.ext = 2 * self.rows + 2
        self.cond = condition[1]
        self.n_one, self.n_two, self.n_skip = masters[0][0], masters[1][0], masters[2][0]
        self.cols = masters[3][1]
        self.n_bias = masters[4][0]
        self.rows_n, self.groups = rows_n, groups_n
        self.devices = rows_n * groups_n
        self.h_one = round_up(-(-self.n_one // 2), 8)
        self.h_two = round_up(-(-self.n_two // 2), 8)
        self.h_skip = round_up(-(-self.n_skip // 2), 8)
        self.at_power = 2 * self.chan
        self.at_norm = self.at_power + 3 * self.slot
        self.at_bias = self.at_norm + 8
        self.at_proj = round_up(self.at_bias + self.n_bias, LANES)
        self.pay_one = round_up(self.at_proj + self.images * self.cols, LANES)
        self.at_cond = 2 * self.slot
        self.pay_two = round_up(self.at_cond + self.images * self.cond, LANES)
        self.pay_three = 3 * self.slot
        self.at_scale = 2 * self.chan
        self.at_terms = self.at_scale + LANES
        self.pay_four = round_up(self.at_terms + self.images * self.cols, LANES)
        self.edge = 3 * self.width + 2 * 2 * self.width * (1 + 1)


def position():
    return lax.axis_index("rows"), lax.axis_index("x"), lax.axis_index("core")


def group_position():
    return lax.axis_index("x") * lax.axis_size("core") + lax.axis_index("core")


def live_of(counts, image):
    return jnp.where(image < counts[group_position()], 1.0, 0.0).astype(F32)


def live_total(counts, sizes):
    total = counts[0]
    for g in range(1, sizes.groups):
        total = total + counts[g]
    return total.astype(F32)


def inside(row, sizes, scale):
    at = lax.axis_index("rows") * (scale * sizes.rows) + row
    return jnp.where((at >= 0) & (at < scale * sizes.rows * sizes.rows_n), 1.0, 0.0).astype(F32)


def sigmoid(values):
    return 1.0 / (1.0 + jnp.exp(-values))


def shifted(values, step):
    width = values.shape[0]
    rolled = pltpu.roll(values, (-step) % width, 0)
    where = lax.broadcasted_iota(jnp.int32, values.shape, 0)
    edge = 0 if step < 0 else width - 1
    return jnp.where(where == edge, 0.0, rolled)


def dot(a, b, dims=((1,), (0,)), precision=None):
    return lax.dot_general(a, b, (dims, ((), ())), preferred_element_type=F32, precision=precision)


def prep_kernel(sizes, counts, image, cot, cond, vec, vec_t, one_t, two_t, skip, cond_t, bias,
                pay, half_one, half_two, near, far, left_one, left_two, left_skip, line):
    s = sizes
    row_pos, _, core = position()
    even = lax.rem(row_pos, 2) == 0
    last, w = s.rows - 1, s.width

    def edges(ref, low_row, high_row):
        for t in range(3):
            ref[:, t * w : (t + 1) * w, :] = image[:, low_row, :, t * LANES : (t + 1) * LANES]
        at = 3 * w
        for k in range(2):
            ref[:, at : at + 2 * w, :] = cot[:, high_row + k, :, :LANES]
            at += 2 * w
        for k in range(2):
            ref[:, at : at + 2 * w, : s.out - LANES] = cot[:, high_row + k, :, LANES:]
            at += 2 * w

    @pl.when(even)
    def _():
        edges(near, last, 2 * s.rows - 2)
        edges(far, 0, 0)

    @pl.when(jnp.logical_not(even))
    def _():
        edges(near, 0, 0)
        edges(far, last, 2 * s.rows - 2)

    line[...] = jnp.zeros_like(line)
    sums = jnp.zeros((8, s.chan), F32)
    squares = jnp.zeros((8, s.chan), F32)
    for b in range(s.images):
        part = jnp.zeros((8, s.chan), F32)
        part_sq = jnp.zeros((8, s.chan), F32)
        for i in range(s.rows):
            x = image[b, i].astype(F32).reshape(w // 8, 8, s.chan)
            part += jnp.sum(x, axis=0)
            part_sq += jnp.sum(x * x, axis=0)
        sums += part * live_of(counts, b)
        squares += part_sq * live_of(counts, b)
    line[0:1, : s.chan] = jnp.sum(sums, axis=0, keepdims=True)
    line[0:1, s.chan : 2 * s.chan] = jnp.sum(squares, axis=0, keepdims=True)

    def power(k, low, left_row):
        column = jnp.sum(low * vec[k : k + 1, :], axis=1, keepdims=True)
        row = jnp.sum(low * column, axis=0, keepdims=True)
        at = s.at_power + k * s.slot
        line[0:1, at : at + s.out] = row
        line[0:1, s.at_norm + k : s.at_norm + k + 1] = jnp.sum(column * column, axis=0, keepdims=True)
        return column

    low_t = one_t[...].astype(BF16).astype(F32)
    left_one[...] = jnp.sum(low_t * vec_t[:, 0:1], axis=0, keepdims=True)
    low = jnp.transpose(low_t)
    power(0, low, left_one)
    n, h = s.n_one, s.h_one
    half = jnp.where(core == 0, low[:h], low[n - h :]).astype(BF16)
    for r in range(s.rows_n):
        half_one[r] = half
    low_t = two_t[...].astype(BF16).astype(F32)
    left_two[...] = jnp.sum(low_t * vec_t[:, 1:2], axis=0, keepdims=True)
    low = jnp.transpose(low_t)
    power(1, low, left_two)
    n, h = s.n_two, s.h_two
    half_a = jnp.where(core == 0, low[:h], low[n - h :])
    low = skip[...].astype(BF16).astype(F32)
    left_skip[...] = power(2, low, None)
    n, h = s.n_skip, s.h_skip
    half_b = jnp.where(core == 0, low[:h], low[n - h :])
    half = jnp.concatenate([half_a, half_b], axis=0).astype(BF16)
    for r in range(s.rows_n):
        half_two[r] = half

    line[0:1, s.at_bias : s.at_bias + s.n_bias] = bias[...].astype(BF16).astype(F32)
    proj = dot(cond[...], cond_t[...].astype(BF16), ((1,), (1,)))
    for b in range(s.images):
        at = s.at_proj + b * s.cols
        line[0:1, at : at + s.cols] = proj[b : b + 1]
    whole = line[...]
    for d in range(s.devices):
        pay[d] = whole


def act_kernel(sizes, counts, got, image, near, far, slots, proj, stats, spec):
    s = sizes
    row_pos, _, _ = position()
    even = lax.rem(row_pos, 2) == 0
    group = group_position()
    sums = jnp.sum(got[:, :, : 2 * s.chan], axis=0)
    count = live_total(counts, s) * (s.width * s.width)
    mean = sums[:, : s.chan] / count
    rstd = lax.rsqrt(sums[:, s.chan :] / count - mean * mean + NORM_EPS)
    stats[0:1, :] = mean
    stats[1:2, :] = rstd

    spec[...] = jnp.zeros_like(spec)
    total = got[group, :, s.at_power : s.at_proj]
    for r in range(1, s.rows_n):
        total = total + got[r * s.groups + group, :, s.at_power : s.at_proj]
    for k in range(3):
        at = 3 * s.slot + k
        inv_norm = lax.rsqrt(total[:, at : at + 1])
        row = total[:, k * s.slot : k * s.slot + s.out] * inv_norm
        inv_sigma = lax.rsqrt(jnp.sum(row * row, axis=1, keepdims=True))
        spec[k : k + 1, : s.out] = row * inv_sigma
        spec[3 + k : 4 + k, :] = jnp.broadcast_to(inv_sigma, (1, s.slot))
        spec[8 + k : 9 + k, :] = jnp.broadcast_to(inv_norm, (1, s.slot))
    for r in range(s.rows_n):
        piece = got[r * s.groups + group, :, s.at_bias : s.at_bias + s.n_bias]
        spec[6:7, r * s.n_bias : (r + 1) * s.n_bias] = piece
        for b in range(s.images):
            at = s.at_proj + b * s.cols
            proj[b : b + 1, r * s.cols : (r + 1) * s.cols] = got[
                r * s.groups + group, :, at : at + s.cols
            ]

    w = s.width

    def one(b, e, x, keep):
        gain = 1.0 + proj[pl.ds(b, 1), : s.chan]
        shift = proj[pl.ds(b, 1), s.chan : 2 * s.chan]
        pre = gain * ((x - mean) * rstd) + shift
        act = pre * sigmoid(pre)
        if keep is not None:
            act = act * keep
        low = act.astype(BF16)
        slots[b, e, :, s.chan : 2 * s.chan] = low
        slots[b, e, :, 2 * s.chan : 3 * s.chan] = low
        slots[b, e, :, : s.chan] = shifted(act, -1).astype(BF16)
        slots[b, e, :, 3 * s.chan :] = shifted(act, 1).astype(BF16)

    def edge(ref, b):
        return jnp.concatenate(
            [ref[b, t * w : (t + 1) * w, :].astype(F32) for t in range(3)], axis=1
        )

    @pl.loop(0, s.images)
    def _(b):
        a, c = edge(near, b), edge(far, b)
        one(b, 0, jnp.where(even, c, a), inside(-1, s, 1))
        for i in range(s.rows):
            one(b, i + 1, image[b, i].astype(F32), None)
        one(b, s.rows + 1, jnp.where(even, a, c), inside(s.rows, s, 1))


def conv_one_kernel(sizes, counts, slots, mine, other, cond, hidden, weight, pay, line, wide):
    s = sizes
    _, _, core = position()
    first = core == 0
    for r in range(s.rows_n):
        a, b = mine[r].astype(F32), other[r].astype(F32)
        at = r * s.n_one
        wide[at : at + s.h_one, :] = jnp.where(first, a, b)
        at += s.n_one - s.h_one
        wide[at : at + s.h_one, :] = jnp.where(first, b, a)
    for t in range(9):
        weight[t * s.chan : (t + 1) * s.chan] = wide[t * s.chan : (t + 1) * s.chan, :].astype(BF16)
    depth = 3 * s.chan
    rows = s.rows + 1
    sums = jnp.zeros((8, s.out), F32)
    squares = jnp.zeros((8, s.out), F32)
    for phase in range(4):
        a, b = divmod(phase, 2)
        total = None
        for dy in range(3):
            start = (a + dy - 1) // 2 + 1 - a
            lhs = slots[:, start : start + rows, :, b * s.chan : b * s.chan + depth]
            part = dot(
                lhs.reshape(s.images * rows * s.width, depth),
                weight[dy * depth : (dy + 1) * depth, :],
            )
            total = part if total is None else total + part
        total = total.reshape(s.images, rows, s.width, s.out)
        for i in range(s.images):
            part = jnp.zeros((8, s.out), F32)
            part_sq = jnp.zeros((8, s.out), F32)
            for k in range(rows):
                e = 2 * k + 1 - a
                value = total[i, k]
                hidden[i, e, b] = value
                if 0 < e < s.ext - 1:
                    x = value.reshape(s.width // 8, 8, s.out)
                    part += jnp.sum(x, axis=0)
                    part_sq += jnp.sum(x * x, axis=0)
            sums += part * live_of(counts, i)
            squares += part_sq * live_of(counts, i)
    line[...] = jnp.zeros_like(line)
    line[0:1, : s.out] = jnp.sum(sums, axis=0, keepdims=True)
    line[0:1, s.slot : s.slot + s.out] = jnp.sum(squares, axis=0, keepdims=True)
    for i in range(s.images):
        at = s.at_cond + i * s.cond
        line[0:1, at : at + s.cond] = cond[i : i + 1, :].astype(F32)
    whole = line[...]
    for d in range(s.devices):
        pay[d] = whole


def cot_kernel(sizes, counts, cot, near, far, image, mine, other, spec, dact, phases, grad_low,
               grad_skip, skip_part, two, skip_w, misc, slots, wide, pair, flip):
    s = sizes
    row_pos, _, core = position()
    even = lax.rem(row_pos, 2) == 0
    first = core == 0
    w = s.width
    for r in range(s.rows_n):
        a, b = mine[r].astype(F32), other[r].astype(F32)
        lo, hi = jnp.where(first, a, b), jnp.where(first, b, a)
        at = r * s.n_two
        wide[at : at + s.h_two, :] = lo[: s.h_two]
        at += s.n_two - s.h_two
        wide[at : at + s.h_two, :] = hi[: s.h_two]
        at = 9 * s.out + r * s.n_skip
        wide[at : at + s.h_skip, :] = lo[s.h_two :]
        at += s.n_skip - s.h_skip
        wide[at : at + s.h_skip, :] = hi[s.h_two :]
    two[...] = jnp.zeros_like(two)
    flip[...] = jnp.zeros_like(flip)
    for t in range(9):
        dy, dx = divmod(t, 3)
        tap = wide[t * s.out : (t + 1) * s.out, :]
        two[dy, dx * s.slot : dx * s.slot + s.out, :] = tap.astype(BF16)
        back = jnp.transpose(tap).astype(BF16)
        flip[2 - dy, (2 - dx) * s.slot : (2 - dx) * s.slot + s.out, :] = back
    skip_w[...] = wide[9 * s.out : 9 * s.out + s.chan, :].astype(BF16)

    slots[...] = jnp.zeros_like(slots)
    inv_two = spec[4:5, : s.out]
    inv_skip = spec[5:6, : s.out]

    def split(b, q, row, own):
        pair[0] = row[:, :LANES]
        pair[1, :, : s.out - LANES] = row[:, LANES:]
        both = []
        for ph in range(2):
            value = jnp.concatenate(
                [pair[0, pl.ds(ph, w, 2), :], pair[1, pl.ds(ph, w, 2), :][:, : s.out - LANES]],
                axis=1,
            )
            low = (value * inv_two).astype(BF16)
            both.append(value)
            if own is not None:
                phases[b, own, ph] = value.astype(BF16)
                grad_low[b, own, ph] = low
            at = (1 + ph) * s.slot
            slots[b, q, :, at : at + s.out] = low
            if ph == 1:
                slots[b, q, :, : s.out] = shifted(low.astype(F32), -1).astype(BF16)
            else:
                slots[b, q, :, 3 * s.slot : 3 * s.slot + s.out] = shifted(
                    low.astype(F32), 1
                ).astype(BF16)
        return both[0] + both[1]

    def edge_row(ref, b, k):
        at = 3 * w + k * 2 * w
        return jnp.concatenate(
            [
                ref[b, at : at + 2 * w, :].astype(F32),
                ref[b, at + 4 * w : at + 6 * w, : s.out - LANES].astype(F32),
            ],
            axis=1,
        )

    misc[...] = jnp.zeros_like(misc)

    @pl.loop(0, s.images)
    def _(b):
        live = live_of(counts, b)
        above = inside(-1, s, 1) * live
        below = inside(s.rows, s, 1) * live
        for k in range(2):
            a, c = edge_row(near, b, k), edge_row(far, b, k)
            split(b, k, jnp.where(even, c, a) * above, None)
            split(b, 2 * s.rows + 2 + k, jnp.where(even, a, c) * below, None)
        bias = jnp.zeros((1, s.out), F32)
        skip_sum = jnp.zeros((1, s.out), F32)
        for i in range(s.rows):
            pooled = split(b, 2 * i + 2, cot[b, 2 * i].astype(F32) * live, 2 * i)
            pooled += split(b, 2 * i + 3, cot[b, 2 * i + 1].astype(F32) * live, 2 * i + 1)
            grad_skip[b, i] = (pooled * inv_skip).astype(BF16)
            bias += jnp.sum(pooled, axis=0, keepdims=True)
            raw = dot(image[b, i], skip_w[...])
            skip_part[b, i] = raw * inv_skip
            skip_sum += jnp.sum(pooled * raw, axis=0, keepdims=True)
        misc[0:1, : s.out] += bias
        misc[1:2, : s.out] += skip_sum

    depth = 3 * s.slot
    for ph in range(2):
        total = None
        for dy in range(3):
            lhs = slots[:, dy : dy + s.ext, :, ph * s.slot : ph * s.slot + depth]
            part = dot(lhs.reshape(s.images * s.ext * w, depth), flip[dy])
            total = part if total is None else total + part
        dact[:, :, ph] = total.reshape(s.images, s.ext, w, s.out)


def norm_two_kernel(sizes, counts, got, hidden, dact, spec, proj, misc, slots, dnorm, stats,
                    terms, pay, line):
    s = sizes
    w = s.width
    inv = spec[3:4, : s.out]
    sums = jnp.sum(got[:, :, : 2 * s.slot], axis=0)
    count = live_total(counts, s) * (4 * w * w)
    mean = sums[:, : s.out] * inv / count
    square = sums[:, s.slot : s.slot + s.out] * inv * inv / count
    rstd = lax.rsqrt(square - mean * mean + NORM_EPS)
    stats[0:1, : s.out] = mean
    stats[1:2, : s.out] = rstd
    scale = inv * rstd
    offset = mean * rstd
    slots[...] = jnp.zeros_like(slots)
    base = 2 * s.chan

    def one(b, e, keep):
        gain = 1.0 + proj[pl.ds(b, 1), base : base + s.out]
        shift = proj[pl.ds(b, 1), base + s.out : base + 2 * s.out]
        dsum = jnp.zeros((8, s.out), F32)
        dgain = jnp.zeros((8, s.out), F32)
        for ph in range(2):
            normed = hidden[b, e, ph] * scale - offset
            pre = gain * normed + shift
            sig = sigmoid(pre)
            act = pre * sig
            if keep is not None:
                act = act * keep
            at = (1 + ph) * s.slot
            slots[b, e, :, at : at + s.out] = act.astype(BF16)
            if ph == 1:
                slots[b, e, :, : s.out] = shifted(act, -1).astype(BF16)
            else:
                slots[b, e, :, 3 * s.slot : 3 * s.slot + s.out] = shifted(act, 1).astype(BF16)
            dpre = dact[b, e, ph] * (sig * (1.0 + pre * (1.0 - sig)))
            dnorm[b, e, ph] = gain * dpre
            if keep is None:
                dsum += jnp.sum(dpre.reshape(w // 8, 8, s.out), axis=0)
                dgain += jnp.sum((dpre * normed).reshape(w // 8, 8, s.out), axis=0)
        return dsum, dgain

    terms[...] = jnp.zeros_like(terms)

    @pl.loop(0, s.images)
    def _(b):
        one(b, 0, inside(-1, s, 2))
        dsum = jnp.zeros((8, s.out), F32)
        dgain = jnp.zeros((8, s.out), F32)
        for e in range(1, s.ext - 1):
            a, c = one(b, e, None)
            dsum += a
            dgain += c
        one(b, s.ext - 1, inside(2 * s.rows, s, 2))
        terms[pl.ds(b, 1), : s.out] = jnp.sum(dgain, axis=0, keepdims=True)
        terms[pl.ds(b, 1), s.out : 2 * s.out] = jnp.sum(dsum, axis=0, keepdims=True)

    total = jnp.zeros((1, s.out), F32)
    cross = jnp.zeros((1, s.out), F32)
    for b in range(s.images):
        gain = 1.0 + proj[b : b + 1, base : base + s.out]
        cross += gain * terms[b : b + 1, : s.out]
        total += gain * terms[b : b + 1, s.out : 2 * s.out]
    line[...] = jnp.zeros_like(line)
    line[0:1, : s.out] = total
    line[0:1, s.slot : s.slot + s.out] = cross
    line[0:1, 2 * s.slot : 2 * s.slot + s.out] = misc[0:1, : s.out]
    whole = line[...]
    for d in range(s.devices):
        pay[d] = whole


def conv_two_kernel(sizes, slots, two, phases, grad_low, grad_skip, skip_part, image, spec,
                    out, mine, other, scale, pair, grads):
    s = sizes
    _, _, core = position()
    w = s.width
    depth = 3 * s.slot
    own = 2 * s.rows
    inv_two = spec[4:5, : s.out]
    bias = spec[6:7, : s.out]
    dots = jnp.zeros((1, s.out), F32)
    results = []
    for ph in range(2):
        total = None
        for dy in range(3):
            lhs = slots[:, dy : dy + own, :, ph * s.slot : ph * s.slot + depth]
            part = dot(lhs.reshape(s.images * own * w, depth), two[dy])
            total = part if total is None else total + part
        results.append(total.reshape(s.images, own, w, s.out))
    for b in range(s.images):
        for e in range(own):
            for ph in range(2):
                raw = results[ph][b, e]
                dots += jnp.sum(raw * phases[b, e, ph].astype(F32), axis=0, keepdims=True)
                value = raw * inv_two + skip_part[b, e // 2] + bias
                pair[0, pl.ds(ph, w, 2), :] = value[:, :LANES]
                pair[1, pl.ds(ph, w, 2), :] = jnp.concatenate(
                    [value[:, LANES:], jnp.zeros((w, 2 * LANES - s.out), F32)], axis=1
                )
            out[b, e, :, :LANES] = pair[0].astype(BF16)
            out[b, e, :, LANES:] = pair[1][:, : s.out - LANES].astype(BF16)
    scale[...] = jnp.broadcast_to(jnp.sum(dots, axis=1, keepdims=True), scale.shape)

    count = s.images * own * w
    flips = [
        jnp.transpose(grad_low[:, :, ph].reshape(count, s.out)) for ph in range(2)
    ]
    for dy in range(3):
        total = None
        for ph in range(2):
            rhs = slots[:, dy : dy + own, :, ph * s.slot : ph * s.slot + depth]
            part = dot(flips[ph], rhs.reshape(count, depth))
            total = part if total is None else total + part
        for dx in range(3):
            at = (3 * dy + dx) * s.out
            grads[:, at : at + s.out] = total[:, dx * s.slot : dx * s.slot + s.out]
    count = s.images * s.rows * w
    flip = jnp.transpose(grad_skip[...].reshape(count, s.out))
    grads[:, 9 * s.out : 9 * s.out + s.chan] = dot(flip, image[...].reshape(count, s.chan))
    half = s.out // 2
    for ref, which in ((mine, core), (other, 1 - core)):
        at = pl.multiple_of(which * half, 8)
        for r in range(s.rows_n):
            start = r * s.n_two
            ref[r, :, : s.n_two] = grads[pl.ds(at, half), start : start + s.n_two]
            start = 9 * s.out + r * s.n_skip
            ref[r, :, s.n_two :] = grads[pl.ds(at, half), start : start + s.n_skip]


def hidden_grad_kernel(sizes, counts, got, dnorm, hidden, stats, spec, acts, slots, mine, other,
                       scale, bias_grad, low, grads):
    s = sizes
    _, _, core = position()
    w = s.width
    sums = jnp.sum(got[...], axis=0)
    count = live_total(counts, s) * (4 * w * w)
    mean, rstd = stats[0:1, : s.out], stats[1:2, : s.out]
    inv = spec[3:4, : s.out]
    total = sums[:, : s.out] / count
    cross = sums[:, s.slot : s.slot + s.out] / count
    bias_grad[...] = jnp.broadcast_to(sums[:, 2 * s.slot :], bias_grad.shape)
    slots[...] = jnp.zeros_like(slots)
    norm_scale = inv * rstd
    offset = mean * rstd

    def one(b, e, keep, own):
        par, k = e % 2, e // 2
        dots = jnp.zeros((8, s.out), F32)
        for ph in range(2):
            raw = hidden[b, e, ph]
            normed = raw * norm_scale - offset
            grad = keep * (rstd * (dnorm[b, e, ph] - total - normed * cross))
            if own:
                dots += jnp.sum((grad * raw).reshape(w // 8, 8, s.out), axis=0)
            value = grad * inv
            small = value.astype(BF16)
            at = (1 + ph) * s.slot
            slots[b, par, k, :, at : at + s.out] = small
            if own:
                low[1 - par, ph, b, (e - 1) // 2] = small
            if ph == 1:
                slots[b, par, k, :, : s.out] = shifted(value, -1).astype(BF16)
            else:
                slots[b, par, k, :, 3 * s.slot : 3 * s.slot + s.out] = shifted(value, 1).astype(
                    BF16
                )
        return dots

    scale[...] = jnp.zeros_like(scale)

    @pl.loop(0, s.images)
    def _(b):
        live = live_of(counts, b)
        one(b, 0, live * inside(-1, s, 2), False)
        dots = jnp.zeros((8, s.out), F32)
        for e in range(1, s.ext - 1):
            dots += one(b, e, live, True)
        one(b, s.ext - 1, live * inside(2 * s.rows, s, 2), False)
        scale[0:1, : s.out] += jnp.sum(dots, axis=0, keepdims=True)

    count = s.images * s.rows * w
    depth = 3 * s.chan
    for dy in range(3):
        total = None
        for phase in range(4):
            a, b = divmod(phase, 2)
            flip = jnp.transpose(low[a, b].reshape(count, s.out))
            start = 1 + (a + dy - 1) // 2
            rhs = acts[:, start : start + s.rows, :, b * s.chan : b * s.chan + depth]
            part = dot(flip, rhs.reshape(count, depth))
            total = part if total is None else total + part
        grads[:, dy * depth : (dy + 1) * depth] = total
    half = s.out // 2
    for ref, which in ((mine, core), (other, 1 - core)):
        at = pl.multiple_of(which * half, 8)
        for r in range(s.rows_n):
            start = r * s.n_one
            ref[r] = grads[pl.ds(at, half), start : start + s.n_one]


def input_grad_kernel(sizes, slots, weight, image, stats, proj, terms_two, scale_one, scale_two,
                      misc, dnorm, pay, back, terms, line):
    s = sizes
    w = s.width
    depth = 3 * s.slot
    back[...] = jnp.zeros_like(back)
    for t in range(9):
        dy, dx = divmod(t, 3)
        tap = weight[t * s.chan : (t + 1) * s.chan, :].astype(F32)
        at = (2 - dx) * s.slot
        back[dy, at : at + s.out, :] = jnp.transpose(tap).astype(BF16)
    total = None
    for a in range(2):
        for dy in range(3):
            par, k = (a + 2 - dy) % 2, (a + 2 - dy) // 2
            for ph in range(2):
                lhs = slots[:, par, k : k + s.rows, :, ph * s.slot : ph * s.slot + depth]
                part = dot(lhs.reshape(s.images * s.rows * w, depth), back[dy])
                total = part if total is None else total + part
    total = total.reshape(s.images, s.rows, w, s.chan)
    mean, rstd = stats[0:1, :], stats[1:2, :]
    all_sum = jnp.zeros((1, s.chan), F32)
    all_cross = jnp.zeros((1, s.chan), F32)
    for b in range(s.images):
        gain = 1.0 + proj[b : b + 1, : s.chan]
        shift = proj[b : b + 1, s.chan : 2 * s.chan]
        dsum = jnp.zeros((8, s.chan), F32)
        dgain = jnp.zeros((8, s.chan), F32)
        for i in range(s.rows):
            normed = (image[b, i].astype(F32) - mean) * rstd
            pre = gain * normed + shift
            sig = sigmoid(pre)
            dpre = total[b, i] * (sig * (1.0 + pre * (1.0 - sig)))
            dnorm[b, i] = gain * dpre
            dsum += jnp.sum(dpre.reshape(w // 8, 8, s.chan), axis=0)
            dgain += jnp.sum((dpre * normed).reshape(w // 8, 8, s.chan), axis=0)
        dsum = jnp.sum(dsum, axis=0, keepdims=True)
        dgain = jnp.sum(dgain, axis=0, keepdims=True)
        terms[b : b + 1, : s.chan] = dgain
        terms[b : b + 1, s.chan : 2 * s.chan] = dsum
        terms[b : b + 1, 2 * s.chan :] = terms_two[b : b + 1, : 2 * s.out]
        all_sum += gain * dsum
        all_cross += gain * dgain
    line[...] = jnp.zeros_like(line)
    line[0:1, : s.chan] = all_sum
    line[0:1, s.chan : 2 * s.chan] = all_cross
    at = s.at_scale
    line[0:1, at : at + 1] = jnp.sum(scale_one[0:1, : s.out], axis=1, keepdims=True)
    line[0:1, at + 1 : at + 2] = scale_two[0:1, 0:1]
    line[0:1, at + 2 : at + 3] = jnp.sum(misc[1:2, : s.out], axis=1, keepdims=True)
    for r in range(s.rows_n):
        for b in range(s.images):
            at = s.at_terms + b * s.cols
            line[0:1, at : at + s.cols] = terms[b : b + 1, r * s.cols : (r + 1) * s.cols]
        whole = line[...]
        for g in range(s.groups):
            pay[r * s.groups + g] = whole


def adamw(weight, first_old, second, gradient, learn_rate):
    first_new = BETA_ONE * first_old + (1.0 - BETA_ONE) * gradient
    second_new = BETA_TWO * second + (1.0 - BETA_TWO) * gradient * gradient
    first_hat = first_new / (1.0 - BETA_ONE**STEP)
    second_hat = second_new / (1.0 - BETA_TWO**STEP)
    weight_new = weight - learn_rate * (
        first_hat / (jnp.sqrt(second_hat) + ADAM_EPS) + DECAY_RATE * weight
    )
    return (weight_new, first_new, second_new)


def store_adamw(refs, olds, gradient, rate):
    for ref, value in zip(refs, adamw(*(old[...] for old in olds), gradient, rate)):
        ref[...] = value


def finish_kernel(sizes, counts, got, cond_got, bias_got, image, dnorm, grad_skip, skip_w, stats, proj,
                  cw, cm, cv, bw, bm, bv,
                  image_grad, cw_new, cm_new, cv_new, bw_new, bm_new, bv_new, scales, terms, conds):
    s = sizes
    w = s.width
    row_pos, _, _ = position()
    sums = jnp.sum(got[:, :, : s.at_terms], axis=0)
    scales[...] = jnp.broadcast_to(sums[:, s.at_scale :], scales.shape)
    count = live_total(counts, s) * (w * w)
    total = sums[:, : s.chan] / count
    cross = sums[:, s.chan : 2 * s.chan] / count
    mean, rstd = stats[0:1, :], stats[1:2, :]
    grad = dot(
        grad_skip[...].reshape(s.images * s.rows * w, s.out), skip_w[...], ((1,), (1,))
    ).reshape(s.images, s.rows, w, s.chan)
    for b in range(s.images):
        keep = live_of(counts, b) * rstd
        for i in range(s.rows):
            normed = (image[b, i].astype(F32) - mean) * rstd
            image_grad[b, i] = keep * (dnorm[b, i] - total - normed * cross) + grad[b, i]
    for g in range(s.groups):
        part = got[g, :, s.at_terms :]
        for r in range(1, s.rows_n):
            part = part + got[r * s.groups + g, :, s.at_terms :]
        for b in range(s.images):
            k = g * s.images + b
            terms[k : k + 1, :] = part[:, b * s.cols : (b + 1) * s.cols]
            at = s.at_cond + b * s.cond
            conds[k : k + 1, :] = cond_got[g, :, at : at + s.cond]
    grad = dot(terms[...], conds[...], ((0,), (0,)), precise)
    store_adamw((cw_new, cm_new, cv_new), (cw, cm, cv), grad, LEARN_RATES[3])
    grad = bias_got[0:1, : s.n_bias]
    for r in range(1, s.rows_n):
        grad = jnp.where(row_pos == r, bias_got[0:1, r * s.n_bias : (r + 1) * s.n_bias], grad)
    store_adamw((bw_new, bm_new, bv_new), (bw, bm, bv), grad, LEARN_RATES[4])


def weights_kernel(sizes, one_grad, two_grad, scales, spec, left_one, left_two, left_skip,
                   ow, om, ov, tw, tm, tv, sw, sm, sv,
                   ow_new, om_new, ov_new, tw_new, tm_new, tv_new, sw_new, sm_new, sv_new):
    s = sizes
    columns = jnp.transpose(spec[...])

    def factor(k):
        inv = spec[3 + k : 4 + k, 0:1]
        return scales[0:1, k : k + 1] * inv * inv * spec[8 + k : 9 + k, 0:1]

    grad = one_grad[...] - columns[: s.out, 0:1] * (left_one[...] * factor(0))
    store_adamw((ow_new, om_new, ov_new), (ow, om, ov), grad, LEARN_RATES[0])
    both = two_grad[...]
    grad = both[:, : s.n_two] - columns[: s.out, 1:2] * (left_two[...] * factor(1))
    store_adamw((tw_new, tm_new, tv_new), (tw, tm, tv), grad, LEARN_RATES[1])
    grad = jnp.transpose(both[:, s.n_two :])
    grad = grad - (left_skip[...] * factor(2)) * spec[2:3, : s.out]
    store_adamw((sw_new, sm_new, sv_new), (sw, sm, sv), grad, LEARN_RATES[2])


def share(chunks):
    return lax.all_to_all(chunks, ALL, 0, 0, tiled=True)


def core_swap(values):
    return lax.ppermute(values, "core", [(0, 1), (1, 0)])


def row_swaps(near, far):
    devices = lax.axis_size("rows")
    pairs = [(i, i ^ 1) for i in range(devices)]
    odd = [(i, i + 1) for i in range(1, devices - 1, 2)]
    odd = odd + [(j, i) for i, j in odd]
    return lax.ppermute(near, "rows", pairs), lax.ppermute(far, "rows", odd)


def scatter_sum(mine, other):
    rows_n, half, width = mine.shape
    n_x = lax.axis_size("x")
    held = mine + core_swap(other)
    got = lax.all_to_all(held.reshape(rows_n * n_x, half // n_x, width), ("rows", "x"), 0, 0, tiled=True)
    total = jnp.sum(got.reshape(rows_n * n_x, half // n_x, width), axis=0)
    return lax.all_gather(total, ("core", "x"), axis=0, tiled=True)


def body(
    image_in,
    condition,
    group_counts,
    out_cotangent,
    power_vectors,
    conv1_weight,
    conv2_weight,
    skip_weight,
    cond_weight,
    out_bias,
    conv1_first,
    conv2_first,
    skip_first,
    cond_first,
    bias_first,
    conv1_second,
    conv2_second,
    skip_second,
    cond_second,
    bias_second,
):
    rows_n = lax.axis_size("rows")
    groups_n = lax.axis_size("x") * lax.axis_size("core")
    masters = [conv1_weight, conv2_weight, skip_weight, cond_weight, out_bias]
    s = Sizes(
        image_in.shape, out_cotangent.shape, condition.shape, [m.shape for m in masters], rows_n, groups_n
    )
    bind = functools.partial
    scratch = pltpu.VMEM
    n, w = s.images, s.width
    depth = 3 * s.slot

    pay, half_one, half_two, near, far, left_one, left_two, left_skip = run(
        bind(prep_kernel, s),
        [
            shape((s.devices, 1, s.pay_one)),
            shape((rows_n, s.h_one, s.out), BF16),
            shape((rows_n, s.h_two + s.h_skip, s.out), BF16),
            shape((n, s.edge, LANES), BF16),
            shape((n, s.edge, LANES), BF16),
            shape((1, s.n_one)),
            shape((1, s.n_two)),
            shape((s.n_skip, 1)),
        ],
        [
            group_counts,
            image_in,
            out_cotangent,
            condition,
            power_vectors,
            power_vectors.T,
            conv1_weight.T,
            conv2_weight.T,
            skip_weight,
            cond_weight.T,
            out_bias[None],
        ],
        [scratch((1, s.pay_one), F32)],
    )
    near, far = row_swaps(near, far)
    mine_one = lax.all_to_all(half_one, "rows", 0, 0, tiled=True)
    got_one = share(pay)
    mine_two = lax.all_to_all(half_two, "rows", 0, 0, tiled=True)
    other_one = core_swap(mine_one)
    other_two = core_swap(mine_two)

    acts, proj, stats_one, spec = run(
        bind(act_kernel, s),
        [
            shape((n, s.rows + 2, w, 4 * s.chan), BF16),
            shape((n, rows_n * s.cols)),
            shape((2, s.chan)),
            shape((16, s.slot)),
        ],
        [group_counts, got_one, image_in, near, far],
    )
    hidden, weight_one, pay = run(
        bind(conv_one_kernel, s),
        [
            shape((n, s.ext, 2, w, s.out)),
            shape((9 * s.chan, s.out), BF16),
            shape((s.devices, 1, s.pay_two)),
        ],
        [group_counts, acts, mine_one, other_one, condition],
        [scratch((1, s.pay_two), F32), scratch((9 * s.chan, s.out), F32)],
        flops=2 * n * s.ext * 2 * w * 9 * s.chan * s.out,
    )
    got_two = share(pay)
    dact, phases, grad_low, grad_skip, skip_part, weight_two, weight_skip, misc = run(
        bind(cot_kernel, s),
        [
            shape((n, s.ext, 2, w, s.out)),
            shape((n, 2 * s.rows, 2, w, s.out), BF16),
            shape((n, 2 * s.rows, 2, w, s.out), BF16),
            shape((n, s.rows, w, s.out), BF16),
            shape((n, s.rows, w, s.out)),
            shape((3, depth, s.out), BF16),
            shape((s.chan, s.out), BF16),
            shape((8, s.slot)),
        ],
        [group_counts, out_cotangent, near, far, image_in, mine_two, other_two, spec],
        [
            scratch((n, 2 * s.rows + 4, w, 4 * s.slot), BF16),
            scratch((9 * s.out + s.chan, s.out), F32),
            scratch((2, 2 * w, LANES), F32),
            scratch((3, depth, s.out), BF16),
        ],
        flops=2 * n * s.ext * 2 * w * 9 * s.out * s.out,
    )
    slots_two, dnorm, stats_two, terms_two, pay = run(
        bind(norm_two_kernel, s),
        [
            shape((n, s.ext, w, 4 * s.slot), BF16),
            shape((n, s.ext, 2, w, s.out)),
            shape((2, s.slot)),
            shape((8, 2 * s.slot)),
            shape((s.devices, 1, s.pay_three)),
        ],
        [group_counts, got_two, hidden, dact, spec, proj, misc],
        [scratch((1, s.pay_three), F32)],
    )
    got_three = share(pay)
    out_image, mine, other, scale_two = run(
        bind(conv_two_kernel, s),
        [
            shape(out_cotangent.shape, BF16),
            shape((rows_n, s.out // 2, s.n_two + s.n_skip)),
            shape((rows_n, s.out // 2, s.n_two + s.n_skip)),
            shape((8, LANES)),
        ],
        [slots_two, weight_two, phases, grad_low, grad_skip, skip_part, image_in, spec],
        [scratch((2, 2 * w, LANES), F32), scratch((s.out, 9 * s.out + s.chan), F32)],
        scalars=0,
        flops=8 * n * s.rows * 2 * w * 9 * s.out * s.out,
    )
    two_grad = scatter_sum(mine, other)
    slots_one, mine, other, scale_one, bias_grad = run(
        bind(hidden_grad_kernel, s),
        [
            shape((n, 2, s.rows + 1, w, 4 * s.slot), BF16),
            shape((rows_n, s.out // 2, s.n_one)),
            shape((rows_n, s.out // 2, s.n_one)),
            shape((8, s.slot)),
            shape((8, s.slot)),
        ],
        [group_counts, got_three, dnorm, hidden, stats_two, spec, acts],
        [scratch((2, 2, n, s.rows, w, s.out), BF16), scratch((s.out, 9 * s.chan), F32)],
        flops=8 * n * s.rows * w * 9 * s.chan * s.out,
    )
    one_grad = scatter_sum(mine, other)
    dnorm_one, pay = run(
        bind(input_grad_kernel, s),
        [shape((n, s.rows, w, s.chan)), shape((s.devices, 1, s.pay_four))],
        [slots_one, weight_one, image_in, stats_one, proj, terms_two, scale_one, scale_two, misc],
        [
            scratch((3, depth, s.chan), BF16),
            scratch((8, rows_n * s.cols), F32),
            scratch((1, s.pay_four), F32),
        ],
        scalars=0,
        flops=8 * n * s.rows * w * 9 * s.chan * s.out,
    )
    got_four = share(pay)
    moments = [cond_weight, cond_first, cond_second]
    biases = [out_bias, bias_first, bias_second]
    image_grad, *rest, scales = run(
        bind(finish_kernel, s),
        [
            shape(image_in.shape),
            *[shape((s.cols, s.cond))] * 3,
            *[shape((1, s.n_bias))] * 3,
            shape((8, LANES)),
        ],
        [
            group_counts,
            got_four,
            got_two,
            bias_grad,
            image_in,
            dnorm_one,
            grad_skip,
            weight_skip,
            stats_one,
            proj,
            *[m.T for m in moments],
            *[b[None] for b in biases],
        ],
        [
            scratch((groups_n * n, s.cols), F32),
            scratch((groups_n * n, s.cond), F32),
        ],
    )
    cond_new = [c.T for c in rest[:3]]
    bias_new = [b[0] for b in rest[3:]]
    olds = [
        *[m.T for m in (conv1_weight, conv1_first, conv1_second)],
        *[m.T for m in (conv2_weight, conv2_first, conv2_second)],
        skip_weight,
        skip_first,
        skip_second,
    ]
    news = run(
        bind(weights_kernel, s),
        [shape(o.shape) for o in olds],
        [one_grad, two_grad, scales, spec, left_one, left_two, left_skip, *olds],
        scalars=0,
    )
    weights_new = [m.T for m in news[:6]] + list(news[6:])
    return (out_image, image_grad, *weights_new, *cond_new, *bias_new)


def solution(mesh):
    rows_n, imgs_n = mesh.devices.shape
    fine = Mesh(np.asarray(mesh.devices).reshape(rows_n, imgs_n // 2, 2), ALL)
    groups = ("x", "core")
    picture = P(groups, "rows", None, None)
    weight = P("rows", None)
    column = P(None, "rows")
    masters = (weight, weight, weight, column, P("rows"))
    return jax.shard_map(
        body,
        mesh=fine,
        in_specs=(picture, P(groups, None), P(), picture, P(), *masters, *masters, *masters),
        out_specs=(
            picture,
            picture,
            *(weight,) * 9,
            *(column,) * 3,
            *(P("rows"),) * 3,
        ),
        check_vma=False,
    )
```

time: 675 us -> 285 us (0.42)
  blocking collectives: 308 us -> 48.3 us
  matrix products: 60.1 us -> 0 us
  other arithmetic: 51.6 us -> 6.77 us
  Pallas kernels: 0 us -> 43.5 us
  local copies, waits for them, and re-layouts: 89.9 us -> 60.1 us
  waiting for transfers between devices: 103 us -> 76.3 us
  between operations: 26.3 us -> 1.3 us
  starting transfers between devices: 27 us -> 44.8 us
    psum x5 -> x0, blocking collectives: 169 us -> none  [the longest x1 41.8 us: body(): lax.psum((jnp.sum(normgrad_two, axis=(0, 1, 2)), jnp.sum(normgrad_two * n...]
    all_gather x3 -> x2, blocking collectives: 97.2 us -> 24.6 us  [scatter_sum(): return lax.all_gather(total, ('core', 'x'), axis=0, tiled=True)]
    unnamed x9 -> x0, waiting for transfers between devices: 68.4 us -> none
    all_to_all x0 -> x7, waiting for transfers between devices: none -> 54 us  [the longest x2 40.1 us: scatter_sum(): lax.all_to_all(held.reshape(rows_n * n_x, half // n_x, width), ('rows', '...]
    pallas_call x0 -> x10, Pallas kernels: none -> 43.5 us  [run(): pl.pallas_call(kernel, out_shape=tuple(outs), in_specs=specs, out_specs=t...]
    unnamed x2 -> x0, blocking collectives: 41.8 us -> none
    all_to_all x0 -> x7, starting transfers between devices: none -> 41.5 us  [the longest x4 25.6 us: share(): return lax.all_to_all(chunks, ALL, 0, 0, tiled=True)]
    dot_general x29 -> x0, matrix products: 35.5 us -> none  [the longest x18 25.8 us: tap_grads(): jnp.einsum('irwc,irwo->co', padded[:, tap_row:tap_row + height, tap_col:t...]
  transfers between devices with their start and end apart: 14 -> 13, of which waited for: 4 -> 6; matrix products, arithmetic and copies ran while one was open for 20% -> 5% of each run, Pallas kernels for 0% -> 13%
where the time goes in v1:
time: 285 us; the launch traced here: 281 us
  waiting for transfers between devices  76.3 us (27%)
  local copies, waits for them, and re-layouts  60.1 us (21%)
  blocking collectives  48.3 us (17%)
  starting transfers between devices  44.8 us (16%)
  Pallas kernels  43.5 us (15%)
  other arithmetic  6.77 us (2%)
    unnamed x175, local copies, waits for them, and re-layouts  50.9 us
    pallas_call x10, Pallas kernels, run(): pl.pallas_call(kernel, out_shape=tuple(outs), in_specs=specs, out_specs=t...  43.5 us
    all_to_all x2, waiting for transfers between devices, scatter_sum(): lax.all_to_all(held.reshape(rows_n * n_x, half // n_x, width), ('rows', '...  40.1 us
    all_to_all x4, starting transfers between devices, share(): return lax.all_to_all(chunks, ALL, 0, 0, tiled=True)  25.6 us
    all_gather x2, blocking collectives, scatter_sum(): return lax.all_gather(total, ('core', 'x'), axis=0, tiled=True)  24.6 us
    all_to_all x1, blocking collectives, body(): mine_one = lax.all_to_all(half_one, 'rows', 0, 0, tiled=True)  23.7 us
    ppermute x2, waiting for transfers between devices, row_swaps(): return (lax.ppermute(near, 'rows', pairs), lax.ppermute(far, 'rows', odd))  19.1 us
    all_to_all x4, waiting for transfers between devices, share(): return lax.all_to_all(chunks, ALL, 0, 0, tiled=True)  13.9 us
  transfers between devices with their start and end apart: 13, of which 6 were waited for; matrix products, arithmetic and copies ran while one was open for 5% of the time, Pallas kernels for 13%

profile of v1, /device:TPU:0, one launch (start us, length us, event | category | flops | bytes accessed | tf_op | source)
XLA Modules:
  0.0 281.0 jit_solution(12621953853525238576)
XLA Ops:
  13.9 7.3 %all-to-all-start = ((f32[32,1,2304]{2,1,0:T(1,128)}), f32[32,1,2304]{2,1,0:T(1,128)S(1)}, u32[]{:S(2)}, u32[]{:S(2)}) async-start(f32[32,1,2304]{2,1,0:T(1,128)} %get-tuple-element.73), calls=%async_computation | async-start | bytes 589824 | tf_op jit(solution)/shard_map/all_to_all | solution.py:752
  22.4 10.1 %all-to-all-done.got = f32[32,1,2304]{2,1,0:T(1,128)S(1)} async-done(((f32[32,1,2304]{2,1,0:T(1,128)}), f32[32,1,2304]{2,1,0:T(1,128)S(1)}, u32[]{:S(2)}, u32[]{:S(2)}) %all-to-all-start) | async-done | bytes 294944 | tf_op jit(solution)/shard_map/all_to_all | solution.py:752
  32.6 23.7 %all_to_all.40 = bf16[8,216,192]{1,2,0:T(8,128)(2,1)S(1)} all-to-all(bf16[8,216,192]{1,2,0:T(8,128)(2,1)} %copy.39), channel_id=1, replica_groups=mesh['rows'=8,'x'=2,'core'=2] {'rows'}, dimensions={0} | all-to-all | bytes 1327104 | tf_op jit(solution)/shard_map/all_to_all | solution.py:837
  56.3 4.2 %all-to-all-start.3 = ((bf16[8,136,192]{2,1,0:T(8,128)(2,1)}), bf16[8,136,192]{2,1,0:T(8,128)(2,1)}, u32[]{:S(2)}, u32[]{:S(2)}) async-start(bf16[8,136,192]{2,1,0:T(8,128)(2,1)} %get-tuple-element.80), calls=%async_computation.3 | async-start | bytes 1114112 | tf_op jit(solution)/shard_map/all_to_all | solution.py:839
  63.0 19.1 %collective-permute-done.near = bf16[4,352,128]{2,1,0:T(8,128)(2,1)S(1)} collective-permute-done((bf16[4,352,128]{2,1,0:T(8,128)(2,1)S(1)}, bf16[4,352,128]{2,1,0:T(8,128)(2,1)S(1)}, u32[]{:S(2)}, u32[]{:S(2)}) %collective-permute-start) | collective-permute-done | bytes 360480 | tf_op jit(solution)/shard_map/ppermute | solution.py:764
  93.0 6.2 %shard_map.325 = (f32[4,10,2,32,192]{4,3,2,1,0:T(8,128)S(1)}, bf16[3456,192]{1,0:T(8,128)(2,1)S(1)}, f32[32,1,1152]{2,1,0:T(1,128)S(1)}) custom-call(s32[4]{0:T(128)S(1)} %copy-done.49, bf16[4,6,32,1536]{3,2,1,0:T(8,128)(2,1)S(1)} %copy-done.68, bf16[8,216,192]{2,1,0:T(8,128)(2,1)S(1)} %copy-done.13, bf16[8,216,192]{2,1,0:T(8,128)(2,1)S(1)} %copy-done.14, ...), custom_call_target="tpu_custom_call" | custom-call | flops 3397386240 | bytes 7128240 | tf_op jit(solution)/shard_map/pallas_call | solution.py:35
  101.2 6.6 %all-to-all-start.2 = ((f32[32,1,1152]{2,1,0:T(1,128)}), f32[32,1,1152]{2,1,0:T(1,128)S(1)}, u32[]{:S(2)}, u32[]{:S(2)}) async-start(f32[32,1,1152]{2,1,0:T(1,128)} %copy-done.33), calls=%async_computation.2 | async-start | bytes 294912 | tf_op jit(solution)/shard_map/all_to_all | solution.py:752
  110.7 7.1 %shard_map.326 = (f32[4,10,2,32,192]{4,3,2,1,0:T(8,128)S(1)}, bf16[4,8,2,32,192]{4,3,2,1,0:T(8,128)(2,1)S(1)}, bf16[4,8,2,32,192]{4,3,2,1,0:T(8,128)(2,1)S(1)}, ...) custom-call(s32[4]{0:T(128)S(1)} %copy-done.49, ...), custom_call_target="tpu_custom_call" | custom-call | flops 1698693120 | bytes 7921680 | tf_op jit(solution)/shard_map/pallas_call | solution.py:35
  126.9 3.0 %shard_map.327 = (bf16[4,10,32,1024]{3,2,1,0:T(8,128)(2,1)S(1)}, f32[4,10,2,32,192]{4,3,2,1,0:T(8,128)S(1)}, f32[2,256]{1,0:T(2,128)S(1)}, f32[8,512]{1,0:T(8,128)S(1)}, f32[32,1,768]{2,1,0:T(1,128)S(1)}) custom-call(s32[4]{0:T(128)S(1)} %copy-done.49, f32[32,1,1152]{2,1,0:T(1,128)S(1)} %all-to-all-done.2.got.cond_got, ...), custom_call_target="tpu_custom_call" | custom-call | bytes 8826896 | tf_op jit(solution)/shard_map/pallas_call | solution.py:35
  135.0 6.0 %all-to-all-start.4 = ((f32[32,1,768]{2,1,0:T(1,128)}), f32[32,1,768]{2,1,0:T(1,128)S(1)}, u32[]{:S(2)}, u32[]{:S(2)}) async-start(f32[32,1,768]{2,1,0:T(1,128)} %copy-done.34), calls=%async_computation.4 | async-start | bytes 196608 | tf_op jit(solution)/shard_map/all_to_all | solution.py:752
  148.2 6.6 %shard_map.328 = (bf16[4,8,64,192]{3,2,1,0:T(8,128)(2,1)}, f32[8,96,264]{2,1,0:T(8,128)S(1)}, f32[8,96,264]{2,1,0:T(8,128)S(1)}, f32[8,128]{1,0:T(8,128)S(1)}) custom-call(bf16[4,10,32,1024]{3,2,1,0:T(8,128)(2,1)S(1)} %copy-done.66, bf16[3,768,192]{2,1,0:T(8,128)(2,1)S(1)} %copy-done.76, bf16[4,8,2,32,192]{4,3,2,1,0:T(8,128)(2,1)S(1)} %copy-done.78, ...), custom_call_target="tpu_custom_call" | custom-call | flops 2717908992 | bytes 8491008 | tf_op jit(solution)/shard_map/pallas_call | solution.py:35
  156.9 2.7 copy.42
  164.5 5.9 %shard_map.329 = (bf16[4,2,5,32,1024]{4,3,2,1,0:T(8,128)(2,1)S(1)}, f32[8,96,432]{2,1,0:T(8,128)S(1)}, f32[8,96,432]{2,1,0:T(8,128)S(1)}, f32[8,256]{1,0:T(8,128)S(1)}, f32[8,256]{1,0:T(8,128)S(1)}) custom-call(s32[4]{0:T(128)S(1)} %copy-done.49, f32[32,1,768]{2,1,0:T(1,128)S(1)} %all-to-all-done.4.got, f32[4,10,2,32,192]{4,3,2,1,0:T(8,128)S(1)} %copy-done.64, ...), custom_call_target="tpu_custom_call" | custom-call | flops 2717908992 | bytes 11700240 | tf_op jit(solution)/shard_map/pallas_call | solution.py:35
  170.5 6.3 %shard_map.330 = (f32[4,4,32,384]{3,2,1,0:T(8,128)S(1)}, f32[32,1,1536]{2,1,0:T(1,128)}) custom-call(bf16[4,2,5,32,1024]{4,3,2,1,0:T(8,128)(2,1)S(1)} %get-tuple-element.95.slots, bf16[3456,192]{1,0:T(8,128)(2,1)S(1)} %copy-done.82, bf16[4,4,32,384]{3,2,1,0:T(8,128)(2,1)S(1)} %copy-done.1, f32[2,384]{1,0:T(2,128)S(1)} %copy-done.51, ...), custom_call_target="tpu_custom_call" | custom-call | flops 2717908992 | bytes 5383168 | tf_op jit(solution)/shard_map/pallas_call | solution.py:35
  176.9 5.7 %all-to-all-start.5 = ((f32[32,1,1536]{2,1,0:T(1,128)}), f32[32,1,1536]{2,1,0:T(1,128)S(1)}, u32[]{:S(2)}, u32[]{:S(2)}) async-start(f32[32,1,1536]{2,1,0:T(1,128)} %get-tuple-element.101), calls=%async_computation.5 | async-start | bytes 393216 | tf_op jit(solution)/shard_map/all_to_all | solution.py:752
  182.6 2.7 copy.43
  187.8 3.7 %all-to-all-done.5.got = f32[32,1,1536]{2,1,0:T(1,128)S(1)} async-done(((f32[32,1,1536]{2,1,0:T(1,128)}), f32[32,1,1536]{2,1,0:T(1,128)S(1)}, u32[]{:S(2)}, u32[]{:S(2)}) %all-to-all-start.5) | async-done | bytes 196640 | tf_op jit(solution)/shard_map/all_to_all | solution.py:752
  191.5 4.4 %all-to-all-start.7 = ((f32[16,48,264]{2,1,0:T(8,128)}), f32[16,48,264]{2,1,0:T(8,128)}, u32[]{:S(2)}, u32[]{:S(2)}) async-start(f32[16,48,264]{2,1,0:T(8,128)} %bitcast.45), calls=%async_computation.7 | async-start | bytes 2359296 | tf_op jit(solution)/shard_map/all_to_all | solution.py:771
  196.5 3.2 %collective-permute-done.4 = f32[8,96,432]{2,1,0:T(8,128)S(1)} collective-permute-done((f32[8,96,432]{2,1,0:T(8,128)}, f32[8,96,432]{2,1,0:T(8,128)S(1)}, u32[]{:S(2)}, u32[]{:S(2)}) %collective-permute-start.4) | collective-permute-done | bytes 1327136 | tf_op jit(solution)/shard_map/ppermute | solution.py:756
  201.3 22.4 %all-to-all-done.7 = f32[16,48,264]{2,1,0:T(8,128)} async-done(((f32[16,48,264]{2,1,0:T(8,128)}), f32[16,48,264]{2,1,0:T(8,128)}, u32[]{:S(2)}, u32[]{:S(2)}) %all-to-all-start.7) | async-done | bytes 811040 | tf_op jit(solution)/shard_map/all_to_all | solution.py:771
  223.7 7.3 %all-to-all-start.6 = ((f32[16,48,432]{2,1,0:T(8,128)}), f32[16,48,432]{2,1,0:T(8,128)}, u32[]{:S(2)}, u32[]{:S(2)}) async-start(f32[16,48,432]{2,1,0:T(8,128)} %bitcast.44), calls=%async_computation.6 | async-start | bytes 3145728 | tf_op jit(solution)/shard_map/all_to_all | solution.py:771
  234.9 12.7 %all_gather.7.two_grad = f32[192,264]{1,0:T(8,128)S(1)} all-gather(f32[48,264]{1,0:T(8,128)S(1)} %reduce_sum.19), channel_id=1, replica_groups=mesh['rows'=8,'x'=2,'core'=2] {'core','x'}, dimensions={0}, use_global_device_ids=true | all-gather | bytes 253440 | tf_op jit(solution)/shard_map/all_gather | solution.py:773
  247.6 17.7 %all-to-all-done.6 = f32[16,48,432]{2,1,0:T(8,128)} async-done(((f32[16,48,432]{2,1,0:T(8,128)}), f32[16,48,432]{2,1,0:T(8,128)}, u32[]{:S(2)}, u32[]{:S(2)}) %all-to-all-start.6) | async-done | bytes 1327136 | tf_op jit(solution)/shard_map/all_to_all | solution.py:771
  266.8 11.9 %all_gather.6.one_grad = f32[192,432]{1,0:T(8,128)S(1)} all-gather(f32[48,432]{1,0:T(8,128)S(1)} %reduce_sum.18), channel_id=1, replica_groups=mesh['rows'=8,'x'=2,'core'=2] {'core','x'}, dimensions={0}, use_global_device_ids=true | all-gather | bytes 414720 | tf_op jit(solution)/shard_map/all_gather | solution.py:773
  (199 shorter events, 73.0 us)
Async XLA Ops:
  13.9 18.7 %all-to-all-start = ((f32[32,1,2304]{2,1,0:T(1,128)}), f32[32,1,2304]{2,1,0:T(1,128)S(1)}, u32[]{:S(2)}, u32[]{:S(2)}) async-start(f32[32,1,2304]{2,1,0:T(1,128)} %get-tuple-element.73), calls=%async_computation | async-start | bytes 589824 | tf_op jit(solution)/shard_map/all_to_all | solution.py:752
  22.4 59.7 %copy-start.1 = (bf16[4,4,32,384]{3,2,1,0:T(8,128)(2,1)S(1)}, bf16[4,4,32,384]{3,2,1,0:T(8,128)(2,1)}, u32[]{:S(2)}) copy-start(bf16[4,4,32,384]{3,2,1,0:T(8,128)(2,1)} %image.11) | copy-start | bytes 1179652
  22.4 59.7 %copy-start.49 = (s32[4]{0:T(128)S(1)}, s32[4]{0:T(128)}, u32[]{:S(2)}) copy-start(s32[4]{0:T(128)} %counts.13) | copy-start | bytes 52
  56.3 30.2 %all-to-all-start.3 = ((bf16[8,136,192]{2,1,0:T(8,128)(2,1)}), bf16[8,136,192]{2,1,0:T(8,128)(2,1)}, u32[]{:S(2)}, u32[]{:S(2)}) async-start(bf16[8,136,192]{2,1,0:T(8,128)(2,1)} %get-tuple-element.80), calls=%async_computation.3 | async-start | bytes 1114112 | tf_op jit(solution)/shard_map/all_to_all | solution.py:839
  60.5 27.3 %collective-permute-start.2 = (bf16[8,216,192]{1,2,0:T(8,128)(2,1)S(1)}, bf16[8,216,192]{1,2,0:T(8,128)(2,1)S(1)}, u32[]{:S(2)}, u32[]{:S(2)}) collective-permute-start(bf16[8,216,192]{1,2,0:T(8,128)(2,1)S(1)} %all_to_all.40), channel_id=1, source_target_pairs={{0,1},{1,0},{2,3},{3,2},{4,5},{5,4},{6,7},{7,6},{8,9},{9,8},{10,11... | collective-permute-start | bytes 1990664 | tf_op jit(solution)/shard_map/ppermute | solution.py:756
  60.5 21.6 %collective-permute-start = (bf16[4,352,128]{2,1,0:T(8,128)(2,1)S(1)}, bf16[4,352,128]{2,1,0:T(8,128)(2,1)S(1)}, u32[]{:S(2)}, u32[]{:S(2)}) collective-permute-start(bf16[4,352,128]{2,1,0:T(8,128)(2,1)S(1)} %get-tuple-element.74), channel_id=1, source_target_pairs={{0,4},{4,0},{8,12},{12,8},{16,20},{20,16},{24,28},{28,24},{1,5},{5... | collective-permute-start | bytes 1081352 | tf_op jit(solution)/shard_map/ppermute | solution.py:764
  62.4 19.8 %collective-permute-start.1 = (bf16[4,352,128]{2,1,0:T(8,128)(2,1)S(1)}, bf16[4,352,128]{2,1,0:T(8,128)(2,1)S(1)}, u32[]{:S(2)}, u32[]{:S(2)}) collective-permute-start(bf16[4,352,128]{2,1,0:T(8,128)(2,1)S(1)} %get-tuple-element.75), channel_id=1, source_target_pairs={{4,8},{12,16},{20,24},{8,4},{16,12},{24,20},{5,9},{13,17},{21,25},... | collective-permute-start | bytes 1081352 | tf_op jit(solution)/shard_map/ppermute | solution.py:764
  86.5 21.3 %collective-permute-start.3 = (bf16[8,136,192]{2,1,0:T(8,128)(2,1)}, bf16[8,136,192]{2,1,0:T(8,128)(2,1)}, u32[]{:S(2)}, u32[]{:S(2)}) collective-permute-start(bf16[8,136,192]{2,1,0:T(8,128)(2,1)} %all-to-all-done.3.mine), channel_id=1, source_target_pairs={{0,1},{1,0},{2,3},{3,2},{4,5},{5,4},{6,7},{7,6},{8,9},{9,8},{10,11... | collective-permute-start | bytes 1253384 | tf_op jit(solution)/shard_map/ppermute | solution.py:756
  101.2 23.3 %all-to-all-start.2 = ((f32[32,1,1152]{2,1,0:T(1,128)}), f32[32,1,1152]{2,1,0:T(1,128)S(1)}, u32[]{:S(2)}, u32[]{:S(2)}) async-start(f32[32,1,1152]{2,1,0:T(1,128)} %copy-done.33), calls=%async_computation.2 | async-start | bytes 294912 | tf_op jit(solution)/shard_map/all_to_all | solution.py:752
  135.0 24.7 %all-to-all-start.4 = ((f32[32,1,768]{2,1,0:T(1,128)}), f32[32,1,768]{2,1,0:T(1,128)S(1)}, u32[]{:S(2)}, u32[]{:S(2)}) async-start(f32[32,1,768]{2,1,0:T(1,128)} %copy-done.34), calls=%async_computation.4 | async-start | bytes 196608 | tf_op jit(solution)/shard_map/all_to_all | solution.py:752
  159.6 23.0 %collective-permute-start.5 = (f32[8,96,264]{1,2,0:T(8,128)}, f32[8,96,264]{1,2,0:T(8,128)}, u32[]{:S(2)}, u32[]{:S(2)}) collective-permute-start(f32[8,96,264]{1,2,0:T(8,128)} %copy.42), channel_id=1, source_target_pairs={{0,1},{1,0},{2,3},{3,2},{4,5},{5,4},{6,7},{7,6},{8,9},{9,8},{10,11... | collective-permute-start | bytes 2433032 | tf_op jit(solution)/shard_map/ppermute | solution.py:756
  176.9 14.6 %all-to-all-start.5 = ((f32[32,1,1536]{2,1,0:T(1,128)}), f32[32,1,1536]{2,1,0:T(1,128)S(1)}, u32[]{:S(2)}, u32[]{:S(2)}) async-start(f32[32,1,1536]{2,1,0:T(1,128)} %get-tuple-element.101), calls=%async_computation.5 | async-start | bytes 393216 | tf_op jit(solution)/shard_map/all_to_all | solution.py:752
  191.5 32.2 %all-to-all-start.7 = ((f32[16,48,264]{2,1,0:T(8,128)}), f32[16,48,264]{2,1,0:T(8,128)}, u32[]{:S(2)}, u32[]{:S(2)}) async-start(f32[16,48,264]{2,1,0:T(8,128)} %bitcast.45), calls=%async_computation.7 | async-start | bytes 2359296 | tf_op jit(solution)/shard_map/all_to_all | solution.py:771
  195.9 3.9 %collective-permute-start.4 = (f32[8,96,432]{2,1,0:T(8,128)}, f32[8,96,432]{2,1,0:T(8,128)S(1)}, u32[]{:S(2)}, u32[]{:S(2)}) collective-permute-start(f32[8,96,432]{2,1,0:T(8,128)} %copy-done.70), channel_id=1, source_target_pairs={{0,1},{1,0},{2,3},{3,2},{4,5},{5,4},{6,7},{7,6},{8,9},{9,8},{10,11... | collective-permute-start | bytes 3981320 | tf_op jit(solution)/shard_map/ppermute | solution.py:756
  223.7 41.5 %all-to-all-start.6 = ((f32[16,48,432]{2,1,0:T(8,128)}), f32[16,48,432]{2,1,0:T(8,128)}, u32[]{:S(2)}, u32[]{:S(2)}) async-start(f32[16,48,432]{2,1,0:T(8,128)} %bitcast.44), calls=%async_computation.6 | async-start | bytes 3145728 | tf_op jit(solution)/shard_map/all_to_all | solution.py:771
  234.7 43.9 %copy-start.7 = (f32[432,192]{0,1:T(8,128)S(1)}, f32[432,192]{0,1:T(8,128)}, u32[]{:S(2)}) copy-start(f32[432,192]{0,1:T(8,128)} %param.25) | copy-start | bytes 995332
  234.7 43.9 %copy-start.16 = (f32[216,192]{0,1:T(8,128)S(1)}, f32[216,192]{0,1:T(8,128)}, u32[]{:S(2)}) copy-start(f32[216,192]{0,1:T(8,128)} %param.26) | copy-start | bytes 497668
  234.8 43.9 %copy-start.19 = (f32[432,192]{0,1:T(8,128)S(1)}, f32[432,192]{0,1:T(8,128)}, u32[]{:S(2)}) copy-start(f32[432,192]{0,1:T(8,128)} %param.30) | copy-start | bytes 995332
  234.8 43.9 %copy-start.20 = (f32[432,192]{0,1:T(8,128)S(1)}, f32[432,192]{0,1:T(8,128)}, u32[]{:S(2)}) copy-start(f32[432,192]{0,1:T(8,128)} %param.35) | copy-start | bytes 995332
  234.8 43.9 %copy-start.27 = (f32[216,192]{0,1:T(8,128)S(1)}, f32[216,192]{0,1:T(8,128)}, u32[]{:S(2)}) copy-start(f32[216,192]{0,1:T(8,128)} %param.31) | copy-start | bytes 497668
  234.8 43.9 %copy-start.28 = (f32[216,192]{0,1:T(8,128)S(1)}, f32[216,192]{0,1:T(8,128)}, u32[]{:S(2)}) copy-start(f32[216,192]{0,1:T(8,128)} %param.36) | copy-start | bytes 497668
  234.8 43.9 %copy-start.30 = (f32[48,192]{1,0:T(8,128)S(1)}, f32[48,192]{1,0:T(8,128)}, u32[]{:S(2)}) copy-start(f32[48,192]{1,0:T(8,128)} %sw.1) | copy-start | bytes 110596
  234.8 43.9 %copy-start.40 = (f32[16,256]{1,0:T(8,128)S(1)}, f32[16,256]{1,0:T(8,128)}, u32[]{:S(2)}) copy-start(f32[16,256]{1,0:T(8,128)} %copy-done.35) | copy-start | bytes 49156
  234.8 43.9 %copy-start.41 = (f32[48,192]{1,0:T(8,128)S(1)}, f32[48,192]{1,0:T(8,128)}, u32[]{:S(2)}) copy-start(f32[48,192]{1,0:T(8,128)} %sm.1) | copy-start | bytes 110596
  (76 other events, 375.3 us)

commit v2 on v1

--- a/solution.py
+++ b/solution.py
@@ -20,17 +20,25 @@
 ALL = ("rows", "x", "core")
 F32, BF16 = jnp.float32, jnp.bfloat16
 LANES = 128
-VMEM_LIMIT = 40 * 2**20
+VMEM_LIMIT = 60 * 2**20
 
 
 def shape(dims, kind=F32):
     return jax.ShapeDtypeStruct(tuple(dims), kind)
 
 
-def run(kernel, outs, args, scratch=(), scalars=1, flops=0, limit=VMEM_LIMIT):
+def skipping(kernel, start, count):
+    return lambda *refs: kernel(*refs[:start], *refs[start + count :])
+
+
+def run(kernel, outs, args, scratch=(), scalars=1, flops=0, limit=VMEM_LIMIT, after=(), whole=()):
     spec = pl.BlockSpec(memory_space=pltpu.VMEM)
     specs = [pl.BlockSpec(memory_space=pltpu.SMEM)] * scalars + [spec] * (len(args) - scalars)
+    specs += [pl.BlockSpec(memory_space=pl.ANY)] * (len(whole) + len(after))
     moved = sum(a.size * a.dtype.itemsize for a in args)
+    args = [*args, *whole, *after]
+    if after:
+        kernel = skipping(kernel, len(args) - len(after), len(after))
     moved += sum(np.prod(o.shape) * np.dtype(o.dtype).itemsize for o in outs)
     return pl.pallas_call(
         kernel,
@@ -50,7 +58,7 @@
 
 
 class Sizes:
-    def __init__(self, image, cot, condition, masters, rows_n, groups_n):
+    def __init__(self, image, cot, condition, masters, rows_n, n_x):
         self.images, self.rows, self.width, self.chan = image
         self.out = cot[3]
         self.slot = round_up(self.out, LANES)
@@ -59,23 +67,98 @@
         self.n_one, self.n_two, self.n_skip = masters[0][0], masters[1][0], masters[2][0]
         self.cols = masters[3][1]
         self.n_bias = masters[4][0]
-        self.rows_n, self.groups = rows_n, groups_n
-        self.devices = rows_n * groups_n
+        self.rows_n, self.groups = rows_n, 2 * n_x
+        self.devices = rows_n * self.groups
         self.h_one = round_up(-(-self.n_one // 2), 8)
         self.h_two = round_up(-(-self.n_two // 2), 8)
         self.h_skip = round_up(-(-self.n_skip // 2), 8)
+        self.pack_one = round_up(packed_rows(self.h_one), 16)
+        self.pack_two = round_up(packed_rows(self.h_two + self.h_skip), 16)
         self.at_power = 2 * self.chan
-        self.at_norm = self.at_power + 3 * self.slot
+        self.at_norm = self.at_power + 3 * self.out
         self.at_bias = self.at_norm + 8
         self.at_proj = round_up(self.at_bias + self.n_bias, LANES)
         self.pay_one = round_up(self.at_proj + self.images * self.cols, LANES)
-        self.at_cond = 2 * self.slot
-        self.pay_two = round_up(self.at_cond + self.images * self.cond, LANES)
-        self.pay_three = 3 * self.slot
+        self.pay_two = round_up(2 * self.out, LANES)
         self.at_scale = 2 * self.chan
-        self.at_terms = self.at_scale + LANES
-        self.pay_four = round_up(self.at_terms + self.images * self.cols, LANES)
-        self.edge = 3 * self.width + 2 * 2 * self.width * (1 + 1)
+        self.at_gbias = self.at_scale + LANES
+        self.at_terms = self.at_gbias + self.slot
+        self.at_cond = self.at_terms + round_up(self.images * self.cols, LANES)
+        self.pay_four = round_up(self.at_cond + self.images * self.cond, LANES)
+        self.part = self.out // 2 // n_x
+        self.n_x = n_x
+        self.grad_one = grad_rows(self.part, self.n_one)
+        self.grad_two = grad_rows(self.part, self.n_two)
+        self.grad_skip = grad_rows(self.part, self.n_skip)
+
+
+HALF = LANES // 2
+
+
+def from_row(near, far, row):
+    row_pos = lax.axis_index("rows")
+    at = (row_pos // 2) ^ (row // 2)
+    same = lax.rem(row_pos, 2) == row % 2
+    return jnp.where(same, near[at].astype(F32), far[at].astype(F32))
+
+
+def packed_rows(rows):
+    return rows + round_up(-(-rows // 2), 8)
+
+
+def pack(values):
+    rows = values.shape[0]
+    h = round_up(-(-rows // 2), 8)
+    right = values[:, LANES:]
+    return jnp.concatenate(
+        [values[:, :LANES], jnp.concatenate([right[:h], right[rows - h :]], axis=1)], axis=0
+    )
+
+
+def unpack(values, rows):
+    h = round_up(-(-rows // 2), 8)
+    right = values[rows : rows + h]
+    low = jnp.concatenate([right[:, :HALF], right[2 * h - rows :, HALF:]], axis=0)
+    return jnp.concatenate([values[:rows], low], axis=1)
+
+
+def grad_rows(part, width):
+    tail = width % LANES
+    rows = part * (width // LANES)
+    if tail:
+        rows += part // 2 if tail <= HALF and part % 16 == 0 else part
+    return rows
+
+
+def pack_grad(ref, at, lead, values):
+    part, width = values.shape
+    full = width // LANES
+    for k in range(full):
+        ref[lead, at + k * part : at + (k + 1) * part, :] = values[:, k * LANES : (k + 1) * LANES]
+    at += full * part
+    tail = width - full * LANES
+    if tail and tail <= HALF and part % 16 == 0:
+        h = part // 2
+        ref[lead, at : at + h, :tail] = values[:h, full * LANES :]
+        ref[lead, at : at + h, HALF : HALF + tail] = values[h:, full * LANES :]
+    elif tail:
+        ref[lead, at : at + part, :tail] = values[:, full * LANES :]
+
+
+def unpack_grad(values, at, part, width):
+    full = width // LANES
+    pieces = [values[at + k * part : at + (k + 1) * part] for k in range(full)]
+    at += full * part
+    tail = width - full * LANES
+    if tail and tail <= HALF and part % 16 == 0:
+        h = part // 2
+        both = values[at : at + h]
+        pieces.append(
+            jnp.concatenate([both[:, :tail], both[:, HALF : HALF + tail]], axis=0)
+        )
+    elif tail:
+        pieces.append(values[at : at + part, :tail])
+    return pieces[0] if len(pieces) == 1 else jnp.concatenate(pieces, axis=1)
 
 
 def position():
@@ -118,35 +201,74 @@
     return lax.dot_general(a, b, (dims, ((), ())), preferred_element_type=F32, precision=precision)
 
 
-def prep_kernel(sizes, counts, image, cot, cond, vec, vec_t, one_t, two_t, skip, cond_t, bias,
-                pay, half_one, half_two, near, far, left_one, left_two, left_skip, line):
+def prep_kernel(sizes, counts, image, cond, vec, one_t, two_t, skip, cond_t, bias,
+                pay, half_one, half_two, near, far, left_one, left_two,
+                left_skip, line):
     s = sizes
     row_pos, _, core = position()
     even = lax.rem(row_pos, 2) == 0
     last, w = s.rows - 1, s.width
 
-    def edges(ref, low_row, high_row):
+    line[...] = jnp.zeros_like(line)
+    vec_t = jnp.transpose(jnp.concatenate([vec[...], jnp.zeros((5, s.out), F32)], axis=0))
+
+    def power(k, low):
+        column = jnp.sum(low * vec[k : k + 1, :], axis=1, keepdims=True)
+        row = jnp.sum(low * column, axis=0, keepdims=True)
+        at = s.at_power + k * s.out
+        line[0:1, at : at + s.out] = row
+        at = s.at_norm + k
+        line[0:1, at : at + 1] = jnp.sum(column * column, axis=0, keepdims=True)
+        return column
+
+    low_t = one_t[...].astype(BF16).astype(F32)
+    left_one[...] = jnp.sum(low_t * vec_t[:, 0:1], axis=0, keepdims=True)
+    low = jnp.transpose(low_t)
+    power(0, low)
+    n, h = s.n_one, s.h_one
+    packed_one = pack(jnp.where(core == 0, low[:h], low[n - h :]))
+    low_t = two_t[...].astype(BF16).astype(F32)
+    left_two[...] = jnp.sum(low_t * vec_t[:, 1:2], axis=0, keepdims=True)
+    low = jnp.transpose(low_t)
+    power(1, low)
+    n, h = s.n_two, s.h_two
+    half_a = jnp.where(core == 0, low[:h], low[n - h :])
+    low = skip[...].astype(BF16).astype(F32)
+    left_skip[...] = power(2, low)
+    n, h = s.n_skip, s.h_skip
+    half_b = jnp.where(core == 0, low[:h], low[n - h :])
+    packed = pack(jnp.concatenate([half_a, half_b], axis=0))
+    if s.pack_two > packed.shape[0]:
+        packed = jnp.concatenate(
+            [packed, jnp.zeros((s.pack_two - packed.shape[0], LANES), F32)], axis=0
+        )
+    packed = packed.astype(BF16)
+    half_two[...] = packed
+    line[0:1, s.at_bias : s.at_bias + s.n_bias] = bias[...].astype(BF16).astype(F32)
+    proj = dot(cond[...], cond_t[...].astype(BF16), ((1,), (1,)))
+    for b in range(s.images):
+        at = s.at_proj + b * s.cols
+        line[0:1, at : at + s.cols] = proj[b : b + 1]
+    if s.pack_one > packed_one.shape[0]:
+        packed_one = jnp.concatenate(
+            [packed_one, jnp.zeros((s.pack_one - packed_one.shape[0], LANES), F32)], axis=0
+        )
+    half_one[...] = packed_one.astype(BF16)
+
+    def edges(ref, row):
         for t in range(3):
-            ref[:, t * w : (t + 1) * w, :] = image[:, low_row, :, t * LANES : (t + 1) * LANES]
-        at = 3 * w
-        for k in range(2):
-            ref[:, at : at + 2 * w, :] = cot[:, high_row + k, :, :LANES]
-            at += 2 * w
-        for k in range(2):
-            ref[:, at : at + 2 * w, : s.out - LANES] = cot[:, high_row + k, :, LANES:]
-            at += 2 * w
+            ref[:, t * w : (t + 1) * w, :] = image[:, row, :, t * LANES : (t + 1) * LANES]
 
     @pl.when(even)
     def _():
-        edges(near, last, 2 * s.rows - 2)
-        edges(far, 0, 0)
+        edges(near, last)
+        edges(far, 0)
 
     @pl.when(jnp.logical_not(even))
     def _():
-        edges(near, 0, 0)
-        edges(far, last, 2 * s.rows - 2)
-
-    line[...] = jnp.zeros_like(line)
+        edges(near, 0)
+        edges(far, last)
+
     sums = jnp.zeros((8, s.chan), F32)
     squares = jnp.zeros((8, s.chan), F32)
     for b in range(s.images):
@@ -160,51 +282,30 @@
         squares += part_sq * live_of(counts, b)
     line[0:1, : s.chan] = jnp.sum(sums, axis=0, keepdims=True)
     line[0:1, s.chan : 2 * s.chan] = jnp.sum(squares, axis=0, keepdims=True)
-
-    def power(k, low, left_row):
-        column = jnp.sum(low * vec[k : k + 1, :], axis=1, keepdims=True)
-        row = jnp.sum(low * column, axis=0, keepdims=True)
-        at = s.at_power + k * s.slot
-        line[0:1, at : at + s.out] = row
-        line[0:1, s.at_norm + k : s.at_norm + k + 1] = jnp.sum(column * column, axis=0, keepdims=True)
-        return column
-
-    low_t = one_t[...].astype(BF16).astype(F32)
-    left_one[...] = jnp.sum(low_t * vec_t[:, 0:1], axis=0, keepdims=True)
-    low = jnp.transpose(low_t)
-    power(0, low, left_one)
-    n, h = s.n_one, s.h_one
-    half = jnp.where(core == 0, low[:h], low[n - h :]).astype(BF16)
-    for r in range(s.rows_n):
-        half_one[r] = half
-    low_t = two_t[...].astype(BF16).astype(F32)
-    left_two[...] = jnp.sum(low_t * vec_t[:, 1:2], axis=0, keepdims=True)
-    low = jnp.transpose(low_t)
-    power(1, low, left_two)
-    n, h = s.n_two, s.h_two
-    half_a = jnp.where(core == 0, low[:h], low[n - h :])
-    low = skip[...].astype(BF16).astype(F32)
-    left_skip[...] = power(2, low, None)
-    n, h = s.n_skip, s.h_skip
-    half_b = jnp.where(core == 0, low[:h], low[n - h :])
-    half = jnp.concatenate([half_a, half_b], axis=0).astype(BF16)
-    for r in range(s.rows_n):
-        half_two[r] = half
-
-    line[0:1, s.at_bias : s.at_bias + s.n_bias] = bias[...].astype(BF16).astype(F32)
-    proj = dot(cond[...], cond_t[...].astype(BF16), ((1,), (1,)))
-    for b in range(s.images):
-        at = s.at_proj + b * s.cols
-        line[0:1, at : at + s.cols] = proj[b : b + 1]
     whole = line[...]
     for d in range(s.devices):
         pay[d] = whole
 
 
-def act_kernel(sizes, counts, got, image, near, far, slots, proj, stats, spec):
+def stack_kernel(sizes, two, *refs):
+    s = sizes
+    *blocks, near, two_out = refs
+    for m, block in enumerate(blocks):
+        near[m] = block[...]
+    two_out[...] = two[...]
+
+
+def act_kernel(sizes, counts, got, image, near, far, cot, slots, proj, stats, spec,
+               near_cot, far_cot, first_rows, last_rows, sems):
     s = sizes
     row_pos, _, _ = position()
     even = lax.rem(row_pos, 2) == 0
+    copies = [
+        pltpu.make_async_copy(cot.at[:, pl.ds(0, 2)], first_rows, sems.at[0]),
+        pltpu.make_async_copy(cot.at[:, pl.ds(2 * s.rows - 2, 2)], last_rows, sems.at[1]),
+    ]
+    for copy in copies:
+        copy.start()
     group = group_position()
     sums = jnp.sum(got[:, :, : 2 * s.chan], axis=0)
     count = live_total(counts, s) * (s.width * s.width)
@@ -214,25 +315,24 @@
     stats[1:2, :] = rstd
 
     spec[...] = jnp.zeros_like(spec)
-    total = got[group, :, s.at_power : s.at_proj]
-    for r in range(1, s.rows_n):
-        total = total + got[r * s.groups + group, :, s.at_power : s.at_proj]
+    total = None
+    for r in range(s.rows_n):
+        piece = got[r * s.groups + group, :, s.at_power :]
+        part = piece[:, : s.at_proj - s.at_power]
+        total = part if total is None else total + part
+        at = s.at_bias - s.at_power
+        spec[6:7, r * s.n_bias : (r + 1) * s.n_bias] = piece[:, at : at + s.n_bias]
+        for b in range(s.images):
+            at = s.at_proj - s.at_power + b * s.cols
+            proj[b : b + 1, r * s.cols : (r + 1) * s.cols] = piece[:, at : at + s.cols]
     for k in range(3):
-        at = 3 * s.slot + k
+        at = s.at_norm - s.at_power + k
         inv_norm = lax.rsqrt(total[:, at : at + 1])
-        row = total[:, k * s.slot : k * s.slot + s.out] * inv_norm
+        row = total[:, k * s.out : (k + 1) * s.out] * inv_norm
         inv_sigma = lax.rsqrt(jnp.sum(row * row, axis=1, keepdims=True))
         spec[k : k + 1, : s.out] = row * inv_sigma
         spec[3 + k : 4 + k, :] = jnp.broadcast_to(inv_sigma, (1, s.slot))
         spec[8 + k : 9 + k, :] = jnp.broadcast_to(inv_norm, (1, s.slot))
-    for r in range(s.rows_n):
-        piece = got[r * s.groups + group, :, s.at_bias : s.at_bias + s.n_bias]
-        spec[6:7, r * s.n_bias : (r + 1) * s.n_bias] = piece
-        for b in range(s.images):
-            at = s.at_proj + b * s.cols
-            proj[b : b + 1, r * s.cols : (r + 1) * s.cols] = got[
-                r * s.groups + group, :, at : at + s.cols
-            ]
 
     w = s.width
 
@@ -262,13 +362,34 @@
             one(b, i + 1, image[b, i].astype(F32), None)
         one(b, s.rows + 1, jnp.where(even, a, c), inside(s.rows, s, 1))
 
-
-def conv_one_kernel(sizes, counts, slots, mine, other, cond, hidden, weight, pay, line, wide):
+    for copy in copies:
+        copy.wait()
+
+    def cot_edges(ref, rows):
+        for b in range(s.images):
+            for k in range(2):
+                ref[b, 2 * w * k : 2 * w * (k + 1), :] = rows[b, k, :, :LANES]
+            right = [rows[b, k, :, LANES:].astype(F32) for k in range(2)]
+            ref[b, 4 * w :, :] = jnp.concatenate(right, axis=1).astype(BF16)
+
+    @pl.when(even)
+    def _():
+        cot_edges(near_cot, last_rows)
+        cot_edges(far_cot, first_rows)
+
+    @pl.when(jnp.logical_not(even))
+    def _():
+        cot_edges(near_cot, first_rows)
+        cot_edges(far_cot, last_rows)
+
+
+def conv_one_kernel(sizes, counts, slots, mine_near, mine_far, other_near, other_far, hidden, weight, pay, line, wide):
     s = sizes
     _, _, core = position()
     first = core == 0
     for r in range(s.rows_n):
-        a, b = mine[r].astype(F32), other[r].astype(F32)
+        a = unpack(from_row(mine_near, mine_far, r), s.h_one)
+        b = unpack(from_row(other_near, other_far, r), s.h_one)
         at = r * s.n_one
         wide[at : at + s.h_one, :] = jnp.where(first, a, b)
         at += s.n_one - s.h_one
@@ -306,16 +427,13 @@
             squares += part_sq * live_of(counts, i)
     line[...] = jnp.zeros_like(line)
     line[0:1, : s.out] = jnp.sum(sums, axis=0, keepdims=True)
-    line[0:1, s.slot : s.slot + s.out] = jnp.sum(squares, axis=0, keepdims=True)
-    for i in range(s.images):
-        at = s.at_cond + i * s.cond
-        line[0:1, at : at + s.cond] = cond[i : i + 1, :].astype(F32)
+    line[0:1, s.out : 2 * s.out] = jnp.sum(squares, axis=0, keepdims=True)
     whole = line[...]
     for d in range(s.devices):
         pay[d] = whole
 
 
-def cot_kernel(sizes, counts, cot, near, far, image, mine, other, spec, dact, phases, grad_low,
+def cot_kernel(sizes, counts, cot, near, far, image, mine_near, mine_far, other_near, other_far, spec, dact, phases, grad_low,
                grad_skip, skip_part, two, skip_w, misc, slots, wide, pair, flip):
     s = sizes
     row_pos, _, core = position()
@@ -323,7 +441,8 @@
     first = core == 0
     w = s.width
     for r in range(s.rows_n):
-        a, b = mine[r].astype(F32), other[r].astype(F32)
+        a = unpack(from_row(mine_near, mine_far, r), s.h_two + s.h_skip)
+        b = unpack(from_row(other_near, other_far, r), s.h_two + s.h_skip)
         lo, hi = jnp.where(first, a, b), jnp.where(first, b, a)
         at = r * s.n_two
         wide[at : at + s.h_two, :] = lo[: s.h_two]
@@ -372,11 +491,11 @@
         return both[0] + both[1]
 
     def edge_row(ref, b, k):
-        at = 3 * w + k * 2 * w
+        right = ref[b, 4 * w :, :].astype(F32)
         return jnp.concatenate(
             [
-                ref[b, at : at + 2 * w, :].astype(F32),
-                ref[b, at + 4 * w : at + 6 * w, : s.out - LANES].astype(F32),
+                ref[b, 2 * w * k : 2 * w * (k + 1), :].astype(F32),
+                right[:, k * HALF : k * HALF + s.out - LANES],
             ],
             axis=1,
         )
@@ -415,15 +534,15 @@
         dact[:, :, ph] = total.reshape(s.images, s.ext, w, s.out)
 
 
-def norm_two_kernel(sizes, counts, got, hidden, dact, spec, proj, misc, slots, dnorm, stats,
+def norm_two_kernel(sizes, counts, got, hidden, dact, spec, proj, slots, dnorm, stats,
                     terms, pay, line):
     s = sizes
     w = s.width
     inv = spec[3:4, : s.out]
-    sums = jnp.sum(got[:, :, : 2 * s.slot], axis=0)
+    sums = jnp.sum(got[...], axis=0)
     count = live_total(counts, s) * (4 * w * w)
     mean = sums[:, : s.out] * inv / count
-    square = sums[:, s.slot : s.slot + s.out] * inv * inv / count
+    square = sums[:, s.out : 2 * s.out] * inv * inv / count
     rstd = lax.rsqrt(square - mean * mean + NORM_EPS)
     stats[0:1, : s.out] = mean
     stats[1:2, : s.out] = rstd
@@ -480,17 +599,14 @@
         total += gain * terms[b : b + 1, s.out : 2 * s.out]
     line[...] = jnp.zeros_like(line)
     line[0:1, : s.out] = total
-    line[0:1, s.slot : s.slot + s.out] = cross
-    line[0:1, 2 * s.slot : 2 * s.slot + s.out] = misc[0:1, : s.out]
+    line[0:1, s.out : 2 * s.out] = cross
     whole = line[...]
     for d in range(s.devices):
         pay[d] = whole
 
 
-def conv_two_kernel(sizes, slots, two, phases, grad_low, grad_skip, skip_part, image, spec,
-                    out, mine, other, scale, pair, grads):
+def conv_two_kernel(sizes, slots, two, phases, skip_part, spec, out, scale, pair):
     s = sizes
-    _, _, core = position()
     w = s.width
     depth = 3 * s.slot
     own = 2 * s.rows
@@ -519,10 +635,13 @@
             out[b, e, :, LANES:] = pair[1][:, : s.out - LANES].astype(BF16)
     scale[...] = jnp.broadcast_to(jnp.sum(dots, axis=1, keepdims=True), scale.shape)
 
+
+def grads_two(s, slots, grad_low, grad_skip, image, grads):
+    w = s.width
+    own = 2 * s.rows
+    depth = 3 * s.slot
     count = s.images * own * w
-    flips = [
-        jnp.transpose(grad_low[:, :, ph].reshape(count, s.out)) for ph in range(2)
-    ]
+    flips = [jnp.transpose(grad_low[:, :, ph].reshape(count, s.out)) for ph in range(2)]
     for dy in range(3):
         total = None
         for ph in range(2):
@@ -535,18 +654,10 @@
     count = s.images * s.rows * w
     flip = jnp.transpose(grad_skip[...].reshape(count, s.out))
     grads[:, 9 * s.out : 9 * s.out + s.chan] = dot(flip, image[...].reshape(count, s.chan))
-    half = s.out // 2
-    for ref, which in ((mine, core), (other, 1 - core)):
-        at = pl.multiple_of(which * half, 8)
-        for r in range(s.rows_n):
-            start = r * s.n_two
-            ref[r, :, : s.n_two] = grads[pl.ds(at, half), start : start + s.n_two]
-            start = 9 * s.out + r * s.n_skip
-            ref[r, :, s.n_two :] = grads[pl.ds(at, half), start : start + s.n_skip]
-
-
-def hidden_grad_kernel(sizes, counts, got, dnorm, hidden, stats, spec, acts, slots, mine, other,
-                       scale, bias_grad, low, grads):
+
+
+def hidden_grad_kernel(sizes, counts, got, dnorm, hidden, stats, spec, acts, slots_two, grad_low,
+                       grad_skip, image, slots, mine, other, scale, low, grads, grads_b):
     s = sizes
     _, _, core = position()
     w = s.width
@@ -555,8 +666,7 @@
     mean, rstd = stats[0:1, : s.out], stats[1:2, : s.out]
     inv = spec[3:4, : s.out]
     total = sums[:, : s.out] / count
-    cross = sums[:, s.slot : s.slot + s.out] / count
-    bias_grad[...] = jnp.broadcast_to(sums[:, 2 * s.slot :], bias_grad.shape)
+    cross = sums[:, s.out : 2 * s.out] / count
     slots[...] = jnp.zeros_like(slots)
     norm_scale = inv * rstd
     offset = mean * rstd
@@ -608,16 +718,25 @@
             part = dot(flip, rhs.reshape(count, depth))
             total = part if total is None else total + part
         grads[:, dy * depth : (dy + 1) * depth] = total
-    half = s.out // 2
+    grads_two(s, slots_two, grad_low, grad_skip, image, grads_b)
     for ref, which in ((mine, core), (other, 1 - core)):
-        at = pl.multiple_of(which * half, 8)
-        for r in range(s.rows_n):
-            start = r * s.n_one
-            ref[r] = grads[pl.ds(at, half), start : start + s.n_one]
+        for x in range(s.n_x):
+            at = pl.multiple_of((which * s.n_x + x) * s.part, 8)
+            here = pl.ds(at, s.part)
+            for r in range(s.rows_n):
+                lead = r * s.n_x + x
+                start = r * s.n_one
+                pack_grad(ref, 0, lead, grads[here, start : start + s.n_one])
+                start = r * s.n_two
+                pack_grad(ref, s.grad_one, lead, grads_b[here, start : start + s.n_two])
+                start = 9 * s.out + r * s.n_skip
+                pack_grad(
+                    ref, s.grad_one + s.grad_two, lead, grads_b[here, start : start + s.n_skip]
+                )
 
 
 def input_grad_kernel(sizes, slots, weight, image, stats, proj, terms_two, scale_one, scale_two,
-                      misc, dnorm, pay, back, terms, line):
+                      misc, cond, dnorm, pay, back, terms, line):
     s = sizes
     w = s.width
     depth = 3 * s.slot
@@ -666,6 +785,11 @@
     line[0:1, at : at + 1] = jnp.sum(scale_one[0:1, : s.out], axis=1, keepdims=True)
     line[0:1, at + 1 : at + 2] = scale_two[0:1, 0:1]
     line[0:1, at + 2 : at + 3] = jnp.sum(misc[1:2, : s.out], axis=1, keepdims=True)
+    at = s.at_gbias
+    line[0:1, at : at + s.out] = misc[0:1, : s.out]
+    for b in range(s.images):
+        at = s.at_cond + b * s.cond
+        line[0:1, at : at + s.cond] = cond[b : b + 1, :].astype(F32)
     for r in range(s.rows_n):
         for b in range(s.images):
             at = s.at_terms + b * s.cols
@@ -691,14 +815,14 @@
         ref[...] = value
 
 
-def finish_kernel(sizes, counts, got, cond_got, bias_got, image, dnorm, grad_skip, skip_w, stats, proj,
+def finish_kernel(sizes, counts, got, image, dnorm, grad_skip, skip_w, stats, proj,
                   cw, cm, cv, bw, bm, bv,
                   image_grad, cw_new, cm_new, cv_new, bw_new, bm_new, bv_new, scales, terms, conds):
     s = sizes
     w = s.width
     row_pos, _, _ = position()
     sums = jnp.sum(got[:, :, : s.at_terms], axis=0)
-    scales[...] = jnp.broadcast_to(sums[:, s.at_scale :], scales.shape)
+    scales[...] = jnp.broadcast_to(sums[:, s.at_scale : s.at_gbias], scales.shape)
     count = live_total(counts, s) * (w * w)
     total = sums[:, : s.chan] / count
     cross = sums[:, s.chan : 2 * s.chan] / count
@@ -712,38 +836,56 @@
             normed = (image[b, i].astype(F32) - mean) * rstd
             image_grad[b, i] = keep * (dnorm[b, i] - total - normed * cross) + grad[b, i]
     for g in range(s.groups):
-        part = got[g, :, s.at_terms :]
+        part = got[g, :, s.at_terms : s.at_cond]
         for r in range(1, s.rows_n):
-            part = part + got[r * s.groups + g, :, s.at_terms :]
+            part = part + got[r * s.groups + g, :, s.at_terms : s.at_cond]
         for b in range(s.images):
             k = g * s.images + b
             terms[k : k + 1, :] = part[:, b * s.cols : (b + 1) * s.cols]
             at = s.at_cond + b * s.cond
-            conds[k : k + 1, :] = cond_got[g, :, at : at + s.cond]
+            conds[k : k + 1, :] = got[g, :, at : at + s.cond]
     grad = dot(terms[...], conds[...], ((0,), (0,)), precise)
     store_adamw((cw_new, cm_new, cv_new), (cw, cm, cv), grad, LEARN_RATES[3])
-    grad = bias_got[0:1, : s.n_bias]
+    grad = sums[:, s.at_gbias : s.at_gbias + s.n_bias]
     for r in range(1, s.rows_n):
-        grad = jnp.where(row_pos == r, bias_got[0:1, r * s.n_bias : (r + 1) * s.n_bias], grad)
+        at = s.at_gbias + r * s.n_bias
+        grad = jnp.where(row_pos == r, sums[:, at : at + s.n_bias], grad)
     store_adamw((bw_new, bm_new, bv_new), (bw, bm, bv), grad, LEARN_RATES[4])
 
 
-def weights_kernel(sizes, one_grad, two_grad, scales, spec, left_one, left_two, left_skip,
+def weights_kernel(sizes, own, beside, beyond, across, scales, spec, left_one, left_two, left_skip,
                    ow, om, ov, tw, tm, tv, sw, sm, sv,
-                   ow_new, om_new, ov_new, tw_new, tm_new, tv_new, sw_new, sm_new, sv_new):
+                   ow_new, om_new, ov_new, tw_new, tm_new, tv_new, sw_new, sm_new, sv_new, one_grad, two_grad, skip_grad):
     s = sizes
+    _, x_pos, core = position()
     columns = jnp.transpose(spec[...])
 
     def factor(k):
         inv = spec[3 + k : 4 + k, 0:1]
         return scales[0:1, k : k + 1] * inv * inv * spec[8 + k : 9 + k, 0:1]
 
+    def place(parts, which):
+        for x, part in enumerate(parts):
+            at = pl.multiple_of((which * s.n_x + x) * s.part, 8)
+            here = pl.ds(at, s.part)
+            one_grad[here, :] = unpack_grad(part, 0, s.part, s.n_one)
+            two_grad[here, :] = unpack_grad(part, s.grad_one, s.part, s.n_two)
+            skip_grad[here, :] = unpack_grad(part, s.grad_one + s.grad_two, s.part, s.n_skip)
+
+    def ordered(mine, other):
+        if s.n_x != 2:
+            return [mine[x] for x in range(s.n_x)]
+        a, b = mine[0], other[0]
+        return [jnp.where(x_pos == 0, a, b), jnp.where(x_pos == 0, b, a)]
+
+    place(ordered(own, beside), core)
+    place(ordered(beyond, across), 1 - core)
+
     grad = one_grad[...] - columns[: s.out, 0:1] * (left_one[...] * factor(0))
     store_adamw((ow_new, om_new, ov_new), (ow, om, ov), grad, LEARN_RATES[0])
-    both = two_grad[...]
-    grad = both[:, : s.n_two] - columns[: s.out, 1:2] * (left_two[...] * factor(1))
+    grad = two_grad[...] - columns[: s.out, 1:2] * (left_two[...] * factor(1))
     store_adamw((tw_new, tm_new, tv_new), (tw, tm, tv), grad, LEARN_RATES[1])
-    grad = jnp.transpose(both[:, s.n_two :])
+    grad = jnp.transpose(skip_grad[...])
     grad = grad - (left_skip[...] * factor(2)) * spec[2:3, : s.out]
     store_adamw((sw_new, sm_new, sv_new), (sw, sm, sv), grad, LEARN_RATES[2])
 
@@ -764,13 +906,137 @@
     return lax.ppermute(near, "rows", pairs), lax.ppermute(far, "rows", odd)
 
 
-def scatter_sum(mine, other):
-    rows_n, half, width = mine.shape
-    n_x = lax.axis_size("x")
-    held = mine + core_swap(other)
-    got = lax.all_to_all(held.reshape(rows_n * n_x, half // n_x, width), ("rows", "x"), 0, 0, tiled=True)
-    total = jnp.sum(got.reshape(rows_n * n_x, half // n_x, width), axis=0)
-    return lax.all_gather(total, ("core", "x"), axis=0, tiled=True)
+def row_swap(values, step):
+    devices = lax.axis_size("rows")
+    return lax.ppermute(values, "rows", [(i, i ^ step) for i in range(devices)])
+
+
+def x_swap(values):
+    return lax.ppermute(values, "x", [(0, 1), (1, 0)])
+
+
+def gather_upper(block):
+    return [block] + [row_swap(block, 2 * m) for m in range(1, lax.axis_size("rows") // 2)]
+
+
+def first_sum_kernel(mine, got, send_a, keep_a, send_b, keep_b):
+    _, x, _ = position()
+    low = lax.rem(lax.axis_index("rows"), 2)
+    half = send_a.shape[0]
+    for i in range(half):
+        for k in range(2):
+            send_a[i, k] = mine[i, k, 1 - x] + got[i, k, 1 - x]
+            keep_a[i, k] = mine[i, k, x] + got[i, k, x]
+            send_b[i, k] = mine[half + i, 1 - low, k] + got[half + i, 1 - low, k]
+            keep_b[i, k] = mine[half + i, low, k] + got[half + i, low, k]
+
+
+def second_sum_kernel(keep_a, got_a, keep_b, got_b, send_a, held_a, send_b, held_b):
+    _, x, _ = position()
+    low = lax.rem(lax.axis_index("rows"), 2)
+    for i in range(keep_a.shape[0]):
+        send_a[i] = keep_a[i, 1 - low] + got_a[i, 1 - low]
+        held_a[i] = keep_a[i, low] + got_a[i, low]
+        send_b[i] = keep_b[i, 1 - x] + got_b[i, 1 - x]
+        held_b[i] = keep_b[i, x] + got_b[i, x]
+
+
+def third_sum_kernel(held_a, got_a, held_b, got_b, *outs):
+    high = lax.axis_index("rows") // 2
+    half = held_a.shape[0]
+    for m, out in enumerate(outs):
+        at = high ^ m
+
+        @pl.when(at < half)
+        def _():
+            out[0] = held_a[jnp.minimum(at, half - 1)] + got_a[jnp.minimum(at, half - 1)]
+
+        @pl.when(at >= half)
+        def _():
+            at_b = jnp.maximum(at - half, 0)
+            out[0] = held_b[at_b] + got_b[at_b]
+
+
+def sum_kernel(*refs):
+    *parts, out = refs
+    total = parts[0][...]
+    for part in parts[1:]:
+        total = total + part[...]
+    out[...] = total
+
+
+class StagedSum:
+    small = 8 * 2**20
+
+    def __init__(self, mine, other):
+        self.high = lax.axis_size("rows") // 2
+        self.tail = mine.shape[1:]
+        mine = mine.reshape(self.high, 2, 2, *self.tail)
+        got = core_swap(other).reshape(self.high, 2, 2, *self.tail)
+        send_a, keep_a, send_b, keep_b = run(
+            first_sum_kernel,
+            [shape((self.high // 2, 2, *self.tail))] * 4,
+            [mine, got],
+            scalars=0,
+            limit=self.small,
+        )
+        self.held = [keep_a, x_swap(send_a), keep_b, row_swap(send_b, 1)]
+
+    def second(self, after):
+        send_a, held_a, send_b, held_b = run(
+            second_sum_kernel,
+            [shape((self.high // 2, *self.tail))] * 4,
+            self.held,
+            scalars=0,
+            limit=self.small,
+            after=after,
+        )
+        self.held = [held_a, row_swap(send_a, 1), held_b, x_swap(send_b)]
+
+    def third(self, after):
+        parts = run(
+            third_sum_kernel,
+            [shape((1, *self.tail))] * self.high,
+            self.held,
+            scalars=0,
+            limit=self.small,
+            after=after,
+        )
+        self.held = [parts[0]] + [row_swap(parts[m], 2 * m) for m in range(1, self.high)]
+
+    def last(self, after):
+        (total,) = run(
+            sum_kernel,
+            [shape((1, *self.tail))],
+            self.held,
+            scalars=0,
+            limit=self.small,
+            after=after,
+        )
+        return total
+
+
+class PlainSum:
+    def __init__(self, mine, other):
+        self.held = lax.all_to_all(mine + core_swap(other), ("rows", "x"), 0, 0, tiled=True)
+
+    def second(self, after):
+        pass
+
+    def third(self, after):
+        pass
+
+    def last(self, after):
+        return jnp.sum(self.held, axis=0, keepdims=True)
+
+
+def spread(total):
+    if lax.axis_size("x") == 2:
+        beside = x_swap(total)
+        return total, beside, core_swap(total), core_swap(beside)
+    total = lax.all_gather(total, "x", axis=0, tiled=True)
+    beyond = core_swap(total)
+    return total, total, beyond, beyond
 
 
 def body(
@@ -796,10 +1062,11 @@
     bias_second,
 ):
     rows_n = lax.axis_size("rows")
-    groups_n = lax.axis_size("x") * lax.axis_size("core")
+    n_x = lax.axis_size("x")
+    groups_n = 2 * n_x
     masters = [conv1_weight, conv2_weight, skip_weight, cond_weight, out_bias]
     s = Sizes(
-        image_in.shape, out_cotangent.shape, condition.shape, [m.shape for m in masters], rows_n, groups_n
+        image_in.shape, out_cotangent.shape, condition.shape, [m.shape for m in masters], rows_n, n_x
     )
     bind = functools.partial
     scratch = pltpu.VMEM
@@ -810,10 +1077,10 @@
         bind(prep_kernel, s),
         [
             shape((s.devices, 1, s.pay_one)),
-            shape((rows_n, s.h_one, s.out), BF16),
-            shape((rows_n, s.h_two + s.h_skip, s.out), BF16),
-            shape((n, s.edge, LANES), BF16),
-            shape((n, s.edge, LANES), BF16),
+            shape((s.pack_one, LANES), BF16),
+            shape((s.pack_two, LANES), BF16),
+            shape((n, 3 * w, LANES), BF16),
+            shape((n, 3 * w, LANES), BF16),
             shape((1, s.n_one)),
             shape((1, s.n_two)),
             shape((s.n_skip, 1)),
@@ -821,10 +1088,8 @@
         [
             group_counts,
             image_in,
-            out_cotangent,
             condition,
             power_vectors,
-            power_vectors.T,
             conv1_weight.T,
             conv2_weight.T,
             skip_weight,
@@ -833,23 +1098,39 @@
         ],
         [scratch((1, s.pay_one), F32)],
     )
+    blocks = gather_upper(half_one)
+    got_one = share(pay)
     near, far = row_swaps(near, far)
-    mine_one = lax.all_to_all(half_one, "rows", 0, 0, tiled=True)
-    got_one = share(pay)
-    mine_two = lax.all_to_all(half_two, "rows", 0, 0, tiled=True)
-    other_one = core_swap(mine_one)
-    other_two = core_swap(mine_two)
-
-    acts, proj, stats_one, spec = run(
+    acts, proj, stats_one, spec, near_cot, far_cot = run(
         bind(act_kernel, s),
         [
             shape((n, s.rows + 2, w, 4 * s.chan), BF16),
             shape((n, rows_n * s.cols)),
             shape((2, s.chan)),
             shape((16, s.slot)),
+            *[shape((n, 6 * w, LANES), BF16)] * 2,
         ],
         [group_counts, got_one, image_in, near, far],
-    )
+        [
+            *[scratch((n, 2, 2 * w, s.out), BF16)] * 2,
+            pltpu.SemaphoreType.DMA((2,)),
+        ],
+        whole=[out_cotangent],
+    )
+    high = rows_n // 2
+    near_one, half_two = run(
+        bind(stack_kernel, s),
+        [shape((high, s.pack_one, LANES), BF16), shape(half_two.shape, BF16)],
+        [half_two, *blocks],
+        scalars=0,
+        after=[acts],
+    )
+    far_one = row_swap(near_one, 1)
+    far_one, near_two = lax.optimization_barrier((far_one, jnp.stack(gather_upper(half_two))))
+    blocks_one = near_one, far_one, core_swap(near_one), core_swap(far_one)
+
+    far_two = row_swap(near_two, 1)
+    near_cot, far_cot = row_swaps(near_cot, far_cot)
     hidden, weight_one, pay = run(
         bind(conv_one_kernel, s),
         [
@@ -857,10 +1138,12 @@
             shape((9 * s.chan, s.out), BF16),
             shape((s.devices, 1, s.pay_two)),
         ],
-        [group_counts, acts, mine_one, other_one, condition],
+        [group_counts, acts, *blocks_one],
         [scratch((1, s.pay_two), F32), scratch((9 * s.chan, s.out), F32)],
         flops=2 * n * s.ext * 2 * w * 9 * s.chan * s.out,
     )
+    far_two, pay = lax.optimization_barrier((far_two, pay))
+    blocks_two = near_two, far_two, core_swap(near_two), core_swap(far_two)
     got_two = share(pay)
     dact, phases, grad_low, grad_skip, skip_part, weight_two, weight_skip, misc = run(
         bind(cot_kernel, s),
@@ -874,7 +1157,7 @@
             shape((s.chan, s.out), BF16),
             shape((8, s.slot)),
         ],
-        [group_counts, out_cotangent, near, far, image_in, mine_two, other_two, spec],
+        [group_counts, out_cotangent, near_cot, far_cot, image_in, *blocks_two, spec],
         [
             scratch((n, 2 * s.rows + 4, w, 4 * s.slot), BF16),
             scratch((9 * s.out + s.chan, s.out), F32),
@@ -890,44 +1173,53 @@
             shape((n, s.ext, 2, w, s.out)),
             shape((2, s.slot)),
             shape((8, 2 * s.slot)),
-            shape((s.devices, 1, s.pay_three)),
-        ],
-        [group_counts, got_two, hidden, dact, spec, proj, misc],
-        [scratch((1, s.pay_three), F32)],
+            shape((s.devices, 1, s.pay_two)),
+        ],
+        [group_counts, got_two, hidden, dact, spec, proj],
+        [scratch((1, s.pay_two), F32)],
     )
     got_three = share(pay)
-    out_image, mine, other, scale_two = run(
+    slots_one, mine, other, scale_one = run(
+        bind(hidden_grad_kernel, s),
+        [
+            shape((n, 2, s.rows + 1, w, 4 * s.slot), BF16),
+            *[shape((s.rows_n * n_x, s.grad_one + s.grad_two + s.grad_skip, LANES))] * 2,
+            shape((8, s.slot)),
+        ],
+        [
+            group_counts,
+            got_three,
+            dnorm,
+            hidden,
+            stats_two,
+            spec,
+            acts,
+            slots_two,
+            grad_low,
+            grad_skip,
+            image_in,
+        ],
+        [
+            scratch((2, 2, n, s.rows, w, s.out), BF16),
+            scratch((s.out, 9 * s.chan), F32),
+            scratch((s.out, 9 * s.out + s.chan), F32),
+        ],
+        flops=8 * n * s.rows * w * 9 * s.chan * s.out,
+    )
+    sums = (StagedSum if n_x == 2 else PlainSum)(mine, other)
+    out_image, scale_two = run(
         bind(conv_two_kernel, s),
-        [
-            shape(out_cotangent.shape, BF16),
-            shape((rows_n, s.out // 2, s.n_two + s.n_skip)),
-            shape((rows_n, s.out // 2, s.n_two + s.n_skip)),
-            shape((8, LANES)),
-        ],
-        [slots_two, weight_two, phases, grad_low, grad_skip, skip_part, image_in, spec],
-        [scratch((2, 2 * w, LANES), F32), scratch((s.out, 9 * s.out + s.chan), F32)],
+        [shape(out_cotangent.shape, BF16), shape((8, LANES))],
+        [slots_two, weight_two, phases, skip_part, spec],
+        [scratch((2, 2 * w, LANES), F32)],
         scalars=0,
+        after=[scale_one],
         flops=8 * n * s.rows * 2 * w * 9 * s.out * s.out,
     )
-    two_grad = scatter_sum(mine, other)
-    slots_one, mine, other, scale_one, bias_grad = run(
-        bind(hidden_grad_kernel, s),
-        [
-            shape((n, 2, s.rows + 1, w, 4 * s.slot), BF16),
-            shape((rows_n, s.out // 2, s.n_one)),
-            shape((rows_n, s.out // 2, s.n_one)),
-            shape((8, s.slot)),
-            shape((8, s.slot)),
-        ],
-        [group_counts, got_three, dnorm, hidden, stats_two, spec, acts],
-        [scratch((2, 2, n, s.rows, w, s.out), BF16), scratch((s.out, 9 * s.chan), F32)],
-        flops=8 * n * s.rows * w * 9 * s.chan * s.out,
-    )
-    one_grad = scatter_sum(mine, other)
     dnorm_one, pay = run(
         bind(input_grad_kernel, s),
         [shape((n, s.rows, w, s.chan)), shape((s.devices, 1, s.pay_four))],
-        [slots_one, weight_one, image_in, stats_one, proj, terms_two, scale_one, scale_two, misc],
+        [slots_one, weight_one, image_in, stats_one, proj, terms_two, scale_one, scale_two, misc, condition],
         [
             scratch((3, depth, s.chan), BF16),
             scratch((8, rows_n * s.cols), F32),
@@ -936,7 +1228,9 @@
         scalars=0,
         flops=8 * n * s.rows * w * 9 * s.chan * s.out,
     )
+    sums.second([pay])
     got_four = share(pay)
+    sums.third([got_four])
     moments = [cond_weight, cond_first, cond_second]
     biases = [out_bias, bias_first, bias_second]
     image_grad, *rest, scales = run(
@@ -950,8 +1244,6 @@
         [
             group_counts,
             got_four,
-            got_two,
-            bias_grad,
             image_in,
             dnorm_one,
             grad_skip,
@@ -966,6 +1258,7 @@
             scratch((groups_n * n, s.cond), F32),
         ],
     )
+    parts = spread(sums.last([scales]))
     cond_new = [c.T for c in rest[:3]]
     bias_new = [b[0] for b in rest[3:]]
     olds = [
@@ -978,7 +1271,8 @@
     news = run(
         bind(weights_kernel, s),
         [shape(o.shape) for o in olds],
-        [one_grad, two_grad, scales, spec, left_one, left_two, left_skip, *olds],
+        [*parts, scales, spec, left_one, left_two, left_skip, *olds],
+        [scratch((s.out, k), F32) for k in (s.n_one, s.n_two, s.n_skip)],
         scalars=0,
     )
     weights_new = [m.T for m in news[:6]] + list(news[6:])

time: 285 us -> 181 us (0.64); the launches traced: 281 us -> 180 us
  local copies, waits for them, and re-layouts: 60.1 us -> 7.63 us
  waiting for transfers between devices: 76.3 us -> 39.2 us
  blocking collectives: 48.3 us -> 13.3 us
  Pallas kernels: 43.5 us -> 74.3 us
  other arithmetic: 6.77 us -> 0.84 us
    unnamed x175 -> x52, local copies, waits for them, and re-layouts: 50.9 us -> 7.63 us
    all_to_all x3 -> x0, waiting for transfers between devices: 40.1 us -> none  [the longest x2 40.1 us: scatter_sum(): lax.all_to_all(held.reshape(rows_n * n_x, half // n_x, width), ('rows', '...]
    pallas_call x10 -> x15, Pallas kernels: 43.5 us -> 74.3 us  [run(): pl.pallas_call(kernel, out_shape=tuple(outs), in_specs=specs, out_specs=t...]
    all_gather x2 -> x0, blocking collectives: 24.6 us -> none  [scatter_sum(): return lax.all_gather(total, ('core', 'x'), axis=0, tiled=True)]
    ppermute x0 -> x16, starting transfers between devices: none -> 21.9 us  [the longest x13 18.9 us: row_swap(): return lax.ppermute(values, 'rows', [(i, i ^ step) for i in range(devices)])]
    ppermute x0 -> x16, waiting for transfers between devices: none -> 21.2 us  [the longest x13 16.8 us: row_swap(): return lax.ppermute(values, 'rows', [(i, i ^ step) for i in range(devices)])]
    ppermute x2 -> x4, waiting for transfers between devices: 19.1 us -> 2.11 us  [row_swaps(): return (lax.ppermute(near, 'rows', pairs), lax.ppermute(far, 'rows', odd))]
    all_to_all x3 -> x0, starting transfers between devices: 15.8 us -> none  [the longest x2 11.7 us: scatter_sum(): lax.all_to_all(held.reshape(rows_n * n_x, half // n_x, width), ('rows', '...]
  transfers between devices with their start and end apart: 13 -> 30, of which waited for: 6 -> 14; matrix products, arithmetic and copies ran while one was open for 5% -> 0% of each run, Pallas kernels for 13% -> 23%
where the time goes in v2:
time: 181 us; the launch traced here: 180 us
  Pallas kernels  74.3 us (41%)
  starting transfers between devices  43.8 us (24%)
  waiting for transfers between devices  39.2 us (22%)
  blocking collectives  13.3 us (7%)
  local copies, waits for them, and re-layouts  7.63 us (4%)
    pallas_call x15, Pallas kernels, run(): pl.pallas_call(kernel, out_shape=tuple(outs), in_specs=specs, out_specs=t...  74.3 us
    ppermute x13, starting transfers between devices, row_swap(): return lax.ppermute(values, 'rows', [(i, i ^ step) for i in range(devices)])  18.9 us
    ppermute x13, waiting for transfers between devices, row_swap(): return lax.ppermute(values, 'rows', [(i, i ^ step) for i in range(devices)])  16.8 us
    all_to_all x3, starting transfers between devices, share(): return lax.all_to_all(chunks, ALL, 0, 0, tiled=True)  16.3 us
    all_to_all x1, blocking collectives, share(): return lax.all_to_all(chunks, ALL, 0, 0, tiled=True)  13.3 us
    all_to_all x3, waiting for transfers between devices, share(): return lax.all_to_all(chunks, ALL, 0, 0, tiled=True)  9.12 us
    unnamed x52, local copies, waits for them, and re-layouts  7.63 us
    ppermute x7, waiting for transfers between devices, core_swap(): return lax.ppermute(values, 'core', [(0, 1), (1, 0)])  6.68 us
  transfers between devices with their start and end apart: 30, of which 14 were waited for; matrix products, arithmetic and copies ran while one was open for 0% of the time, Pallas kernels for 23%

profile of v2, /device:TPU:0, one launch (start us, length us, event | category | flops | bytes accessed | tf_op | source)
XLA Modules:
  0.0 180.1 jit_solution(8006543678853369629)
XLA Ops:
  0.7 2.8 %shard_map.323 = (f32[32,1,2048]{2,1,0:T(1,128)}, bf16[336,128]{1,0:T(8,128)(2,1)}, bf16[208,128]{1,0:T(8,128)(2,1)}, bf16[4,96,128]{2,1,0:T(8,128)(2,1)}, bf16[...) custom-call(s32[4]{0:T(128)} %counts.13, bf16[4,4,32,384]{3,2,1,0:T(8,128)(2,1)} %image.11, ...), custom_call_target="tpu_custom_call" | custom-call | bytes 1617392 | tf_op jit(solution)/shard_map/pallas_call | solution.py:43
  3.5 7.3 %all-to-all-start = ((f32[32,1,2048]{2,1,0:T(1,128)}), f32[32,1,2048]{2,1,0:T(1,128)S(1)}, u32[]{:S(2)}, u32[]{:S(2)}) async-start(f32[32,1,2048]{2,1,0:T(1,128)} %get-tuple-element.92), calls=%async_computation | async-start | bytes 524288 | tf_op jit(solution)/shard_map/all_to_all | solution.py:894
  13.3 5.1 %collective-permute-start.2 = (bf16[336,128]{1,0:T(8,128)(2,1)}, bf16[336,128]{1,0:T(8,128)(2,1)S(1)}, u32[]{:S(2)}, u32[]{:S(2)}) collective-permute-start(bf16[336,128]{1,0:T(8,128)(2,1)} %get-tuple-element.91.refs_1_), channel_id=1, source_target_pairs={{0,24},{4,28},{8,16},{12,20},{16,8},{20,12},{24,0},{28,4},{1,25},{... | collective-permute-start | bytes 258056 | tf_op jit(solution)/shard_map/ppermute | solution.py:911
  19.1 2.5 %all-to-all-done.got = f32[32,1,2048]{2,1,0:T(1,128)S(1)} async-done(((f32[32,1,2048]{2,1,0:T(1,128)}), f32[32,1,2048]{2,1,0:T(1,128)S(1)}, u32[]{:S(2)}, u32[]{:S(2)}) %all-to-all-start) | async-done | bytes 262176 | tf_op jit(solution)/shard_map/all_to_all | solution.py:894
  22.3 4.0 %shard_map.324 = (bf16[4,6,32,1536]{3,2,1,0:T(8,128)(2,1)}, f32[4,1152]{1,0:T(4,128)}, f32[2,384]{1,0:T(2,128)}, f32[16,256]{1,0:T(8,128)}, bf16[4,192,128]{2,1,0:T(8,128)(2,1)}, /*index=5*/bf16[4,192,128]{2,1,0:T(8,128)(2,1)}) custom-call(s32[4]{0:T(128)} %counts.13, f32[32,1,2048]{2,1,0:T(1,128)} %copy-done.5, bf16[4,4,32,384]{3,2,1,0:T(8,128)(2,1)} %image.11, ...), custom_call_target="tpu_custom_call" | custom-call | bytes 3642384 | tf_op jit(solution)/shard_map/pallas_call | solution.py:43
  26.4 3.3 %collective-permute-done.1.refs_3_ = bf16[336,128]{1,0:T(8,128)(2,1)S(1)} collective-permute-done((bf16[336,128]{1,0:T(8,128)(2,1)}, bf16[336,128]{1,0:T(8,128)(2,1)S(1)}, u32[]{:S(2)}, u32[]{:S(2)}) %collective-permute-start.1) | collective-permute-done | bytes 86048 | tf_op jit(solution)/shard_map/ppermute | solution.py:911
  32.1 2.9 %collective-permute-start.8 = (bf16[208,128]{1,0:T(8,128)(2,1)}, bf16[208,128]{1,0:T(8,128)(2,1)S(1)}, u32[]{:S(2)}, u32[]{:S(2)}) collective-permute-start(bf16[208,128]{1,0:T(8,128)(2,1)} %get-tuple-element.97), channel_id=1, source_target_pairs={{0,24},{4,28},{8,16},{12,20},{16,8},{20,12},{24,0},{28,4},{1,25},{... | collective-permute-start | bytes 159752 | tf_op jit(solution)/shard_map/ppermute | solution.py:911
  35.0 2.8 %collective-permute-start.7 = (bf16[208,128]{1,0:T(8,128)(2,1)}, bf16[208,128]{1,0:T(8,128)(2,1)S(1)}, u32[]{:S(2)}, u32[]{:S(2)}) collective-permute-start(bf16[208,128]{1,0:T(8,128)(2,1)} %get-tuple-element.97), channel_id=1, source_target_pairs={{0,16},{4,20},{8,24},{12,28},{16,0},{20,4},{24,8},{28,12},{1,17},{... | collective-permute-start | bytes 159752 | tf_op jit(solution)/shard_map/ppermute | solution.py:911
  38.3 2.9 %collective-permute-done.7 = bf16[208,128]{1,0:T(8,128)(2,1)S(1)} collective-permute-done((bf16[208,128]{1,0:T(8,128)(2,1)}, bf16[208,128]{1,0:T(8,128)(2,1)S(1)}, u32[]{:S(2)}, u32[]{:S(2)}) %collective-permute-start.7) | collective-permute-done | bytes 53280 | tf_op jit(solution)/shard_map/ppermute | solution.py:911
  45.5 9.0 %shard_map.326 = (f32[4,10,2,32,192]{4,3,2,1,0:T(8,128)}, bf16[3456,192]{1,0:T(8,128)(2,1)}, f32[32,1,384]{2,1,0:T(1,128)}) custom-call(s32[4]{0:T(128)} %counts.13, bf16[4,6,32,1536]{3,2,1,0:T(8,128)(2,1)} %get-tuple-element.95.refs_5_.slots.acts, bf16[4,336,128]{2,1,0:T(8,128)(2,1)} %get-tuple-element.96.mine_near, bf16[4,336,128]{2,1,0:T(8,128)(2,1)} %copy-done.16, ...), custom_call_target="tpu_custom_call" | custom-call | flops 3397386240 | bytes 7077904 | tf_op jit(solution)/shard_map/pallas_call | solution.py:43
  56.9 6.3 %all-to-all-start.1 = ((f32[32,1,384]{2,1,0:T(1,128)}), f32[32,1,384]{2,1,0:T(1,128)S(1)}, u32[]{:S(2)}, u32[]{:S(2)}) async-start(f32[32,1,384]{2,1,0:T(1,128)} %get-tuple-element.101), calls=%async_computation.1 | async-start | bytes 98304 | tf_op jit(solution)/shard_map/all_to_all | solution.py:894
  66.2 9.2 %shard_map.327 = (f32[4,10,2,32,192]{4,3,2,1,0:T(8,128)}, bf16[4,8,2,32,192]{4,3,2,1,0:T(8,128)(2,1)}, bf16[4,8,2,32,192]{4,3,2,1,0:T(8,128)(2,1)}, bf16[4,4,32,...) custom-call(s32[4]{0:T(128)} %counts.13, ...), custom_call_target="tpu_custom_call" | custom-call | flops 1698693120 | bytes 7610384 | tf_op jit(solution)/shard_map/pallas_call | solution.py:43
  76.0 7.4 %shard_map.328 = (bf16[4,10,32,1024]{3,2,1,0:T(8,128)(2,1)}, f32[4,10,2,32,192]{4,3,2,1,0:T(8,128)}, f32[2,256]{1,0:T(2,128)}, f32[8,512]{1,0:T(8,128)}, f32[32,1,384]{2,1,0:T(1,128)}) custom-call(s32[4]{0:T(128)} %counts.13, f32[32,1,384]{2,1,0:T(1,128)} %copy-done.7, f32[4,10,2,32,192]{4,3,2,1,0:T(8,128)} %get-tuple-element.102.hidden, ...), custom_call_target="tpu_custom_call" | custom-call | bytes 8671248 | tf_op jit(solution)/shard_map/pallas_call | solution.py:43
  83.4 13.3 %all_to_all.20.got = f32[32,1,384]{2,1,0:T(1,128)} all-to-all(f32[32,1,384]{2,1,0:T(1,128)} %get-tuple-element.113), channel_id=1, replica_groups=mesh['rows'=8,'x'=2,'core'=2] {'rows','x','core'}, dimensions={0} | all-to-all | bytes 98304 | tf_op jit(solution)/shard_map/all_to_all | solution.py:894
  96.7 15.5 %shard_map.329 = (bf16[4,2,5,32,1024]{4,3,2,1,0:T(8,128)(2,1)}, f32[16,288,128]{2,1,0:T(8,128)}, f32[16,288,128]{2,1,0:T(8,128)}, f32[8,256]{1,0:T(8,128)}) custom-call(s32[4]{0:T(128)} %counts.13, f32[32,1,384]{2,1,0:T(1,128)} %all_to_all.20.got, f32[4,10,2,32,192]{4,3,2,1,0:T(8,128)} %get-tuple-element.114.dnorm, ...), custom_call_target="tpu_custom_call" | custom-call | flops 2717908992 | bytes 17704976 | tf_op jit(solution)/shard_map/pallas_call | solution.py:43
  112.3 4.6 %collective-permute-done.16 = f32[16,288,128]{2,1,0:T(8,128)S(1)} collective-permute-done((f32[16,288,128]{2,1,0:T(8,128)}, f32[16,288,128]{2,1,0:T(8,128)S(1)}, u32[]{:S(2)}, u32[]{:S(2)}) %collective-permute-start.16) | collective-permute-done | bytes 2359328 | tf_op jit(solution)/shard_map/ppermute | solution.py:898
  120.9 6.7 %shard_map.330 = (bf16[4,8,64,192]{3,2,1,0:T(8,128)(2,1)}, f32[8,128]{1,0:T(8,128)}) custom-call(bf16[4,10,32,1024]{3,2,1,0:T(8,128)(2,1)} %get-tuple-element.109.slots_two.refs_0_, bf16[3,768,192]{2,1,0:T(8,128)(2,1)} %get-tuple-element.110.refs_1_, bf16[4,8,2,32,192]{4,3,2,1,0:T(8,128)(2,1)} %get-tuple-element.111.refs_2_, ...), custom_call_target="tpu_custom_call" | custom-call | flops 2717908992 | bytes 5492736 | tf_op jit(solution)/shard_map/pallas_call | solution.py:43
  127.6 9.1 %shard_map.331 = (f32[4,4,32,384]{3,2,1,0:T(8,128)}, f32[32,1,2432]{2,1,0:T(1,128)}) custom-call(bf16[4,2,5,32,1024]{4,3,2,1,0:T(8,128)(2,1)} %get-tuple-element.120.slots, bf16[3456,192]{1,0:T(8,128)(2,1)} %get-tuple-element.121.weight, bf16[4,4,32,384]{3,2,1,0:T(8,128)(2,1)} %image.11, f32[2,384]{1,0:T(2,128)} %get-tuple-element.122.stats, ...), custom_call_target="tpu_custom_call" | custom-call | flops 2717908992 | bytes 5499040 | tf_op jit(solution)/shard_map/pallas_call | solution.py:43
  136.7 2.7 %all-to-all-start.3 = ((f32[32,1,2432]{2,1,0:T(1,128)}), f32[32,1,2432]{2,1,0:T(1,128)S(1)}, u32[]{:S(2)}, u32[]{:S(2)}) async-start(f32[32,1,2432]{2,1,0:T(1,128)} %get-tuple-element.126.refs_4_), calls=%async_computation.3 | async-start | bytes 622592 | tf_op jit(solution)/shard_map/all_to_all | solution.py:894
  144.5 6.6 %all-to-all-done.3.got.refs_4_ = f32[32,1,2432]{2,1,0:T(1,128)S(1)} async-done(((f32[32,1,2432]{2,1,0:T(1,128)}), f32[32,1,2432]{2,1,0:T(1,128)S(1)}, u32[]{:S(2)}, u32[]{:S(2)}) %all-to-all-start.3) | async-done | bytes 311328 | tf_op jit(solution)/shard_map/all_to_all | solution.py:894
  157.7 3.4 %shard_map.332 = (f32[4,4,32,384]{3,2,1,0:T(8,128)}, f32[144,148]{1,0:T(8,128)}, f32[144,148]{1,0:T(8,128)}, f32[144,148]{1,0:T(8,128)}, f32[1,24]{1,0:T(1,128)}...) custom-call(s32[4]{0:T(128)} %counts.13, f32[32,1,2432]{2,1,0:T(1,128)} %copy-done, ...), custom_call_target="tpu_custom_call" | custom-call | bytes 3159120 | tf_op jit(solution)/shard_map/pallas_call | solution.py:43
  161.0 7.5 %collective-permute-done.22.refs_2_ = f32[1,288,128]{2,1,0:T(8,128)S(1)} collective-permute-done((f32[1,288,128]{2,1,0:T(8,128)S(1)}, f32[1,288,128]{2,1,0:T(8,128)S(1)}, u32[]{:S(2)}, u32[]{:S(2)}) %collective-permute-start.22) | collective-permute-done | bytes 147488 | tf_op jit(solution)/shard_map/ppermute | solution.py:911
  170.3 4.1 %collective-permute-done.24.beside = f32[1,288,128]{2,1,0:T(8,128)S(1)} collective-permute-done((f32[1,288,128]{2,1,0:T(8,128)S(1)}, f32[1,288,128]{2,1,0:T(8,128)S(1)}, u32[]{:S(2)}, u32[]{:S(2)}) %collective-permute-start.24) | collective-permute-done | bytes 147488 | tf_op jit(solution)/shard_map/ppermute | solution.py:915
  176.5 3.4 %shard_map.337 = (f32[192,432]{1,0:T(8,128)}, f32[192,432]{1,0:T(8,128)}, f32[192,432]{1,0:T(8,128)}, f32[192,216]{1,0:T(8,128)}, f32[192,216]{1,0:T(8,128)}, /*...) custom-call(f32[1,288,128]{2,1,0:T(8,128)} %copy-done.3, ...), custom_call_target="tpu_custom_call" | custom-call | bytes 3820256 | tf_op jit(solution)/shard_map/pallas_call | solution.py:43
  (105 shorter events, 36.4 us)
Async XLA Ops:
  3.5 18.1 %all-to-all-start = ((f32[32,1,2048]{2,1,0:T(1,128)}), f32[32,1,2048]{2,1,0:T(1,128)S(1)}, u32[]{:S(2)}, u32[]{:S(2)}) async-start(f32[32,1,2048]{2,1,0:T(1,128)} %get-tuple-element.92), calls=%async_computation | async-start | bytes 524288 | tf_op jit(solution)/shard_map/all_to_all | solution.py:894
  10.8 8.3 %collective-permute-start.3 = (bf16[4,96,128]{2,1,0:T(8,128)(2,1)}, bf16[4,96,128]{2,1,0:T(8,128)(2,1)S(1)}, u32[]{:S(2)}, u32[]{:S(2)}) collective-permute-start(bf16[4,96,128]{2,1,0:T(8,128)(2,1)} %get-tuple-element.93), channel_id=1, source_target_pairs={{0,4},{4,0},{8,12},{12,8},{16,20},{20,16},{24,28},{28,24},{1,5},{5... | collective-permute-start | bytes 294920 | tf_op jit(solution)/shard_map/ppermute | solution.py:906
  12.6 6.4 %collective-permute-start.4 = (bf16[4,96,128]{2,1,0:T(8,128)(2,1)}, bf16[4,96,128]{2,1,0:T(8,128)(2,1)S(1)}, u32[]{:S(2)}, u32[]{:S(2)}) collective-permute-start(bf16[4,96,128]{2,1,0:T(8,128)(2,1)} %get-tuple-element.94), channel_id=1, source_target_pairs={{4,8},{12,16},{20,24},{8,4},{16,12},{24,20},{5,9},{13,17},{21,25},... | collective-permute-start | bytes 294920 | tf_op jit(solution)/shard_map/ppermute | solution.py:906
  13.3 13.0 %collective-permute-start.2 = (bf16[336,128]{1,0:T(8,128)(2,1)}, bf16[336,128]{1,0:T(8,128)(2,1)S(1)}, u32[]{:S(2)}, u32[]{:S(2)}) collective-permute-start(bf16[336,128]{1,0:T(8,128)(2,1)} %get-tuple-element.91.refs_1_), channel_id=1, source_target_pairs={{0,24},{4,28},{8,16},{12,20},{16,8},{20,12},{24,0},{28,4},{1,25},{... | collective-permute-start | bytes 258056 | tf_op jit(solution)/shard_map/ppermute | solution.py:911
  18.4 11.2 %collective-permute-start.1 = (bf16[336,128]{1,0:T(8,128)(2,1)}, bf16[336,128]{1,0:T(8,128)(2,1)S(1)}, u32[]{:S(2)}, u32[]{:S(2)}) collective-permute-start(bf16[336,128]{1,0:T(8,128)(2,1)} %get-tuple-element.91.refs_1_), channel_id=1, source_target_pairs={{0,16},{4,20},{8,24},{12,28},{16,0},{20,4},{24,8},{28,12},{1,17},{... | collective-permute-start | bytes 258056 | tf_op jit(solution)/shard_map/ppermute | solution.py:911
  18.4 11.2 %collective-permute-start = (bf16[336,128]{1,0:T(8,128)(2,1)}, bf16[336,128]{1,0:T(8,128)(2,1)S(1)}, u32[]{:S(2)}, u32[]{:S(2)}) collective-permute-start(bf16[336,128]{1,0:T(8,128)(2,1)} %get-tuple-element.91.refs_1_), channel_id=1, source_target_pairs={{0,8},{4,12},{8,0},{12,4},{16,24},{20,28},{24,16},{28,20},{1,9},{5... | collective-permute-start | bytes 258056 | tf_op jit(solution)/shard_map/ppermute | solution.py:911
  32.1 10.9 %collective-permute-start.5 = (bf16[4,336,128]{2,1,0:T(8,128)(2,1)}, bf16[4,336,128]{2,1,0:T(8,128)(2,1)S(1)}, u32[]{:S(2)}, u32[]{:S(2)}) collective-permute-start(bf16[4,336,128]{2,1,0:T(8,128)(2,1)} %get-tuple-element.96.mine_near), channel_id=1, source_target_pairs={{0,4},{4,0},{8,12},{12,8},{16,20},{20,16},{24,28},{28,24},{1,5},{5... | collective-permute-start | bytes 1032200 | tf_op jit(solution)/shard_map/ppermute | solution.py:911
  32.1 6.2 %collective-permute-start.8 = (bf16[208,128]{1,0:T(8,128)(2,1)}, bf16[208,128]{1,0:T(8,128)(2,1)S(1)}, u32[]{:S(2)}, u32[]{:S(2)}) collective-permute-start(bf16[208,128]{1,0:T(8,128)(2,1)} %get-tuple-element.97), channel_id=1, source_target_pairs={{0,24},{4,28},{8,16},{12,20},{16,8},{20,12},{24,0},{28,4},{1,25},{... | collective-permute-start | bytes 159752 | tf_op jit(solution)/shard_map/ppermute | solution.py:911
  35.0 6.2 %collective-permute-start.7 = (bf16[208,128]{1,0:T(8,128)(2,1)}, bf16[208,128]{1,0:T(8,128)(2,1)S(1)}, u32[]{:S(2)}, u32[]{:S(2)}) collective-permute-start(bf16[208,128]{1,0:T(8,128)(2,1)} %get-tuple-element.97), channel_id=1, source_target_pairs={{0,16},{4,20},{8,24},{12,28},{16,0},{20,4},{24,8},{28,12},{1,17},{... | collective-permute-start | bytes 159752 | tf_op jit(solution)/shard_map/ppermute | solution.py:911
  37.8 6.3 %collective-permute-start.10 = (bf16[4,336,128]{2,1,0:T(8,128)(2,1)}, bf16[4,336,128]{2,1,0:T(8,128)(2,1)S(1)}, u32[]{:S(2)}, u32[]{:S(2)}) collective-permute-start(bf16[4,336,128]{2,1,0:T(8,128)(2,1)} %get-tuple-element.96.mine_near), channel_id=1, source_target_pairs={{0,1},{1,0},{2,3},{3,2},{4,5},{5,4},{6,7},{7,6},{8,9},{9,8},{10,11... | collective-permute-start | bytes 1032200 | tf_op jit(solution)/shard_map/ppermute | solution.py:898
  43.1 22.2 %collective-permute-start.14 = (bf16[4,208,128]{2,1,0:T(8,128)(2,1)S(1)}, bf16[4,208,128]{2,1,0:T(8,128)(2,1)S(1)}, u32[]{:S(2)}, u32[]{:S(2)}) collective-permute-start(bf16[4,208,128]{2,1,0:T(8,128)(2,1)S(1)} %pad_maximum_fusion.mine_near), channel_id=1, source_target_pairs={{0,1},{1,0},{2,3},{3,2},{4,5},{5,4},{6,7},{7,6},{8,9},{9,8},{10,11... | collective-permute-start | bytes 638984 | tf_op jit(solution)/shard_map/ppermute | solution.py:898
  43.6 10.9 %collective-permute-start.9 = (bf16[4,208,128]{2,1,0:T(8,128)(2,1)S(1)}, bf16[4,208,128]{2,1,0:T(8,128)(2,1)S(1)}, u32[]{:S(2)}, u32[]{:S(2)}) collective-permute-start(bf16[4,208,128]{2,1,0:T(8,128)(2,1)S(1)} %pad_maximum_fusion.mine_near), channel_id=1, source_target_pairs={{0,4},{4,0},{8,12},{12,8},{16,20},{20,16},{24,28},{28,24},{1,5},{5... | collective-permute-start | bytes 638984 | tf_op jit(solution)/shard_map/ppermute | solution.py:911
  54.5 10.8 %collective-permute-start.15 = (bf16[4,208,128]{2,1,0:T(8,128)(2,1)S(1)}, bf16[4,208,128]{2,1,0:T(8,128)(2,1)S(1)}, u32[]{:S(2)}, u32[]{:S(2)}) collective-permute-start(bf16[4,208,128]{2,1,0:T(8,128)(2,1)S(1)} %collective-permute-done.9.mine_far), channel_id=1, source_target_pairs={{0,1},{1,0},{2,3},{3,2},{4,5},{5,4},{6,7},{7,6},{8,9},{9,8},{10,11... | collective-permute-start | bytes 638984 | tf_op jit(solution)/shard_map/ppermute | solution.py:898
  54.7 10.6 %collective-permute-start.12 = (bf16[4,192,128]{2,1,0:T(8,128)(2,1)S(1)}, bf16[4,192,128]{2,1,0:T(8,128)(2,1)S(1)}, u32[]{:S(2)}, u32[]{:S(2)}) collective-permute-start(bf16[4,192,128]{2,1,0:T(8,128)(2,1)S(1)} %copy-done.23), channel_id=1, source_target_pairs={{0,4},{4,0},{8,12},{12,8},{16,20},{20,16},{24,28},{28,24},{1,5},{5... | collective-permute-start | bytes 589832 | tf_op jit(solution)/shard_map/ppermute | solution.py:906
  56.3 9.1 %collective-permute-start.13 = (bf16[4,192,128]{2,1,0:T(8,128)(2,1)S(1)}, bf16[4,192,128]{2,1,0:T(8,128)(2,1)S(1)}, u32[]{:S(2)}, u32[]{:S(2)}) collective-permute-start(bf16[4,192,128]{2,1,0:T(8,128)(2,1)S(1)} %copy-done.22), channel_id=1, source_target_pairs={{4,8},{12,16},{20,24},{8,4},{16,12},{24,20},{5,9},{13,17},{21,25},... | collective-permute-start | bytes 589832 | tf_op jit(solution)/shard_map/ppermute | solution.py:906
  56.9 18.5 %all-to-all-start.1 = ((f32[32,1,384]{2,1,0:T(1,128)}), f32[32,1,384]{2,1,0:T(1,128)S(1)}, u32[]{:S(2)}, u32[]{:S(2)}) async-start(f32[32,1,384]{2,1,0:T(1,128)} %get-tuple-element.101), calls=%async_computation.1 | async-start | bytes 98304 | tf_op jit(solution)/shard_map/all_to_all | solution.py:894
  119.7 19.7 %collective-permute-start.17 = (f32[2,2,288,128]{3,2,1,0:T(8,128)}, f32[2,2,288,128]{3,2,1,0:T(8,128)S(1)}, u32[]{:S(2)}, u32[]{:S(2)}) collective-permute-start(f32[2,2,288,128]{3,2,1,0:T(8,128)} %get-tuple-element.133), channel_id=1, source_target_pairs={{0,2},{2,0},{1,3},{3,1},{4,6},{6,4},{5,7},{7,5},{8,10},{10,8},{9,1... | collective-permute-start | bytes 1769480 | tf_op jit(solution)/shard_map/ppermute | solution.py:915
  120.1 19.3 %collective-permute-start.18 = (f32[2,2,288,128]{3,2,1,0:T(8,128)S(1)}, f32[2,2,288,128]{3,2,1,0:T(8,128)S(1)}, u32[]{:S(2)}, u32[]{:S(2)}) collective-permute-start(f32[2,2,288,128]{3,2,1,0:T(8,128)S(1)} %get-tuple-element.135), channel_id=1, source_target_pairs={{0,4},{4,0},{8,12},{12,8},{16,20},{20,16},{24,28},{28,24},{1,5},{5... | collective-permute-start | bytes 1769480 | tf_op jit(solution)/shard_map/ppermute | solution.py:911
  136.7 14.4 %all-to-all-start.3 = ((f32[32,1,2432]{2,1,0:T(1,128)}), f32[32,1,2432]{2,1,0:T(1,128)S(1)}, u32[]{:S(2)}, u32[]{:S(2)}) async-start(f32[32,1,2432]{2,1,0:T(1,128)} %get-tuple-element.126.refs_4_), calls=%async_computation.3 | async-start | bytes 622592 | tf_op jit(solution)/shard_map/all_to_all | solution.py:894
  141.3 11.6 %collective-permute-start.19 = (f32[2,288,128]{2,1,0:T(8,128)}, f32[2,288,128]{2,1,0:T(8,128)S(1)}, u32[]{:S(2)}, u32[]{:S(2)}) collective-permute-start(f32[2,288,128]{2,1,0:T(8,128)} %get-tuple-element.137), channel_id=1, source_target_pairs={{0,4},{4,0},{8,12},{12,8},{16,20},{20,16},{24,28},{28,24},{1,5},{5... | collective-permute-start | bytes 884744 | tf_op jit(solution)/shard_map/ppermute | solution.py:911
  143.0 10.0 %collective-permute-start.20 = (f32[2,288,128]{2,1,0:T(8,128)S(1)}, f32[2,288,128]{2,1,0:T(8,128)S(1)}, u32[]{:S(2)}, u32[]{:S(2)}) collective-permute-start(f32[2,288,128]{2,1,0:T(8,128)S(1)} %get-tuple-element.139), channel_id=1, source_target_pairs={{0,2},{2,0},{1,3},{3,1},{4,6},{6,4},{5,7},{7,5},{8,10},{10,8},{9,1... | collective-permute-start | bytes 884744 | tf_op jit(solution)/shard_map/ppermute | solution.py:915
  153.2 7.8 %collective-permute-start.21 = (f32[1,288,128]{2,1,0:T(8,128)S(1)}, f32[1,288,128]{2,1,0:T(8,128)S(1)}, u32[]{:S(2)}, u32[]{:S(2)}) collective-permute-start(f32[1,288,128]{2,1,0:T(8,128)S(1)} %get-tuple-element.141), channel_id=1, source_target_pairs={{0,8},{4,12},{8,0},{12,4},{16,24},{20,28},{24,16},{28,20},{1,9},{5... | collective-permute-start | bytes 442376 | tf_op jit(solution)/shard_map/ppermute | solution.py:911
  154.8 13.7 %collective-permute-start.22 = (f32[1,288,128]{2,1,0:T(8,128)S(1)}, f32[1,288,128]{2,1,0:T(8,128)S(1)}, u32[]{:S(2)}, u32[]{:S(2)}) collective-permute-start(f32[1,288,128]{2,1,0:T(8,128)S(1)} %get-tuple-element.142), channel_id=1, source_target_pairs={{0,16},{4,20},{8,24},{12,28},{16,0},{20,4},{24,8},{28,12},{1,17},{... | collective-permute-start | bytes 442376 | tf_op jit(solution)/shard_map/ppermute | solution.py:911
  156.7 11.8 %collective-permute-start.23 = (f32[1,288,128]{2,1,0:T(8,128)S(1)}, f32[1,288,128]{2,1,0:T(8,128)S(1)}, u32[]{:S(2)}, u32[]{:S(2)}) collective-permute-start(f32[1,288,128]{2,1,0:T(8,128)S(1)} %get-tuple-element.143), channel_id=1, source_target_pairs={{0,24},{4,28},{8,16},{12,20},{16,8},{20,12},{24,0},{28,4},{1,25},{... | collective-permute-start | bytes 442376 | tf_op jit(solution)/shard_map/ppermute | solution.py:911
  (32 other events, 106.0 us)

commit v3 on v2

--- a/solution.py
+++ b/solution.py
@@ -20,31 +20,28 @@
 ALL = ("rows", "x", "core")
 F32, BF16 = jnp.float32, jnp.bfloat16
 LANES = 128
-VMEM_LIMIT = 60 * 2**20
+VMEM_LIMIT = 56 * 2**20
 
 
 def shape(dims, kind=F32):
     return jax.ShapeDtypeStruct(tuple(dims), kind)
 
 
-def skipping(kernel, start, count):
-    return lambda *refs: kernel(*refs[:start], *refs[start + count :])
-
-
-def run(kernel, outs, args, scratch=(), scalars=1, flops=0, limit=VMEM_LIMIT, after=(), whole=()):
+def run(kernel, outs, args, scratch=(), scalars=1, flops=0, limit=VMEM_LIMIT, whole=(), results=()):
     spec = pl.BlockSpec(memory_space=pltpu.VMEM)
     specs = [pl.BlockSpec(memory_space=pltpu.SMEM)] * scalars + [spec] * (len(args) - scalars)
-    specs += [pl.BlockSpec(memory_space=pl.ANY)] * (len(whole) + len(after))
+    specs += [pl.BlockSpec(memory_space=pl.ANY)] * len(whole)
     moved = sum(a.size * a.dtype.itemsize for a in args)
-    args = [*args, *whole, *after]
-    if after:
-        kernel = skipping(kernel, len(args) - len(after), len(after))
+    args = [*args, *whole]
+    scratch = [pltpu.VMEM(a.shape, a.dtype) for a in (*whole, *results)] + list(scratch)
+    out_specs = [spec] * len(outs) + [pl.BlockSpec(memory_space=pl.ANY)] * len(results)
+    outs = [*outs, *results]
     moved += sum(np.prod(o.shape) * np.dtype(o.dtype).itemsize for o in outs)
     return pl.pallas_call(
         kernel,
         out_shape=tuple(outs),
         in_specs=specs,
-        out_specs=tuple(spec for _ in outs),
+        out_specs=tuple(out_specs),
         scratch_shapes=scratch,
         cost_estimate=pl.CostEstimate(
             flops=int(flops), bytes_accessed=int(moved), transcendentals=0
@@ -81,15 +78,14 @@
         self.pay_one = round_up(self.at_proj + self.images * self.cols, LANES)
         self.pay_two = round_up(2 * self.out, LANES)
         self.at_scale = 2 * self.chan
-        self.at_gbias = self.at_scale + LANES
-        self.at_terms = self.at_gbias + self.slot
-        self.at_cond = self.at_terms + round_up(self.images * self.cols, LANES)
-        self.pay_four = round_up(self.at_cond + self.images * self.cond, LANES)
+        self.at_gbias = self.at_scale + HALF
+        self.at_terms = self.at_gbias + self.out
+        self.pay_four = round_up(self.at_terms + self.images * self.cols, LANES)
         self.part = self.out // 2 // n_x
         self.n_x = n_x
-        self.grad_one = grad_rows(self.part, self.n_one)
-        self.grad_two = grad_rows(self.part, self.n_two)
-        self.grad_skip = grad_rows(self.part, self.n_skip)
+        self.wide = self.n_one + self.n_two + self.n_skip
+        self.pitch = round_up(self.wide, LANES)
+        self.grad_rows = grad_rows(self.part, self.wide)
 
 
 HALF = LANES // 2
@@ -130,19 +126,22 @@
     return rows
 
 
-def pack_grad(ref, at, lead, values):
-    part, width = values.shape
+def pack_grad(ref, lead, grads, here, begin, width):
+    part = here.size
     full = width // LANES
     for k in range(full):
-        ref[lead, at + k * part : at + (k + 1) * part, :] = values[:, k * LANES : (k + 1) * LANES]
-    at += full * part
+        at = begin + k * LANES
+        ref[lead, k * part : (k + 1) * part, :] = grads[here, at : at + LANES]
     tail = width - full * LANES
-    if tail and tail <= HALF and part % 16 == 0:
+    if not tail:
+        return
+    at = full * part
+    rest = grads[here, begin + full * LANES : begin + (full + 1) * LANES]
+    if tail <= HALF and part % 16 == 0:
         h = part // 2
-        ref[lead, at : at + h, :tail] = values[:h, full * LANES :]
-        ref[lead, at : at + h, HALF : HALF + tail] = values[h:, full * LANES :]
-    elif tail:
-        ref[lead, at : at + part, :tail] = values[:, full * LANES :]
+        ref[lead, at : at + h, :] = jnp.concatenate([rest[:h, :HALF], rest[h:, :HALF]], axis=1)
+    else:
+        ref[lead, at : at + part, :] = rest
 
 
 def unpack_grad(values, at, part, width):
@@ -183,6 +182,12 @@
 def inside(row, sizes, scale):
     at = lax.axis_index("rows") * (scale * sizes.rows) + row
     return jnp.where((at >= 0) & (at < scale * sizes.rows * sizes.rows_n), 1.0, 0.0).astype(F32)
+
+
+def start(source, target, sem):
+    copy = pltpu.make_async_copy(source, target, sem)
+    copy.start()
+    return copy
 
 
 def sigmoid(values):
@@ -287,25 +292,15 @@
         pay[d] = whole
 
 
-def stack_kernel(sizes, two, *refs):
-    s = sizes
-    *blocks, near, two_out = refs
-    for m, block in enumerate(blocks):
-        near[m] = block[...]
-    two_out[...] = two[...]
-
-
 def act_kernel(sizes, counts, got, image, near, far, cot, slots, proj, stats, spec,
-               near_cot, far_cot, first_rows, last_rows, sems):
+               near_cot, far_cot, rows, sems):
     s = sizes
     row_pos, _, _ = position()
     even = lax.rem(row_pos, 2) == 0
     copies = [
-        pltpu.make_async_copy(cot.at[:, pl.ds(0, 2)], first_rows, sems.at[0]),
-        pltpu.make_async_copy(cot.at[:, pl.ds(2 * s.rows - 2, 2)], last_rows, sems.at[1]),
+        start(cot.at[:, pl.ds(at, 2)], rows.at[:, pl.ds(at, 2)], sems.at[k])
+        for k, at in enumerate(sorted({0, 2 * s.rows - 2}))
     ]
-    for copy in copies:
-        copy.start()
     group = group_position()
     sums = jnp.sum(got[:, :, : 2 * s.chan], axis=0)
     count = live_total(counts, s) * (s.width * s.width)
@@ -365,22 +360,22 @@
     for copy in copies:
         copy.wait()
 
-    def cot_edges(ref, rows):
+    def cot_edges(ref, row):
         for b in range(s.images):
             for k in range(2):
-                ref[b, 2 * w * k : 2 * w * (k + 1), :] = rows[b, k, :, :LANES]
-            right = [rows[b, k, :, LANES:].astype(F32) for k in range(2)]
+                ref[b, 2 * w * k : 2 * w * (k + 1), :] = rows[b, row + k, :, :LANES]
+            right = [rows[b, row + k, :, LANES:].astype(F32) for k in range(2)]
             ref[b, 4 * w :, :] = jnp.concatenate(right, axis=1).astype(BF16)
 
     @pl.when(even)
     def _():
-        cot_edges(near_cot, last_rows)
-        cot_edges(far_cot, first_rows)
+        cot_edges(near_cot, 2 * s.rows - 2)
+        cot_edges(far_cot, 0)
 
     @pl.when(jnp.logical_not(even))
     def _():
-        cot_edges(near_cot, first_rows)
-        cot_edges(far_cot, last_rows)
+        cot_edges(near_cot, 0)
+        cot_edges(far_cot, 2 * s.rows - 2)
 
 
 def conv_one_kernel(sizes, counts, slots, mine_near, mine_far, other_near, other_far, hidden, weight, pay, line, wide):
@@ -404,8 +399,8 @@
         a, b = divmod(phase, 2)
         total = None
         for dy in range(3):
-            start = (a + dy - 1) // 2 + 1 - a
-            lhs = slots[:, start : start + rows, :, b * s.chan : b * s.chan + depth]
+            at = (a + dy - 1) // 2 + 1 - a
+            lhs = slots[:, at : at + rows, :, b * s.chan : b * s.chan + depth]
             part = dot(
                 lhs.reshape(s.images * rows * s.width, depth),
                 weight[dy * depth : (dy + 1) * depth, :],
@@ -534,10 +529,13 @@
         dact[:, :, ph] = total.reshape(s.images, s.ext, w, s.out)
 
 
-def norm_two_kernel(sizes, counts, got, hidden, dact, spec, proj, slots, dnorm, stats,
-                    terms, pay, line):
+def norm_two_kernel(sizes, counts, got, spec, proj, hidden_from, dact_from, stats, terms, pay,
+                    slots_to, dnorm_to, hidden, dact, slots, dnorm, line, sems):
     s = sizes
     w = s.width
+    for b in range(s.images):
+        start(hidden_from.at[b], hidden.at[b], sems.at[0, b])
+        start(dact_from.at[b], dact.at[b], sems.at[1, b])
     inv = spec[3:4, : s.out]
     sums = jnp.sum(got[...], axis=0)
     count = live_total(counts, s) * (4 * w * w)
@@ -578,8 +576,16 @@
 
     terms[...] = jnp.zeros_like(terms)
 
+    def sent(b):
+        return [
+            pltpu.make_async_copy(slots.at[b], slots_to.at[b], sems.at[2, b]),
+            pltpu.make_async_copy(dnorm.at[b], dnorm_to.at[b], sems.at[3, b]),
+        ]
+
     @pl.loop(0, s.images)
     def _(b):
+        pltpu.make_async_copy(hidden_from.at[b], hidden.at[b], sems.at[0, b]).wait()
+        pltpu.make_async_copy(dact_from.at[b], dact.at[b], sems.at[1, b]).wait()
         one(b, 0, inside(-1, s, 2))
         dsum = jnp.zeros((8, s.out), F32)
         dgain = jnp.zeros((8, s.out), F32)
@@ -590,6 +596,8 @@
         one(b, s.ext - 1, inside(2 * s.rows, s, 2))
         terms[pl.ds(b, 1), : s.out] = jnp.sum(dgain, axis=0, keepdims=True)
         terms[pl.ds(b, 1), s.out : 2 * s.out] = jnp.sum(dsum, axis=0, keepdims=True)
+        for copy in sent(b):
+            copy.start()
 
     total = jnp.zeros((1, s.out), F32)
     cross = jnp.zeros((1, s.out), F32)
@@ -603,6 +611,9 @@
     whole = line[...]
     for d in range(s.devices):
         pay[d] = whole
+    for b in range(s.images):
+        for copy in sent(b):
+            copy.wait()
 
 
 def conv_two_kernel(sizes, slots, two, phases, skip_part, spec, out, scale, pair):
@@ -636,6 +647,14 @@
     scale[...] = jnp.broadcast_to(jnp.sum(dots, axis=1, keepdims=True), scale.shape)
 
 
+def place(s, grads, values, first, shard, offset):
+    end = first + values.shape[1]
+    for r in range(first // shard, (end - 1) // shard + 1):
+        low, high = max(first, r * shard), min(end, (r + 1) * shard)
+        at = r * s.pitch + offset + low - r * shard
+        grads[:, at : at + high - low] = values[:, low - first : high - first]
+
+
 def grads_two(s, slots, grad_low, grad_skip, image, grads):
     w = s.width
     own = 2 * s.rows
@@ -649,18 +668,29 @@
             part = dot(flips[ph], rhs.reshape(count, depth))
             total = part if total is None else total + part
         for dx in range(3):
-            at = (3 * dy + dx) * s.out
-            grads[:, at : at + s.out] = total[:, dx * s.slot : dx * s.slot + s.out]
+            tap = total[:, dx * s.slot : dx * s.slot + s.out]
+            place(s, grads, tap, (3 * dy + dx) * s.out, s.n_two, s.n_one)
     count = s.images * s.rows * w
     flip = jnp.transpose(grad_skip[...].reshape(count, s.out))
-    grads[:, 9 * s.out : 9 * s.out + s.chan] = dot(flip, image[...].reshape(count, s.chan))
-
-
-def hidden_grad_kernel(sizes, counts, got, dnorm, hidden, stats, spec, acts, slots_two, grad_low,
-                       grad_skip, image, slots, mine, other, scale, low, grads, grads_b):
+    place(s, grads, dot(flip, image[...].reshape(count, s.chan)), 0, s.n_skip, s.n_one + s.n_two)
+
+
+def hidden_grad_kernel(sizes, counts, got, stats, spec, grad_skip, image,
+                       dnorm_from, hidden_from, acts_from, slots_two_from, grad_low_from,
+                       scale, other_to, mine_to, slots_to,
+                       dnorm, hidden, acts, slots_two, grad_low, other, mine, slots,
+                       low, grads, sems):
     s = sizes
     _, _, core = position()
     w = s.width
+    for b in range(s.images):
+        start(hidden_from.at[b], hidden.at[b], sems.at[0, b])
+        start(dnorm_from.at[b], dnorm.at[b], sems.at[1, b])
+    fetch_acts = start(acts_from, acts, sems.at[3, 0])
+    fetch_two = [
+        start(slots_two_from, slots_two, sems.at[3, 1]),
+        start(grad_low_from, grad_low, sems.at[3, 2]),
+    ]
     sums = jnp.sum(got[...], axis=0)
     count = live_total(counts, s) * (4 * w * w)
     mean, rstd = stats[0:1, : s.out], stats[1:2, : s.out]
@@ -696,8 +726,13 @@
 
     scale[...] = jnp.zeros_like(scale)
 
+    def sent(b):
+        return pltpu.make_async_copy(slots.at[b], slots_to.at[b], sems.at[2, b])
+
     @pl.loop(0, s.images)
     def _(b):
+        pltpu.make_async_copy(hidden_from.at[b], hidden.at[b], sems.at[0, b]).wait()
+        pltpu.make_async_copy(dnorm_from.at[b], dnorm.at[b], sems.at[1, b]).wait()
         live = live_of(counts, b)
         one(b, 0, live * inside(-1, s, 2), False)
         dots = jnp.zeros((8, s.out), F32)
@@ -705,7 +740,9 @@
             dots += one(b, e, live, True)
         one(b, s.ext - 1, live * inside(2 * s.rows, s, 2), False)
         scale[0:1, : s.out] += jnp.sum(dots, axis=0, keepdims=True)
-
+        sent(b).start()
+
+    fetch_acts.wait()
     count = s.images * s.rows * w
     depth = 3 * s.chan
     for dy in range(3):
@@ -713,30 +750,30 @@
         for phase in range(4):
             a, b = divmod(phase, 2)
             flip = jnp.transpose(low[a, b].reshape(count, s.out))
-            start = 1 + (a + dy - 1) // 2
-            rhs = acts[:, start : start + s.rows, :, b * s.chan : b * s.chan + depth]
+            first = 1 + (a + dy - 1) // 2
+            rhs = acts[:, first : first + s.rows, :, b * s.chan : b * s.chan + depth]
             part = dot(flip, rhs.reshape(count, depth))
             total = part if total is None else total + part
-        grads[:, dy * depth : (dy + 1) * depth] = total
-    grads_two(s, slots_two, grad_low, grad_skip, image, grads_b)
-    for ref, which in ((mine, core), (other, 1 - core)):
+        place(s, grads, total, dy * depth, s.n_one, 0)
+    for copy in fetch_two:
+        copy.wait()
+    grads_two(s, slots_two, grad_low, grad_skip, image, grads)
+    copies = []
+    for ref, to, which in ((other, other_to, 1 - core), (mine, mine_to, core)):
         for x in range(s.n_x):
             at = pl.multiple_of((which * s.n_x + x) * s.part, 8)
             here = pl.ds(at, s.part)
             for r in range(s.rows_n):
-                lead = r * s.n_x + x
-                start = r * s.n_one
-                pack_grad(ref, 0, lead, grads[here, start : start + s.n_one])
-                start = r * s.n_two
-                pack_grad(ref, s.grad_one, lead, grads_b[here, start : start + s.n_two])
-                start = 9 * s.out + r * s.n_skip
-                pack_grad(
-                    ref, s.grad_one + s.grad_two, lead, grads_b[here, start : start + s.n_skip]
-                )
+                pack_grad(ref, r * s.n_x + x, grads, here, r * s.pitch, s.wide)
+        copies.append(start(ref, to, sems.at[4, len(copies)]))
+    for b in range(s.images):
+        copies.append(sent(b))
+    for copy in copies:
+        copy.wait()
 
 
 def input_grad_kernel(sizes, slots, weight, image, stats, proj, terms_two, scale_one, scale_two,
-                      misc, cond, dnorm, pay, back, terms, line):
+                      misc, dnorm, pay, back, terms, line):
     s = sizes
     w = s.width
     depth = 3 * s.slot
@@ -787,9 +824,6 @@
     line[0:1, at + 2 : at + 3] = jnp.sum(misc[1:2, : s.out], axis=1, keepdims=True)
     at = s.at_gbias
     line[0:1, at : at + s.out] = misc[0:1, : s.out]
-    for b in range(s.images):
-        at = s.at_cond + b * s.cond
-        line[0:1, at : at + s.cond] = cond[b : b + 1, :].astype(F32)
     for r in range(s.rows_n):
         for b in range(s.images):
             at = s.at_terms + b * s.cols
@@ -815,14 +849,14 @@
         ref[...] = value
 
 
-def finish_kernel(sizes, counts, got, image, dnorm, grad_skip, skip_w, stats, proj,
+def finish_kernel(sizes, counts, got, cond_all, image, dnorm, grad_skip, skip_w, stats, proj,
                   cw, cm, cv, bw, bm, bv,
                   image_grad, cw_new, cm_new, cv_new, bw_new, bm_new, bv_new, scales, terms, conds):
     s = sizes
     w = s.width
     row_pos, _, _ = position()
     sums = jnp.sum(got[:, :, : s.at_terms], axis=0)
-    scales[...] = jnp.broadcast_to(sums[:, s.at_scale : s.at_gbias], scales.shape)
+    scales[...] = jnp.broadcast_to(sums[:, s.at_scale : s.at_scale + LANES], scales.shape)
     count = live_total(counts, s) * (w * w)
     total = sums[:, : s.chan] / count
     cross = sums[:, s.chan : 2 * s.chan] / count
@@ -836,14 +870,13 @@
             normed = (image[b, i].astype(F32) - mean) * rstd
             image_grad[b, i] = keep * (dnorm[b, i] - total - normed * cross) + grad[b, i]
     for g in range(s.groups):
-        part = got[g, :, s.at_terms : s.at_cond]
+        part = got[g, :, s.at_terms :]
         for r in range(1, s.rows_n):
-            part = part + got[r * s.groups + g, :, s.at_terms : s.at_cond]
+            part = part + got[r * s.groups + g, :, s.at_terms :]
         for b in range(s.images):
             k = g * s.images + b
             terms[k : k + 1, :] = part[:, b * s.cols : (b + 1) * s.cols]
-            at = s.at_cond + b * s.cond
-            conds[k : k + 1, :] = got[g, :, at : at + s.cond]
+            conds[k : k + 1, :] = cond_all[g, b : b + 1, :].astype(F32)
     grad = dot(terms[...], conds[...], ((0,), (0,)), precise)
     store_adamw((cw_new, cm_new, cv_new), (cw, cm, cv), grad, LEARN_RATES[3])
     grad = sums[:, s.at_gbias : s.at_gbias + s.n_bias]
@@ -855,7 +888,7 @@
 
 def weights_kernel(sizes, own, beside, beyond, across, scales, spec, left_one, left_two, left_skip,
                    ow, om, ov, tw, tm, tv, sw, sm, sv,
-                   ow_new, om_new, ov_new, tw_new, tm_new, tv_new, sw_new, sm_new, sv_new, one_grad, two_grad, skip_grad):
+                   ow_new, om_new, ov_new, tw_new, tm_new, tv_new, sw_new, sm_new, sv_new, grads):
     s = sizes
     _, x_pos, core = position()
     columns = jnp.transpose(spec[...])
@@ -868,9 +901,7 @@
         for x, part in enumerate(parts):
             at = pl.multiple_of((which * s.n_x + x) * s.part, 8)
             here = pl.ds(at, s.part)
-            one_grad[here, :] = unpack_grad(part, 0, s.part, s.n_one)
-            two_grad[here, :] = unpack_grad(part, s.grad_one, s.part, s.n_two)
-            skip_grad[here, :] = unpack_grad(part, s.grad_one + s.grad_two, s.part, s.n_skip)
+            grads[here, : s.wide] = unpack_grad(part, 0, s.part, s.wide)
 
     def ordered(mine, other):
         if s.n_x != 2:
@@ -881,11 +912,11 @@
     place(ordered(own, beside), core)
     place(ordered(beyond, across), 1 - core)
 
-    grad = one_grad[...] - columns[: s.out, 0:1] * (left_one[...] * factor(0))
+    grad = grads[:, : s.n_one] - columns[: s.out, 0:1] * (left_one[...] * factor(0))
     store_adamw((ow_new, om_new, ov_new), (ow, om, ov), grad, LEARN_RATES[0])
-    grad = two_grad[...] - columns[: s.out, 1:2] * (left_two[...] * factor(1))
+    grad = grads[:, s.n_one : s.n_one + s.n_two] - columns[: s.out, 1:2] * (left_two[...] * factor(1))
     store_adamw((tw_new, tm_new, tv_new), (tw, tm, tv), grad, LEARN_RATES[1])
-    grad = jnp.transpose(skip_grad[...])
+    grad = jnp.transpose(grads[:, s.n_one + s.n_two : s.wide])
     grad = grad - (left_skip[...] * factor(2)) * spec[2:3, : s.out]
     store_adamw((sw_new, sm_new, sv_new), (sw, sm, sv), grad, LEARN_RATES[2])
 
@@ -917,6 +948,17 @@
 
 def gather_upper(block):
     return [block] + [row_swap(block, 2 * m) for m in range(1, lax.axis_size("rows") // 2)]
+
+
+def gather_groups(values):
+    if lax.axis_size("x") != 2:
+        return lax.all_gather(values, ("x", "core"), axis=0)
+    x, core = lax.axis_index("x"), lax.axis_index("core")
+    pair = jnp.stack([values, core_swap(values)])
+    pair = jnp.where(core == 0, pair, pair[::-1])
+    both = jnp.stack([pair, x_swap(pair)])
+    both = jnp.where(x == 0, both, both[::-1])
+    return both.reshape(4, *values.shape)
 
 
 def first_sum_kernel(mine, got, send_a, keep_a, send_b, keep_b):
@@ -965,10 +1007,14 @@
     out[...] = total
 
 
+def tied(values, after):
+    return list(lax.optimization_barrier((tuple(values), tuple(after)))[0])
+
+
 class StagedSum:
     small = 8 * 2**20
 
-    def __init__(self, mine, other):
+    def __init__(self, mine, other, after):
         self.high = lax.axis_size("rows") // 2
         self.tail = mine.shape[1:]
         mine = mine.reshape(self.high, 2, 2, *self.tail)
@@ -976,7 +1022,7 @@
         send_a, keep_a, send_b, keep_b = run(
             first_sum_kernel,
             [shape((self.high // 2, 2, *self.tail))] * 4,
-            [mine, got],
+            tied([mine, got], after),
             scalars=0,
             limit=self.small,
         )
@@ -986,10 +1032,9 @@
         send_a, held_a, send_b, held_b = run(
             second_sum_kernel,
             [shape((self.high // 2, *self.tail))] * 4,
-            self.held,
+            tied(self.held, after),
             scalars=0,
             limit=self.small,
-            after=after,
         )
         self.held = [held_a, row_swap(send_a, 1), held_b, x_swap(send_b)]
 
@@ -997,10 +1042,9 @@
         parts = run(
             third_sum_kernel,
             [shape((1, *self.tail))] * self.high,
-            self.held,
+            tied(self.held, after),
             scalars=0,
             limit=self.small,
-            after=after,
         )
         self.held = [parts[0]] + [row_swap(parts[m], 2 * m) for m in range(1, self.high)]
 
@@ -1008,16 +1052,15 @@
         (total,) = run(
             sum_kernel,
             [shape((1, *self.tail))],
-            self.held,
+            tied(self.held, after),
             scalars=0,
             limit=self.small,
-            after=after,
         )
         return total
 
 
 class PlainSum:
-    def __init__(self, mine, other):
+    def __init__(self, mine, other, after):
         self.held = lax.all_to_all(mine + core_swap(other), ("rows", "x"), 0, 0, tiled=True)
 
     def second(self, after):
@@ -1097,10 +1140,12 @@
             out_bias[None],
         ],
         [scratch((1, s.pay_one), F32)],
+        limit=60 * 2**20,
     )
     blocks = gather_upper(half_one)
+    near, far = row_swaps(near, far)
+    (pay,) = tied([pay], [near, far])
     got_one = share(pay)
-    near, far = row_swaps(near, far)
     acts, proj, stats_one, spec, near_cot, far_cot = run(
         bind(act_kernel, s),
         [
@@ -1111,22 +1156,14 @@
             *[shape((n, 6 * w, LANES), BF16)] * 2,
         ],
         [group_counts, got_one, image_in, near, far],
-        [
-            *[scratch((n, 2, 2 * w, s.out), BF16)] * 2,
-            pltpu.SemaphoreType.DMA((2,)),
-        ],
+        [pltpu.SemaphoreType.DMA((2,))],
         whole=[out_cotangent],
     )
-    high = rows_n // 2
-    near_one, half_two = run(
-        bind(stack_kernel, s),
-        [shape((high, s.pack_one, LANES), BF16), shape(half_two.shape, BF16)],
-        [half_two, *blocks],
-        scalars=0,
-        after=[acts],
-    )
+    near_one = jnp.stack(blocks)
+    (half_two,) = tied([half_two], [near_one])
     far_one = row_swap(near_one, 1)
-    far_one, near_two = lax.optimization_barrier((far_one, jnp.stack(gather_upper(half_two))))
+    near_two = jnp.stack(gather_upper(half_two))
+    far_one, near_two, acts = lax.optimization_barrier((far_one, near_two, acts))
     blocks_one = near_one, far_one, core_swap(near_one), core_swap(far_one)
 
     far_two = row_swap(near_two, 1)
@@ -1142,7 +1179,7 @@
         [scratch((1, s.pay_two), F32), scratch((9 * s.chan, s.out), F32)],
         flops=2 * n * s.ext * 2 * w * 9 * s.chan * s.out,
     )
-    far_two, pay = lax.optimization_barrier((far_two, pay))
+    far_two, near_cot, far_cot, pay = lax.optimization_barrier((far_two, near_cot, far_cot, pay))
     blocks_two = near_two, far_two, core_swap(near_two), core_swap(far_two)
     got_two = share(pay)
     dact, phases, grad_low, grad_skip, skip_part, weight_two, weight_skip, misc = run(
@@ -1166,60 +1203,44 @@
         ],
         flops=2 * n * s.ext * 2 * w * 9 * s.out * s.out,
     )
-    slots_two, dnorm, stats_two, terms_two, pay = run(
+    stats_two, terms_two, pay, slots_two, dnorm = run(
         bind(norm_two_kernel, s),
-        [
-            shape((n, s.ext, w, 4 * s.slot), BF16),
-            shape((n, s.ext, 2, w, s.out)),
-            shape((2, s.slot)),
-            shape((8, 2 * s.slot)),
-            shape((s.devices, 1, s.pay_two)),
-        ],
-        [group_counts, got_two, hidden, dact, spec, proj],
-        [scratch((1, s.pay_two), F32)],
+        [shape((2, s.slot)), shape((8, 2 * s.slot)), shape((s.devices, 1, s.pay_two))],
+        [group_counts, got_two, spec, proj],
+        [scratch((1, s.pay_two), F32), pltpu.SemaphoreType.DMA((4, n))],
+        whole=[hidden, dact],
+        results=[shape((n, s.ext, w, 4 * s.slot), BF16), shape((n, s.ext, 2, w, s.out))],
     )
     got_three = share(pay)
-    slots_one, mine, other, scale_one = run(
+    sent = shape((s.rows_n * n_x, s.grad_rows, LANES))
+    scale_one, other, mine, slots_one = run(
         bind(hidden_grad_kernel, s),
-        [
-            shape((n, 2, s.rows + 1, w, 4 * s.slot), BF16),
-            *[shape((s.rows_n * n_x, s.grad_one + s.grad_two + s.grad_skip, LANES))] * 2,
-            shape((8, s.slot)),
-        ],
-        [
-            group_counts,
-            got_three,
-            dnorm,
-            hidden,
-            stats_two,
-            spec,
-            acts,
-            slots_two,
-            grad_low,
-            grad_skip,
-            image_in,
-        ],
+        [shape((8, s.slot))],
+        [group_counts, got_three, stats_two, spec, grad_skip, image_in],
         [
             scratch((2, 2, n, s.rows, w, s.out), BF16),
-            scratch((s.out, 9 * s.chan), F32),
-            scratch((s.out, 9 * s.out + s.chan), F32),
+            scratch((s.out, rows_n * s.pitch), F32),
+            pltpu.SemaphoreType.DMA((5, max(n, 3))),
         ],
         flops=8 * n * s.rows * w * 9 * s.chan * s.out,
+        whole=[dnorm, hidden, acts, slots_two, grad_low],
+        results=[sent, sent, shape((n, 2, s.rows + 1, w, 4 * s.slot), BF16)],
+        limit=48 * 2**20,
     )
-    sums = (StagedSum if n_x == 2 else PlainSum)(mine, other)
     out_image, scale_two = run(
         bind(conv_two_kernel, s),
         [shape(out_cotangent.shape, BF16), shape((8, LANES))],
-        [slots_two, weight_two, phases, skip_part, spec],
+        tied([slots_two, weight_two, phases, skip_part, spec], [scale_one]),
         [scratch((2, 2 * w, LANES), F32)],
         scalars=0,
-        after=[scale_one],
         flops=8 * n * s.rows * 2 * w * 9 * s.out * s.out,
+        limit=48 * 2**20,
     )
+    sums = (StagedSum if n_x == 2 else PlainSum)(mine, other, [scale_two])
     dnorm_one, pay = run(
         bind(input_grad_kernel, s),
         [shape((n, s.rows, w, s.chan)), shape((s.devices, 1, s.pay_four))],
-        [slots_one, weight_one, image_in, stats_one, proj, terms_two, scale_one, scale_two, misc, condition],
+        [slots_one, weight_one, image_in, stats_one, proj, terms_two, scale_one, scale_two, misc],
         [
             scratch((3, depth, s.chan), BF16),
             scratch((8, rows_n * s.cols), F32),
@@ -1229,6 +1250,8 @@
         flops=8 * n * s.rows * w * 9 * s.chan * s.out,
     )
     sums.second([pay])
+    late_condition, pay = lax.optimization_barrier((condition, pay))
+    cond_all = gather_groups(late_condition)
     got_four = share(pay)
     sums.third([got_four])
     moments = [cond_weight, cond_first, cond_second]
@@ -1244,6 +1267,7 @@
         [
             group_counts,
             got_four,
+            cond_all,
             image_in,
             dnorm_one,
             grad_skip,
@@ -1257,6 +1281,7 @@
             scratch((groups_n * n, s.cols), F32),
             scratch((groups_n * n, s.cond), F32),
         ],
+        limit=60 * 2**20,
     )
     parts = spread(sums.last([scales]))
     cond_new = [c.T for c in rest[:3]]
@@ -1272,7 +1297,8 @@
         bind(weights_kernel, s),
         [shape(o.shape) for o in olds],
         [*parts, scales, spec, left_one, left_two, left_skip, *olds],
-        [scratch((s.out, k), F32) for k in (s.n_one, s.n_two, s.n_skip)],
+        [scratch((s.out, s.pitch), F32)],
+        limit=24 * 2**20,
         scalars=0,
     )
     weights_new = [m.T for m in news[:6]] + list(news[6:])

time: 181 us -> 157 us (0.87)
  Pallas kernels: 74.3 us -> 63.1 us
  waiting for transfers between devices: 39.2 us -> 28.4 us
  local copies, waits for them, and re-layouts: 7.63 us -> 4.33 us
    pallas_call x15 -> x14, Pallas kernels: 74.3 us -> 63.1 us  [run(): pl.pallas_call(kernel, out_shape=tuple(outs), in_specs=specs, out_specs=t...]
    ppermute x7 -> x8, waiting for transfers between devices: 6.68 us -> 1.39 us  [core_swap(): return lax.ppermute(values, 'core', [(0, 1), (1, 0)])]
    all_to_all x3, waiting for transfers between devices: 9.12 us -> 4.63 us  [share(): return lax.all_to_all(chunks, ALL, 0, 0, tiled=True)]
    unnamed x52 -> x80, local copies, waits for them, and re-layouts: 7.63 us -> 4.33 us
    ppermute x3 -> x4, waiting for transfers between devices: 4.41 us -> 4.83 us  [x_swap(): return lax.ppermute(values, 'x', [(0, 1), (1, 0)])]
  transfers between devices with their start and end apart: 30 -> 32, of which waited for: 14 -> 9; matrix products, arithmetic and copies ran while one was open for 0% -> 2% of each run, Pallas kernels for 23% -> 25%
where the time goes in v3:
time: 157 us
  Pallas kernels  63.1 us (40%)
  starting transfers between devices  43.9 us (28%)
  waiting for transfers between devices  28.4 us (18%)
  blocking collectives  13.2 us (8%)
  local copies, waits for them, and re-layouts  4.33 us (3%)
  other arithmetic  2.41 us (2%)
    pallas_call x14, Pallas kernels, run(): pl.pallas_call(kernel, out_shape=tuple(outs), in_specs=specs, out_specs=t...  63.1 us
    ppermute x13, starting transfers between devices, row_swap(): return lax.ppermute(values, 'rows', [(i, i ^ step) for i in range(devices)])  19.9 us
    all_to_all x3, starting transfers between devices, share(): return lax.all_to_all(chunks, ALL, 0, 0, tiled=True)  15.2 us
    ppermute x13, waiting for transfers between devices, row_swap(): return lax.ppermute(values, 'rows', [(i, i ^ step) for i in range(devices)])  15.1 us
    all_to_all x1, blocking collectives, share(): return lax.all_to_all(chunks, ALL, 0, 0, tiled=True)  13.2 us
    ppermute x4, starting transfers between devices, row_swaps(): return (lax.ppermute(near, 'rows', pairs), lax.ppermute(far, 'rows', odd))  4.92 us
    ppermute x4, waiting for transfers between devices, x_swap(): return lax.ppermute(values, 'x', [(0, 1), (1, 0)])  4.83 us
    all_to_all x3, waiting for transfers between devices, share(): return lax.all_to_all(chunks, ALL, 0, 0, tiled=True)  4.63 us
  transfers between devices with their start and end apart: 32, of which 9 were waited for; matrix products, arithmetic and copies ran while one was open for 2% of the time, Pallas kernels for 25%

profile of v3, /device:TPU:0, one launch (start us, length us, event | category | flops | bytes accessed | tf_op | source)
XLA Modules:
  0.0 156.6 jit_solution(17595405502755999186)
XLA Ops:
  0.7 2.8 %shard_map.323 = (f32[32,1,2048]{2,1,0:T(1,128)}, bf16[336,128]{1,0:T(8,128)(2,1)}, bf16[208,128]{1,0:T(8,128)(2,1)}, bf16[4,96,128]{2,1,0:T(8,128)(2,1)}, bf16[...) custom-call(s32[4]{0:T(128)} %counts.13, bf16[4,4,32,384]{3,2,1,0:T(8,128)(2,1)} %image.11, ...), custom_call_target="tpu_custom_call" | custom-call | bytes 1617392 | tf_op jit(solution)/shard_map/pallas_call | solution.py:40
  3.5 3.1 %collective-permute-start.7 = (bf16[4,96,128]{2,1,0:T(8,128)(2,1)}, bf16[4,96,128]{2,1,0:T(8,128)(2,1)S(1)}, u32[]{:S(2)}, u32[]{:S(2)}) collective-permute-start(bf16[4,96,128]{2,1,0:T(8,128)(2,1)} %get-tuple-element.118), channel_id=1, source_target_pairs={{0,4},{4,0},{8,12},{12,8},{16,20},{20,16},{24,28},{28,24},{1,5},{5... | collective-permute-start | bytes 294920 | tf_op jit(solution)/shard_map/ppermute | solution.py:937
  7.2 2.9 %collective-permute-start = (bf16[336,128]{1,0:T(8,128)(2,1)}, bf16[336,128]{1,0:T(8,128)(2,1)S(1)}, u32[]{:S(2)}, u32[]{:S(2)}) collective-permute-start(bf16[336,128]{1,0:T(8,128)(2,1)} %get-tuple-element.114), channel_id=1, source_target_pairs={{0,8},{4,12},{8,0},{12,4},{16,24},{20,28},{24,16},{28,20},{1,9},{5... | collective-permute-start | bytes 258056 | tf_op jit(solution)/shard_map/ppermute | solution.py:942
  10.1 2.9 %collective-permute-start.1 = (bf16[336,128]{1,0:T(8,128)(2,1)}, bf16[336,128]{1,0:T(8,128)(2,1)S(1)}, u32[]{:S(2)}, u32[]{:S(2)}) collective-permute-start(bf16[336,128]{1,0:T(8,128)(2,1)} %get-tuple-element.114), channel_id=1, source_target_pairs={{0,16},{4,20},{8,24},{12,28},{16,0},{20,4},{24,8},{28,12},{1,17},{... | collective-permute-start | bytes 258056 | tf_op jit(solution)/shard_map/ppermute | solution.py:942
  13.0 7.4 %all-to-all-start = ((f32[32,1,2048]{2,1,0:T(1,128)}), f32[32,1,2048]{2,1,0:T(1,128)S(1)}, u32[]{:S(2)}, u32[]{:S(2)}) async-start(f32[32,1,2048]{2,1,0:T(1,128)} %get-tuple-element.120), calls=%async_computation | async-start | bytes 524288 | tf_op jit(solution)/shard_map/all_to_all | solution.py:925
  23.3 2.4 %collective-permute-start.5 = (bf16[208,128]{1,0:T(8,128)(2,1)}, bf16[208,128]{1,0:T(8,128)(2,1)S(1)}, u32[]{:S(2)}, u32[]{:S(2)}) collective-permute-start(bf16[208,128]{1,0:T(8,128)(2,1)} %get-tuple-element.116), channel_id=1, source_target_pairs={{0,16},{4,20},{8,24},{12,28},{16,0},{20,4},{24,8},{28,12},{1,17},{... | collective-permute-start | bytes 159752 | tf_op jit(solution)/shard_map/ppermute | solution.py:942
  27.2 6.5 %collective-permute-done.5 = bf16[208,128]{1,0:T(8,128)(2,1)S(1)} collective-permute-done((bf16[208,128]{1,0:T(8,128)(2,1)}, bf16[208,128]{1,0:T(8,128)(2,1)S(1)}, u32[]{:S(2)}, u32[]{:S(2)}) %collective-permute-start.5) | collective-permute-done | bytes 53280 | tf_op jit(solution)/shard_map/ppermute | solution.py:942
  35.4 4.0 %shard_map.324 = (bf16[4,6,32,1536]{3,2,1,0:T(8,128)(2,1)}, f32[4,1152]{1,0:T(4,128)}, f32[2,384]{1,0:T(2,128)}, f32[16,256]{1,0:T(8,128)}, bf16[4,192,128]{2,1,0:T(8,128)(2,1)}, /*index=5*/bf16[4,192,128]{2,1,0:T(8,128)(2,1)}) custom-call(s32[4]{0:T(128)} %counts.13, f32[32,1,2048]{2,1,0:T(1,128)} %copy-done.25, bf16[4,4,32,384]{3,2,1,0:T(8,128)(2,1)} %image.11, ...), custom_call_target="tpu_custom_call" | custom-call | bytes 3642384 | tf_op jit(solution)/shard_map/pallas_call | solution.py:40
  43.2 9.0 %shard_map.325 = (f32[4,10,2,32,192]{4,3,2,1,0:T(8,128)}, bf16[3456,192]{1,0:T(8,128)(2,1)}, f32[32,1,384]{2,1,0:T(1,128)}) custom-call(s32[4]{0:T(128)} %counts.13, bf16[4,6,32,1536]{3,2,1,0:T(8,128)(2,1)} %get-tuple-element.125.slots.acts_from, bf16[4,336,128]{2,1,0:T(8,128)(2,1)} %copy-done.26, bf16[4,336,128]{2,1,0:T(8,128)(2,1)} %copy-done.32, ...), custom_call_target="tpu_custom_call" | custom-call | flops 3397386240 | bytes 7077904 | tf_op jit(solution)/shard_map/pallas_call | solution.py:40
  52.2 2.5 %collective-permute-done.10.near = bf16[4,192,128]{2,1,0:T(8,128)(2,1)S(1)} collective-permute-done((bf16[4,192,128]{2,1,0:T(8,128)(2,1)}, bf16[4,192,128]{2,1,0:T(8,128)(2,1)S(1)}, u32[]{:S(2)}, u32[]{:S(2)}) %collective-permute-start.10) | collective-permute-done | bytes 196640 | tf_op jit(solution)/shard_map/ppermute | solution.py:937
  54.8 4.4 %all-to-all-start.1 = ((f32[32,1,384]{2,1,0:T(1,128)}), f32[32,1,384]{2,1,0:T(1,128)S(1)}, u32[]{:S(2)}, u32[]{:S(2)}) async-start(f32[32,1,384]{2,1,0:T(1,128)} %get-tuple-element.128), calls=%async_computation.1 | async-start | bytes 98304 | tf_op jit(solution)/shard_map/all_to_all | solution.py:925
  60.0 9.1 %shard_map.326 = (f32[4,10,2,32,192]{4,3,2,1,0:T(8,128)}, bf16[4,8,2,32,192]{4,3,2,1,0:T(8,128)(2,1)}, bf16[4,8,2,32,192]{4,3,2,1,0:T(8,128)(2,1)}, bf16[4,4,32,...) custom-call(s32[4]{0:T(128)} %counts.13, ...), custom_call_target="tpu_custom_call" | custom-call | flops 1698693120 | bytes 7610384 | tf_op jit(solution)/shard_map/pallas_call | solution.py:40
  69.8 6.3 %shard_map.327 = (f32[2,256]{1,0:T(2,128)}, f32[8,512]{1,0:T(8,128)}, f32[32,1,384]{2,1,0:T(1,128)}, bf16[4,10,32,1024]{3,2,1,0:T(8,128)(2,1)}, f32[4,10,2,32,192]{4,3,2,1,0:T(8,128)}) custom-call(s32[4]{0:T(128)} %counts.13, f32[32,1,384]{2,1,0:T(1,128)} %copy-done.28, f32[16,256]{1,0:T(8,128)} %get-tuple-element.150.spec, ...), custom_call_target="tpu_custom_call" | custom-call | bytes 4739088 | tf_op jit(solution)/shard_map/pallas_call | solution.py:40
  76.1 13.2 %all_to_all.20.got = f32[32,1,384]{2,1,0:T(1,128)S(1)} all-to-all(f32[32,1,384]{2,1,0:T(1,128)} %get-tuple-element.140), channel_id=1, replica_groups=mesh['rows'=8,'x'=2,'core'=2] {'rows','x','core'}, dimensions={0} | all-to-all | bytes 98304 | tf_op jit(solution)/shard_map/all_to_all | solution.py:925
  90.0 12.4 %shard_map.328 = (f32[8,256]{1,0:T(8,128)S(1)}, f32[16,264,128]{2,1,0:T(8,128)S(1)}, f32[16,264,128]{2,1,0:T(8,128)S(1)}, bf16[4,2,5,32,1024]{4,3,2,1,0:T(8,128)(2,1)}) custom-call(s32[4]{0:T(128)S(1)} %copy-done.15, f32[32,1,384]{2,1,0:T(1,128)S(1)} %all_to_all.20.got, f32[2,256]{1,0:T(2,128)S(1)} %copy-done.17, f32[16,256]{1,0:T(8,128)S(1)} %copy-done.11, ...), custom_call_target="tpu_custom_call" | custom-call | flops 2717908992 | bytes 7612432 | tf_op jit(solution)/shard_map/pallas_call | solution.py:40
  102.6 4.1 %shard_map.329 = (bf16[4,8,64,192]{3,2,1,0:T(8,128)(2,1)}, f32[8,128]{1,0:T(8,128)S(1)}) custom-call(bf16[4,10,32,1024]{3,2,1,0:T(8,128)(2,1)S(1)} %copy-done.1, bf16[3,768,192]{2,1,0:T(8,128)(2,1)S(1)} %copy-done.21, bf16[4,8,2,32,192]{4,3,2,1,0:T(8,128)(2,1)S(1)} %copy-done.22, f32[4,4,32,192]{3,2,1,0:T(8,128)S(1)} %copy-done.23, f32[16,256]{1,0:T(8,128)S(1)} %copy-done.11), custom_call_target="tpu_custom_call" | custom-call | flops 2717908992 | bytes 5492736 | tf_op jit(solution)/shard_map/pallas_call | solution.py:40
  108.3 8.8 %shard_map.330 = (f32[4,4,32,384]{3,2,1,0:T(8,128)}, f32[32,1,1664]{2,1,0:T(1,128)}) custom-call(bf16[4,2,5,32,1024]{4,3,2,1,0:T(8,128)(2,1)} %get-tuple-element.152.slots, bf16[3456,192]{1,0:T(8,128)(2,1)} %get-tuple-element.153.weight, bf16[4,4,32,384]{3,2,1,0:T(8,128)(2,1)} %image.11, f32[2,384]{1,0:T(2,128)} %get-tuple-element.154.stats, ...), custom_call_target="tpu_custom_call" | custom-call | flops 2717908992 | bytes 5399552 | tf_op jit(solution)/shard_map/pallas_call | solution.py:40
  117.1 3.3 %all-to-all-start.3 = ((f32[32,1,1664]{2,1,0:T(1,128)}), f32[32,1,1664]{2,1,0:T(1,128)}, u32[]{:S(2)}, u32[]{:S(2)}) async-start(f32[32,1,1664]{2,1,0:T(1,128)} %get-tuple-element.159), calls=%async_computation.3 | async-start | bytes 425984 | tf_op jit(solution)/shard_map/all_to_all | solution.py:925
  125.2 4.6 %all-to-all-done.3.got = f32[32,1,1664]{2,1,0:T(1,128)} async-done(((f32[32,1,1664]{2,1,0:T(1,128)}), f32[32,1,1664]{2,1,0:T(1,128)}, u32[]{:S(2)}, u32[]{:S(2)}) %all-to-all-start.3) | async-done | bytes 213024 | tf_op jit(solution)/shard_map/all_to_all | solution.py:925
  129.8 2.8 %collective-permute-done.21.got_a = f32[2,264,128]{2,1,0:T(8,128)S(1)} collective-permute-done((f32[2,264,128]{2,1,0:T(8,128)}, f32[2,264,128]{2,1,0:T(8,128)S(1)}, u32[]{:S(2)}, u32[]{:S(2)}) %collective-permute-start.21) | collective-permute-done | bytes 270368 | tf_op jit(solution)/shard_map/ppermute | solution.py:942
  134.7 2.2 %collective-permute-start.24 = (f32[1,264,128]{2,1,0:T(8,128)S(1)}, f32[1,264,128]{2,1,0:T(8,128)S(1)}, u32[]{:S(2)}, u32[]{:S(2)}) collective-permute-start(f32[1,264,128]{2,1,0:T(8,128)S(1)} %get-tuple-element.186), channel_id=1, source_target_pairs={{0,16},{4,20},{8,24},{12,28},{16,0},{20,4},{24,8},{28,12},{1,17},{... | collective-permute-start | bytes 405512 | tf_op jit(solution)/shard_map/ppermute | solution.py:942
  138.3 3.3 %shard_map.331 = (f32[4,4,32,384]{3,2,1,0:T(8,128)}, f32[144,148]{1,0:T(8,128)}, f32[144,148]{1,0:T(8,128)}, f32[144,148]{1,0:T(8,128)}, f32[1,24]{1,0:T(1,128)}...) custom-call(s32[4]{0:T(128)} %counts.13, f32[32,1,1664]{2,1,0:T(1,128)} %all-to-all-done.3.got, ...), custom_call_target="tpu_custom_call" | custom-call | bytes 3065552 | tf_op jit(solution)/shard_map/pallas_call | solution.py:40
  141.6 5.6 %collective-permute-done.24.refs_2_ = f32[1,264,128]{2,1,0:T(8,128)S(1)} collective-permute-done((f32[1,264,128]{2,1,0:T(8,128)S(1)}, f32[1,264,128]{2,1,0:T(8,128)S(1)}, u32[]{:S(2)}, u32[]{:S(2)}) %collective-permute-start.24) | collective-permute-done | bytes 135200 | tf_op jit(solution)/shard_map/ppermute | solution.py:942
  148.0 4.3 %collective-permute-done.26.beside = f32[1,264,128]{2,1,0:T(8,128)S(1)} collective-permute-done((f32[1,264,128]{2,1,0:T(8,128)S(1)}, f32[1,264,128]{2,1,0:T(8,128)S(1)}, u32[]{:S(2)}, u32[]{:S(2)}) %collective-permute-start.26) | collective-permute-done | bytes 135200 | tf_op jit(solution)/shard_map/ppermute | solution.py:946
  (142 shorter events, 27.2 us)
Async XLA Ops:
  3.5 9.6 %collective-permute-start.7 = (bf16[4,96,128]{2,1,0:T(8,128)(2,1)}, bf16[4,96,128]{2,1,0:T(8,128)(2,1)S(1)}, u32[]{:S(2)}, u32[]{:S(2)}) collective-permute-start(bf16[4,96,128]{2,1,0:T(8,128)(2,1)} %get-tuple-element.118), channel_id=1, source_target_pairs={{0,4},{4,0},{8,12},{12,8},{16,20},{20,16},{24,28},{28,24},{1,5},{5... | collective-permute-start | bytes 294920 | tf_op jit(solution)/shard_map/ppermute | solution.py:937
  6.5 6.5 %collective-permute-start.8 = (bf16[4,96,128]{2,1,0:T(8,128)(2,1)}, bf16[4,96,128]{2,1,0:T(8,128)(2,1)S(1)}, u32[]{:S(2)}, u32[]{:S(2)}) collective-permute-start(bf16[4,96,128]{2,1,0:T(8,128)(2,1)} %get-tuple-element.119), channel_id=1, source_target_pairs={{4,8},{12,16},{20,24},{8,4},{16,12},{24,20},{5,9},{13,17},{21,25},... | collective-permute-start | bytes 294920 | tf_op jit(solution)/shard_map/ppermute | solution.py:937
  7.2 13.3 %collective-permute-start = (bf16[336,128]{1,0:T(8,128)(2,1)}, bf16[336,128]{1,0:T(8,128)(2,1)S(1)}, u32[]{:S(2)}, u32[]{:S(2)}) collective-permute-start(bf16[336,128]{1,0:T(8,128)(2,1)} %get-tuple-element.114), channel_id=1, source_target_pairs={{0,8},{4,12},{8,0},{12,4},{16,24},{20,28},{24,16},{28,20},{1,9},{5... | collective-permute-start | bytes 258056 | tf_op jit(solution)/shard_map/ppermute | solution.py:942
  10.1 10.5 %collective-permute-start.1 = (bf16[336,128]{1,0:T(8,128)(2,1)}, bf16[336,128]{1,0:T(8,128)(2,1)S(1)}, u32[]{:S(2)}, u32[]{:S(2)}) collective-permute-start(bf16[336,128]{1,0:T(8,128)(2,1)} %get-tuple-element.114), channel_id=1, source_target_pairs={{0,16},{4,20},{8,24},{12,28},{16,0},{20,4},{24,8},{28,12},{1,17},{... | collective-permute-start | bytes 258056 | tf_op jit(solution)/shard_map/ppermute | solution.py:942
  13.0 7.6 %collective-permute-start.2 = (bf16[336,128]{1,0:T(8,128)(2,1)}, bf16[336,128]{1,0:T(8,128)(2,1)S(1)}, u32[]{:S(2)}, u32[]{:S(2)}) collective-permute-start(bf16[336,128]{1,0:T(8,128)(2,1)} %get-tuple-element.114), channel_id=1, source_target_pairs={{0,24},{4,28},{8,16},{12,20},{16,8},{20,12},{24,0},{28,4},{1,25},{... | collective-permute-start | bytes 258056 | tf_op jit(solution)/shard_map/ppermute | solution.py:942
  13.0 21.6 %all-to-all-start = ((f32[32,1,2048]{2,1,0:T(1,128)}), f32[32,1,2048]{2,1,0:T(1,128)S(1)}, u32[]{:S(2)}, u32[]{:S(2)}) async-start(f32[32,1,2048]{2,1,0:T(1,128)} %get-tuple-element.120), calls=%async_computation | async-start | bytes 524288 | tf_op jit(solution)/shard_map/all_to_all | solution.py:925
  21.6 17.9 %collective-permute-start.3 = (bf16[4,336,128]{2,1,0:T(8,128)(2,1)S(1)}, bf16[4,336,128]{2,1,0:T(8,128)(2,1)S(1)}, u32[]{:S(2)}, u32[]{:S(2)}) collective-permute-start(bf16[4,336,128]{2,1,0:T(8,128)(2,1)S(1)} %pad_maximum_fusion.mine_near), channel_id=1, source_target_pairs={{0,4},{4,0},{8,12},{12,8},{16,20},{20,16},{24,28},{28,24},{1,5},{5... | collective-permute-start | bytes 1032200 | tf_op jit(solution)/shard_map/ppermute | solution.py:942
  23.3 10.5 %collective-permute-start.5 = (bf16[208,128]{1,0:T(8,128)(2,1)}, bf16[208,128]{1,0:T(8,128)(2,1)S(1)}, u32[]{:S(2)}, u32[]{:S(2)}) collective-permute-start(bf16[208,128]{1,0:T(8,128)(2,1)} %get-tuple-element.116), channel_id=1, source_target_pairs={{0,16},{4,20},{8,24},{12,28},{16,0},{20,4},{24,8},{28,12},{1,17},{... | collective-permute-start | bytes 159752 | tf_op jit(solution)/shard_map/ppermute | solution.py:942
  25.8 8.0 %collective-permute-start.6 = (bf16[208,128]{1,0:T(8,128)(2,1)}, bf16[208,128]{1,0:T(8,128)(2,1)S(1)}, u32[]{:S(2)}, u32[]{:S(2)}) collective-permute-start(bf16[208,128]{1,0:T(8,128)(2,1)} %get-tuple-element.116), channel_id=1, source_target_pairs={{0,24},{4,28},{8,16},{12,20},{16,8},{20,12},{24,0},{28,4},{1,25},{... | collective-permute-start | bytes 159752 | tf_op jit(solution)/shard_map/ppermute | solution.py:942
  27.2 6.6 %collective-permute-start.4 = (bf16[208,128]{1,0:T(8,128)(2,1)}, bf16[208,128]{1,0:T(8,128)(2,1)S(1)}, u32[]{:S(2)}, u32[]{:S(2)}) collective-permute-start(bf16[208,128]{1,0:T(8,128)(2,1)} %get-tuple-element.116), channel_id=1, source_target_pairs={{0,8},{4,12},{8,0},{12,4},{16,24},{20,28},{24,16},{28,20},{1,9},{5... | collective-permute-start | bytes 159752 | tf_op jit(solution)/shard_map/ppermute | solution.py:942
  27.2 14.5 %collective-permute-start.12 = (bf16[4,336,128]{2,1,0:T(8,128)(2,1)S(1)}, bf16[4,336,128]{2,1,0:T(8,128)(2,1)S(1)}, u32[]{:S(2)}, u32[]{:S(2)}) collective-permute-start(bf16[4,336,128]{2,1,0:T(8,128)(2,1)S(1)} %pad_maximum_fusion.mine_near), channel_id=1, source_target_pairs={{0,1},{1,0},{2,3},{3,2},{4,5},{5,4},{6,7},{7,6},{8,9},{9,8},{10,11... | collective-permute-start | bytes 1032200 | tf_op jit(solution)/shard_map/ppermute | solution.py:929
  39.5 15.2 %collective-permute-start.9 = (bf16[4,208,128]{2,1,0:T(8,128)(2,1)S(1)}, bf16[4,208,128]{2,1,0:T(8,128)(2,1)S(1)}, u32[]{:S(2)}, u32[]{:S(2)}) collective-permute-start(bf16[4,208,128]{2,1,0:T(8,128)(2,1)S(1)} %pad_maximum_fusion.1.mine_near), channel_id=1, source_target_pairs={{0,4},{4,0},{8,12},{12,8},{16,20},{20,16},{24,28},{28,24},{1,5},{5... | collective-permute-start | bytes 638984 | tf_op jit(solution)/shard_map/ppermute | solution.py:942
  41.0 18.2 %collective-permute-start.14 = (bf16[4,208,128]{2,1,0:T(8,128)(2,1)S(1)}, bf16[4,208,128]{2,1,0:T(8,128)(2,1)S(1)}, u32[]{:S(2)}, u32[]{:S(2)}) collective-permute-start(bf16[4,208,128]{2,1,0:T(8,128)(2,1)S(1)} %pad_maximum_fusion.1.mine_near), channel_id=1, source_target_pairs={{0,1},{1,0},{2,3},{3,2},{4,5},{5,4},{6,7},{7,6},{8,9},{9,8},{10,11... | collective-permute-start | bytes 638984 | tf_op jit(solution)/shard_map/ppermute | solution.py:929
  41.2 13.5 %collective-permute-start.10 = (bf16[4,192,128]{2,1,0:T(8,128)(2,1)}, bf16[4,192,128]{2,1,0:T(8,128)(2,1)S(1)}, u32[]{:S(2)}, u32[]{:S(2)}) collective-permute-start(bf16[4,192,128]{2,1,0:T(8,128)(2,1)} %get-tuple-element.123), channel_id=1, source_target_pairs={{0,4},{4,0},{8,12},{12,8},{16,20},{20,16},{24,28},{28,24},{1,5},{5... | collective-permute-start | bytes 589832 | tf_op jit(solution)/shard_map/ppermute | solution.py:937
  41.8 12.9 %collective-permute-start.11 = (bf16[4,192,128]{2,1,0:T(8,128)(2,1)}, bf16[4,192,128]{2,1,0:T(8,128)(2,1)S(1)}, u32[]{:S(2)}, u32[]{:S(2)}) collective-permute-start(bf16[4,192,128]{2,1,0:T(8,128)(2,1)} %get-tuple-element.124), channel_id=1, source_target_pairs={{4,8},{12,16},{20,24},{8,4},{16,12},{24,20},{5,9},{13,17},{21,25},... | collective-permute-start | bytes 589832 | tf_op jit(solution)/shard_map/ppermute | solution.py:937
  54.8 14.4 %all-to-all-start.1 = ((f32[32,1,384]{2,1,0:T(1,128)}), f32[32,1,384]{2,1,0:T(1,128)S(1)}, u32[]{:S(2)}, u32[]{:S(2)}) async-start(f32[32,1,384]{2,1,0:T(1,128)} %get-tuple-element.128), calls=%async_computation.1 | async-start | bytes 98304 | tf_op jit(solution)/shard_map/all_to_all | solution.py:925
  107.0 15.1 %collective-permute-start.19 = (f32[2,2,264,128]{3,2,1,0:T(8,128)S(1)}, f32[2,2,264,128]{3,2,1,0:T(8,128)S(1)}, u32[]{:S(2)}, u32[]{:S(2)}) collective-permute-start(f32[2,2,264,128]{3,2,1,0:T(8,128)S(1)} %get-tuple-element.169), channel_id=1, source_target_pairs={{0,2},{2,0},{1,3},{3,1},{4,6},{6,4},{5,7},{7,5},{8,10},{10,8},{9,1... | collective-permute-start | bytes 1622024 | tf_op jit(solution)/shard_map/ppermute | solution.py:946
  107.5 14.6 %collective-permute-start.20 = (f32[2,2,264,128]{3,2,1,0:T(8,128)S(1)}, f32[2,2,264,128]{3,2,1,0:T(8,128)S(1)}, u32[]{:S(2)}, u32[]{:S(2)}) collective-permute-start(f32[2,2,264,128]{3,2,1,0:T(8,128)S(1)} %get-tuple-element.171), channel_id=1, source_target_pairs={{0,4},{4,0},{8,12},{12,8},{16,20},{20,16},{24,28},{28,24},{1,5},{5... | collective-permute-start | bytes 1622024 | tf_op jit(solution)/shard_map/ppermute | solution.py:942
  117.1 12.7 %all-to-all-start.3 = ((f32[32,1,1664]{2,1,0:T(1,128)}), f32[32,1,1664]{2,1,0:T(1,128)}, u32[]{:S(2)}, u32[]{:S(2)}) async-start(f32[32,1,1664]{2,1,0:T(1,128)} %get-tuple-element.159), calls=%async_computation.3 | async-start | bytes 425984 | tf_op jit(solution)/shard_map/all_to_all | solution.py:925
  123.1 9.6 %collective-permute-start.21 = (f32[2,264,128]{2,1,0:T(8,128)}, f32[2,264,128]{2,1,0:T(8,128)S(1)}, u32[]{:S(2)}, u32[]{:S(2)}) collective-permute-start(f32[2,264,128]{2,1,0:T(8,128)} %get-tuple-element.177), channel_id=1, source_target_pairs={{0,4},{4,0},{8,12},{12,8},{16,20},{20,16},{24,28},{28,24},{1,5},{5... | collective-permute-start | bytes 811016 | tf_op jit(solution)/shard_map/ppermute | solution.py:942
  124.6 8.5 %collective-permute-start.22 = (f32[2,264,128]{2,1,0:T(8,128)S(1)}, f32[2,264,128]{2,1,0:T(8,128)S(1)}, u32[]{:S(2)}, u32[]{:S(2)}) collective-permute-start(f32[2,264,128]{2,1,0:T(8,128)S(1)} %get-tuple-element.179), channel_id=1, source_target_pairs={{0,2},{2,0},{1,3},{3,1},{4,6},{6,4},{5,7},{7,5},{8,10},{10,8},{9,1... | collective-permute-start | bytes 811016 | tf_op jit(solution)/shard_map/ppermute | solution.py:946
  133.2 8.4 %collective-permute-start.23 = (f32[1,264,128]{2,1,0:T(8,128)S(1)}, f32[1,264,128]{2,1,0:T(8,128)S(1)}, u32[]{:S(2)}, u32[]{:S(2)}) collective-permute-start(f32[1,264,128]{2,1,0:T(8,128)S(1)} %get-tuple-element.185), channel_id=1, source_target_pairs={{0,8},{4,12},{8,0},{12,4},{16,24},{20,28},{24,16},{28,20},{1,9},{5... | collective-permute-start | bytes 405512 | tf_op jit(solution)/shard_map/ppermute | solution.py:942
  134.7 12.4 %collective-permute-start.24 = (f32[1,264,128]{2,1,0:T(8,128)S(1)}, f32[1,264,128]{2,1,0:T(8,128)S(1)}, u32[]{:S(2)}, u32[]{:S(2)}) collective-permute-start(f32[1,264,128]{2,1,0:T(8,128)S(1)} %get-tuple-element.186), channel_id=1, source_target_pairs={{0,16},{4,20},{8,24},{12,28},{16,0},{20,4},{24,8},{28,12},{1,17},{... | collective-permute-start | bytes 405512 | tf_op jit(solution)/shard_map/ppermute | solution.py:942
  137.0 10.2 %collective-permute-start.25 = (f32[1,264,128]{2,1,0:T(8,128)S(1)}, f32[1,264,128]{2,1,0:T(8,128)S(1)}, u32[]{:S(2)}, u32[]{:S(2)}) collective-permute-start(f32[1,264,128]{2,1,0:T(8,128)S(1)} %get-tuple-element.187), channel_id=1, source_target_pairs={{0,24},{4,28},{8,16},{12,20},{16,8},{20,12},{24,0},{28,4},{1,25},{... | collective-permute-start | bytes 405512 | tf_op jit(solution)/shard_map/ppermute | solution.py:942
  (48 other events, 666.0 us)

commit v4 on v3

--- a/solution.py
+++ b/solution.py
@@ -27,16 +27,18 @@
     return jax.ShapeDtypeStruct(tuple(dims), kind)
 
 
-def run(kernel, outs, args, scratch=(), scalars=1, flops=0, limit=VMEM_LIMIT, whole=(), results=()):
+def run(kernel, outs, args, scratch=(), scalars=1, flops=0, limit=VMEM_LIMIT, whole=(), results=(), idle=False):
     spec = pl.BlockSpec(memory_space=pltpu.VMEM)
     specs = [pl.BlockSpec(memory_space=pltpu.SMEM)] * scalars + [spec] * (len(args) - scalars)
     specs += [pl.BlockSpec(memory_space=pl.ANY)] * len(whole)
     moved = sum(a.size * a.dtype.itemsize for a in args)
+    moved += sum(np.prod(o.shape) * np.dtype(o.dtype).itemsize for o in outs)
     args = [*args, *whole]
+    if idle:
+        moved = 0
     scratch = [pltpu.VMEM(a.shape, a.dtype) for a in (*whole, *results)] + list(scratch)
     out_specs = [spec] * len(outs) + [pl.BlockSpec(memory_space=pl.ANY)] * len(results)
     outs = [*outs, *results]
-    moved += sum(np.prod(o.shape) * np.dtype(o.dtype).itemsize for o in outs)
     return pl.pallas_call(
         kernel,
         out_shape=tuple(outs),
@@ -200,6 +202,21 @@
     where = lax.broadcasted_iota(jnp.int32, values.shape, 0)
     edge = 0 if step < 0 else width - 1
     return jnp.where(where == edge, 0.0, rolled)
+
+
+def padded(values, size):
+    rest = size - values.shape[1]
+    if not rest:
+        return values
+    return jnp.concatenate([values, jnp.zeros((values.shape[0], rest), values.dtype)], axis=1)
+
+
+def fill(ref, where, phase, value, slot):
+    value = padded(value, slot)
+    at = (1 + phase) * slot
+    ref[(*where, slice(None), slice(at, at + slot))] = value.astype(BF16)
+    step, at = (-1, 0) if phase else (1, 3 * slot)
+    ref[(*where, slice(None), slice(at, at + slot))] = shifted(value, step).astype(BF16)
 
 
 def dot(a, b, dims=((1,), (0,)), precision=None):
@@ -457,7 +474,6 @@
         flip[2 - dy, (2 - dx) * s.slot : (2 - dx) * s.slot + s.out, :] = back
     skip_w[...] = wide[9 * s.out : 9 * s.out + s.chan, :].astype(BF16)
 
-    slots[...] = jnp.zeros_like(slots)
     inv_two = spec[4:5, : s.out]
     inv_skip = spec[5:6, : s.out]
 
@@ -475,14 +491,7 @@
             if own is not None:
                 phases[b, own, ph] = value.astype(BF16)
                 grad_low[b, own, ph] = low
-            at = (1 + ph) * s.slot
-            slots[b, q, :, at : at + s.out] = low
-            if ph == 1:
-                slots[b, q, :, : s.out] = shifted(low.astype(F32), -1).astype(BF16)
-            else:
-                slots[b, q, :, 3 * s.slot : 3 * s.slot + s.out] = shifted(
-                    low.astype(F32), 1
-                ).astype(BF16)
+            fill(slots, (b, q), ph, low.astype(F32), s.slot)
         return both[0] + both[1]
 
     def edge_row(ref, b, k):
@@ -546,7 +555,6 @@
     stats[1:2, : s.out] = rstd
     scale = inv * rstd
     offset = mean * rstd
-    slots[...] = jnp.zeros_like(slots)
     base = 2 * s.chan
 
     def one(b, e, keep):
@@ -561,12 +569,7 @@
             act = pre * sig
             if keep is not None:
                 act = act * keep
-            at = (1 + ph) * s.slot
-            slots[b, e, :, at : at + s.out] = act.astype(BF16)
-            if ph == 1:
-                slots[b, e, :, : s.out] = shifted(act, -1).astype(BF16)
-            else:
-                slots[b, e, :, 3 * s.slot : 3 * s.slot + s.out] = shifted(act, 1).astype(BF16)
+            fill(slots, (b, e), ph, act, s.slot)
             dpre = dact[b, e, ph] * (sig * (1.0 + pre * (1.0 - sig)))
             dnorm[b, e, ph] = gain * dpre
             if keep is None:
@@ -697,7 +700,6 @@
     inv = spec[3:4, : s.out]
     total = sums[:, : s.out] / count
     cross = sums[:, s.out : 2 * s.out] / count
-    slots[...] = jnp.zeros_like(slots)
     norm_scale = inv * rstd
     offset = mean * rstd
 
@@ -711,17 +713,9 @@
             if own:
                 dots += jnp.sum((grad * raw).reshape(w // 8, 8, s.out), axis=0)
             value = grad * inv
-            small = value.astype(BF16)
-            at = (1 + ph) * s.slot
-            slots[b, par, k, :, at : at + s.out] = small
+            fill(slots, (b, par, k), ph, value, s.slot)
             if own:
-                low[1 - par, ph, b, (e - 1) // 2] = small
-            if ph == 1:
-                slots[b, par, k, :, : s.out] = shifted(value, -1).astype(BF16)
-            else:
-                slots[b, par, k, :, 3 * s.slot : 3 * s.slot + s.out] = shifted(value, 1).astype(
-                    BF16
-                )
+                low[1 - par, ph, b, (e - 1) // 2] = value.astype(BF16)
         return dots
 
     scale[...] = jnp.zeros_like(scale)
@@ -1157,7 +1151,9 @@
         ],
         [group_counts, got_one, image_in, near, far],
         [pltpu.SemaphoreType.DMA((2,))],
+        flops=0, idle=True,
         whole=[out_cotangent],
+        limit=52 * 2**20,
     )
     near_one = jnp.stack(blocks)
     (half_two,) = tied([half_two], [near_one])
@@ -1178,6 +1174,7 @@
         [group_counts, acts, *blocks_one],
         [scratch((1, s.pay_two), F32), scratch((9 * s.chan, s.out), F32)],
         flops=2 * n * s.ext * 2 * w * 9 * s.chan * s.out,
+        limit=52 * 2**20,
     )
     far_two, near_cot, far_cot, pay = lax.optimization_barrier((far_two, near_cot, far_cot, pay))
     blocks_two = near_two, far_two, core_swap(near_two), core_swap(far_two)
@@ -1202,6 +1199,7 @@
             scratch((3, depth, s.out), BF16),
         ],
         flops=2 * n * s.ext * 2 * w * 9 * s.out * s.out,
+        limit=52 * 2**20,
     )
     stats_two, terms_two, pay, slots_two, dnorm = run(
         bind(norm_two_kernel, s),
@@ -1210,6 +1208,7 @@
         [scratch((1, s.pay_two), F32), pltpu.SemaphoreType.DMA((4, n))],
         whole=[hidden, dact],
         results=[shape((n, s.ext, w, 4 * s.slot), BF16), shape((n, s.ext, 2, w, s.out))],
+        limit=53 * 2**20,
     )
     got_three = share(pay)
     sent = shape((s.rows_n * n_x, s.grad_rows, LANES))

time: 157 us -> 153 us (0.975)
  local copies, waits for them, and re-layouts: 4.33 us -> 1.5 us
  Pallas kernels: 63.1 us -> 60.9 us
    unnamed x80 -> x60, local copies, waits for them, and re-layouts: 4.33 us -> 1.5 us
    pallas_call x14, Pallas kernels: 63.1 us -> 60.9 us  [run(): pl.pallas_call(kernel, out_shape=tuple(outs), in_specs=specs, out_specs=t...]
where the time goes in v4:
time: 153 us; the launch traced here: 152 us
  Pallas kernels  60.9 us (40%)
  starting transfers between devices  43.9 us (29%)
  waiting for transfers between devices  29.4 us (19%)
  blocking collectives  13 us (8%)
  other arithmetic  2.41 us (2%)
    pallas_call x14, Pallas kernels, run(): pl.pallas_call(kernel, out_shape=tuple(outs), in_specs=specs, out_specs=t...  60.9 us
    ppermute x13, starting transfers between devices, row_swap(): return lax.ppermute(values, 'rows', [(i, i ^ step) for i in range(devices)])  19.9 us
    all_to_all x3, starting transfers between devices, share(): return lax.all_to_all(chunks, ALL, 0, 0, tiled=True)  15.3 us
    ppermute x13, waiting for transfers between devices, row_swap(): return lax.ppermute(values, 'rows', [(i, i ^ step) for i in range(devices)])  15.1 us
    all_to_all x1, blocking collectives, share(): return lax.all_to_all(chunks, ALL, 0, 0, tiled=True)  13 us
    ppermute x4, starting transfers between devices, row_swaps(): return (lax.ppermute(near, 'rows', pairs), lax.ppermute(far, 'rows', odd))  4.92 us
    ppermute x4, waiting for transfers between devices, x_swap(): return lax.ppermute(values, 'x', [(0, 1), (1, 0)])  4.83 us
    all_to_all x3, waiting for transfers between devices, share(): return lax.all_to_all(chunks, ALL, 0, 0, tiled=True)  4.63 us
  transfers between devices with their start and end apart: 32, of which 9 were waited for; matrix products, arithmetic and copies ran while one was open for 2% of the time, Pallas kernels for 25%

profile of v4, /device:TPU:0, one launch (start us, length us, event | category | flops | bytes accessed | tf_op | source)
XLA Modules:
  0.0 152.4 jit_solution(14602161880590851580)
XLA Ops:
  0.7 2.8 %shard_map.323 = (f32[32,1,2048]{2,1,0:T(1,128)}, bf16[336,128]{1,0:T(8,128)(2,1)}, bf16[208,128]{1,0:T(8,128)(2,1)}, bf16[4,96,128]{2,1,0:T(8,128)(2,1)}, bf16[...) custom-call(s32[4]{0:T(128)} %counts.13, bf16[4,4,32,384]{3,2,1,0:T(8,128)(2,1)} %image.11, ...), custom_call_target="tpu_custom_call" | custom-call | bytes 1617392 | tf_op jit(solution)/shard_map/pallas_call | solution.py:42
  3.5 3.1 %collective-permute-start.7 = (bf16[4,96,128]{2,1,0:T(8,128)(2,1)}, bf16[4,96,128]{2,1,0:T(8,128)(2,1)S(1)}, u32[]{:S(2)}, u32[]{:S(2)}) collective-permute-start(bf16[4,96,128]{2,1,0:T(8,128)(2,1)} %get-tuple-element.118), channel_id=1, source_target_pairs={{0,4},{4,0},{8,12},{12,8},{16,20},{20,16},{24,28},{28,24},{1,5},{5... | collective-permute-start | bytes 294920 | tf_op jit(solution)/shard_map/ppermute | solution.py:931
  7.2 2.9 %collective-permute-start = (bf16[336,128]{1,0:T(8,128)(2,1)}, bf16[336,128]{1,0:T(8,128)(2,1)S(1)}, u32[]{:S(2)}, u32[]{:S(2)}) collective-permute-start(bf16[336,128]{1,0:T(8,128)(2,1)} %get-tuple-element.114), channel_id=1, source_target_pairs={{0,8},{4,12},{8,0},{12,4},{16,24},{20,28},{24,16},{28,20},{1,9},{5... | collective-permute-start | bytes 258056 | tf_op jit(solution)/shard_map/ppermute | solution.py:936
  10.1 2.9 %collective-permute-start.1 = (bf16[336,128]{1,0:T(8,128)(2,1)}, bf16[336,128]{1,0:T(8,128)(2,1)S(1)}, u32[]{:S(2)}, u32[]{:S(2)}) collective-permute-start(bf16[336,128]{1,0:T(8,128)(2,1)} %get-tuple-element.114), channel_id=1, source_target_pairs={{0,16},{4,20},{8,24},{12,28},{16,0},{20,4},{24,8},{28,12},{1,17},{... | collective-permute-start | bytes 258056 | tf_op jit(solution)/shard_map/ppermute | solution.py:936
  13.1 7.5 %all-to-all-start = ((f32[32,1,2048]{2,1,0:T(1,128)}), f32[32,1,2048]{2,1,0:T(1,128)S(1)}, u32[]{:S(2)}, u32[]{:S(2)}) async-start(f32[32,1,2048]{2,1,0:T(1,128)} %get-tuple-element.120), calls=%async_computation | async-start | bytes 524288 | tf_op jit(solution)/shard_map/all_to_all | solution.py:919
  23.4 2.4 %collective-permute-start.5 = (bf16[208,128]{1,0:T(8,128)(2,1)}, bf16[208,128]{1,0:T(8,128)(2,1)S(1)}, u32[]{:S(2)}, u32[]{:S(2)}) collective-permute-start(bf16[208,128]{1,0:T(8,128)(2,1)} %get-tuple-element.116), channel_id=1, source_target_pairs={{0,16},{4,20},{8,24},{12,28},{16,0},{20,4},{24,8},{28,12},{1,17},{... | collective-permute-start | bytes 159752 | tf_op jit(solution)/shard_map/ppermute | solution.py:936
  27.3 6.6 %collective-permute-done.5 = bf16[208,128]{1,0:T(8,128)(2,1)S(1)} collective-permute-done((bf16[208,128]{1,0:T(8,128)(2,1)}, bf16[208,128]{1,0:T(8,128)(2,1)S(1)}, u32[]{:S(2)}, u32[]{:S(2)}) %collective-permute-start.5) | collective-permute-done | bytes 53280 | tf_op jit(solution)/shard_map/ppermute | solution.py:936
  34.7 3.4 %shard_map.324 = (bf16[4,6,32,1536]{3,2,1,0:T(8,128)(2,1)}, f32[4,1152]{1,0:T(4,128)S(1)}, f32[2,384]{1,0:T(2,128)S(1)}, f32[16,256]{1,0:T(8,128)S(1)}, bf16[4,1...) custom-call(s32[4]{0:T(128)S(1)} %copy-done.17, f32[32,1,2048]{2,1,0:T(1,128)S(1)} %all-to-all-done.got, ...), custom_call_target="tpu_custom_call" | custom-call | tf_op jit(solution)/shard_map/pallas_call | solution.py:42
  41.2 8.6 %shard_map.325 = (f32[4,10,2,32,192]{4,3,2,1,0:T(8,128)}, bf16[3456,192]{1,0:T(8,128)(2,1)}, f32[32,1,384]{2,1,0:T(1,128)}) custom-call(s32[4]{0:T(128)S(1)} %copy-done.17, bf16[4,6,32,1536]{3,2,1,0:T(8,128)(2,1)} %get-tuple-element.125.slots.acts_from, bf16[4,336,128]{2,1,0:T(8,128)(2,1)S(1)} %pad_maximum_fusion.mine_near, ...), custom_call_target="tpu_custom_call" | custom-call | flops 3397386240 | bytes 7077904 | tf_op jit(solution)/shard_map/pallas_call | solution.py:42
  49.8 3.5 %collective-permute-done.10.near = bf16[4,192,128]{2,1,0:T(8,128)(2,1)S(1)} collective-permute-done((bf16[4,192,128]{2,1,0:T(8,128)(2,1)S(1)}, bf16[4,192,128]{2,1,0:T(8,128)(2,1)S(1)}, u32[]{:S(2)}, u32[]{:S(2)}) %collective-permute-start.10) | collective-permute-done | bytes 196640 | tf_op jit(solution)/shard_map/ppermute | solution.py:931
  53.3 4.5 %all-to-all-start.1 = ((f32[32,1,384]{2,1,0:T(1,128)}), f32[32,1,384]{2,1,0:T(1,128)S(1)}, u32[]{:S(2)}, u32[]{:S(2)}) async-start(f32[32,1,384]{2,1,0:T(1,128)} %get-tuple-element.128), calls=%async_computation.1 | async-start | bytes 98304 | tf_op jit(solution)/shard_map/all_to_all | solution.py:919
  57.9 8.7 %shard_map.326 = (f32[4,10,2,32,192]{4,3,2,1,0:T(8,128)}, bf16[4,8,2,32,192]{4,3,2,1,0:T(8,128)(2,1)}, bf16[4,8,2,32,192]{4,3,2,1,0:T(8,128)(2,1)}, bf16[4,4,32,...) custom-call(s32[4]{0:T(128)S(1)} %copy-done.17, ...), custom_call_target="tpu_custom_call" | custom-call | flops 1698693120 | bytes 7610384 | tf_op jit(solution)/shard_map/pallas_call | solution.py:42
  67.3 5.4 %shard_map.327 = (f32[2,256]{1,0:T(2,128)S(1)}, f32[8,512]{1,0:T(8,128)S(1)}, f32[32,1,384]{2,1,0:T(1,128)S(1)}, bf16[4,10,32,1024]{3,2,1,0:T(8,128)(2,1)}, f32[4,10,2,32,192]{4,3,2,1,0:T(8,128)}) custom-call(s32[4]{0:T(128)S(1)} %copy-done.17, f32[32,1,384]{2,1,0:T(1,128)S(1)} %all-to-all-done.1.got, f32[16,256]{1,0:T(8,128)S(1)} %get-tuple-element.150.spec, ...), custom_call_target="tpu_custom_call" | custom-call | bytes 151568 | tf_op jit(solution)/shard_map/pallas_call | solution.py:42
  72.8 13.0 %all_to_all.20.got = f32[32,1,384]{2,1,0:T(1,128)S(1)} all-to-all(f32[32,1,384]{2,1,0:T(1,128)S(1)} %get-tuple-element.140), channel_id=1, replica_groups=mesh['rows'=8,'x'=2,'core'=2] {'rows','x','core'}, dimensions={0} | all-to-all | bytes 98304 | tf_op jit(solution)/shard_map/all_to_all | solution.py:919
  85.8 12.4 %shard_map.328 = (f32[8,256]{1,0:T(8,128)S(1)}, f32[16,264,128]{2,1,0:T(8,128)S(1)}, f32[16,264,128]{2,1,0:T(8,128)S(1)}, bf16[4,2,5,32,1024]{4,3,2,1,0:T(8,128)(2,1)}) custom-call(s32[4]{0:T(128)S(1)} %copy-done.17, f32[32,1,384]{2,1,0:T(1,128)S(1)} %all_to_all.20.got, f32[2,256]{1,0:T(2,128)S(1)} %get-tuple-element.141.stats, ...), custom_call_target="tpu_custom_call" | custom-call | flops 2717908992 | bytes 665616 | tf_op jit(solution)/shard_map/pallas_call | solution.py:42
  98.4 4.1 %shard_map.329 = (bf16[4,8,64,192]{3,2,1,0:T(8,128)(2,1)}, f32[8,128]{1,0:T(8,128)S(1)}) custom-call(bf16[4,10,32,1024]{3,2,1,0:T(8,128)(2,1)S(1)} %copy-done.2, bf16[3,768,192]{2,1,0:T(8,128)(2,1)S(1)} %copy-done.24, bf16[4,8,2,32,192]{4,3,2,1,0:T(8,128)(2,1)S(1)} %copy-done.25, f32[4,4,32,192]{3,2,1,0:T(8,128)S(1)} %copy-done.26, ...), custom_call_target="tpu_custom_call" | custom-call | flops 2717908992 | bytes 5492736 | tf_op jit(solution)/shard_map/pallas_call | solution.py:42
  104.1 8.8 %shard_map.330 = (f32[4,4,32,384]{3,2,1,0:T(8,128)}, f32[32,1,1664]{2,1,0:T(1,128)}) custom-call(bf16[4,2,5,32,1024]{4,3,2,1,0:T(8,128)(2,1)} %get-tuple-element.152.slots, bf16[3456,192]{1,0:T(8,128)(2,1)} %get-tuple-element.153.weight, bf16[4,4,32,384]{3,2,1,0:T(8,128)(2,1)} %image.11, f32[2,384]{1,0:T(2,128)} %copy-done.19, f32[4,1152]{1,0:T(4,128)} %copy-done.13, ...), custom_call_target="tpu_custom_call" | custom-call | flops 2717908992 | bytes 5399552 | tf_op jit(solution)/shard_map/pallas_call | solution.py:42
  112.9 3.3 %all-to-all-start.3 = ((f32[32,1,1664]{2,1,0:T(1,128)}), f32[32,1,1664]{2,1,0:T(1,128)}, u32[]{:S(2)}, u32[]{:S(2)}) async-start(f32[32,1,1664]{2,1,0:T(1,128)} %get-tuple-element.159), calls=%async_computation.3 | async-start | bytes 425984 | tf_op jit(solution)/shard_map/all_to_all | solution.py:919
  121.0 4.6 %all-to-all-done.3.got = f32[32,1,1664]{2,1,0:T(1,128)} async-done(((f32[32,1,1664]{2,1,0:T(1,128)}), f32[32,1,1664]{2,1,0:T(1,128)}, u32[]{:S(2)}, u32[]{:S(2)}) %all-to-all-start.3) | async-done | bytes 213024 | tf_op jit(solution)/shard_map/all_to_all | solution.py:919
  125.6 2.8 %collective-permute-done.21.got_a = f32[2,264,128]{2,1,0:T(8,128)S(1)} collective-permute-done((f32[2,264,128]{2,1,0:T(8,128)}, f32[2,264,128]{2,1,0:T(8,128)S(1)}, u32[]{:S(2)}, u32[]{:S(2)}) %collective-permute-start.21) | collective-permute-done | bytes 270368 | tf_op jit(solution)/shard_map/ppermute | solution.py:936
  130.5 2.2 %collective-permute-start.24 = (f32[1,264,128]{2,1,0:T(8,128)S(1)}, f32[1,264,128]{2,1,0:T(8,128)S(1)}, u32[]{:S(2)}, u32[]{:S(2)}) collective-permute-start(f32[1,264,128]{2,1,0:T(8,128)S(1)} %get-tuple-element.186), channel_id=1, source_target_pairs={{0,16},{4,20},{8,24},{12,28},{16,0},{20,4},{24,8},{28,12},{1,17},{... | collective-permute-start | bytes 405512 | tf_op jit(solution)/shard_map/ppermute | solution.py:936
  134.1 3.3 %shard_map.331 = (f32[4,4,32,384]{3,2,1,0:T(8,128)}, f32[144,148]{1,0:T(8,128)}, f32[144,148]{1,0:T(8,128)}, f32[144,148]{1,0:T(8,128)}, f32[1,24]{1,0:T(1,128)}...) custom-call(s32[4]{0:T(128)} %counts.13, f32[32,1,1664]{2,1,0:T(1,128)} %all-to-all-done.3.got, ...), custom_call_target="tpu_custom_call" | custom-call | bytes 3065552 | tf_op jit(solution)/shard_map/pallas_call | solution.py:42
  137.4 5.6 %collective-permute-done.24.refs_2_ = f32[1,264,128]{2,1,0:T(8,128)S(1)} collective-permute-done((f32[1,264,128]{2,1,0:T(8,128)S(1)}, f32[1,264,128]{2,1,0:T(8,128)S(1)}, u32[]{:S(2)}, u32[]{:S(2)}) %collective-permute-start.24) | collective-permute-done | bytes 135200 | tf_op jit(solution)/shard_map/ppermute | solution.py:936
  143.7 4.3 %collective-permute-done.26.beside = f32[1,264,128]{2,1,0:T(8,128)S(1)} collective-permute-done((f32[1,264,128]{2,1,0:T(8,128)S(1)}, f32[1,264,128]{2,1,0:T(8,128)S(1)}, u32[]{:S(2)}, u32[]{:S(2)}) %collective-permute-start.26) | collective-permute-done | bytes 135200 | tf_op jit(solution)/shard_map/ppermute | solution.py:940
  (122 shorter events, 24.3 us)
Async XLA Ops:
  3.5 9.6 %collective-permute-start.7 = (bf16[4,96,128]{2,1,0:T(8,128)(2,1)}, bf16[4,96,128]{2,1,0:T(8,128)(2,1)S(1)}, u32[]{:S(2)}, u32[]{:S(2)}) collective-permute-start(bf16[4,96,128]{2,1,0:T(8,128)(2,1)} %get-tuple-element.118), channel_id=1, source_target_pairs={{0,4},{4,0},{8,12},{12,8},{16,20},{20,16},{24,28},{28,24},{1,5},{5... | collective-permute-start | bytes 294920 | tf_op jit(solution)/shard_map/ppermute | solution.py:931
  6.6 6.5 %collective-permute-start.8 = (bf16[4,96,128]{2,1,0:T(8,128)(2,1)}, bf16[4,96,128]{2,1,0:T(8,128)(2,1)S(1)}, u32[]{:S(2)}, u32[]{:S(2)}) collective-permute-start(bf16[4,96,128]{2,1,0:T(8,128)(2,1)} %get-tuple-element.119), channel_id=1, source_target_pairs={{4,8},{12,16},{20,24},{8,4},{16,12},{24,20},{5,9},{13,17},{21,25},... | collective-permute-start | bytes 294920 | tf_op jit(solution)/shard_map/ppermute | solution.py:931
  7.2 13.3 %collective-permute-start = (bf16[336,128]{1,0:T(8,128)(2,1)}, bf16[336,128]{1,0:T(8,128)(2,1)S(1)}, u32[]{:S(2)}, u32[]{:S(2)}) collective-permute-start(bf16[336,128]{1,0:T(8,128)(2,1)} %get-tuple-element.114), channel_id=1, source_target_pairs={{0,8},{4,12},{8,0},{12,4},{16,24},{20,28},{24,16},{28,20},{1,9},{5... | collective-permute-start | bytes 258056 | tf_op jit(solution)/shard_map/ppermute | solution.py:936
  10.1 10.5 %collective-permute-start.1 = (bf16[336,128]{1,0:T(8,128)(2,1)}, bf16[336,128]{1,0:T(8,128)(2,1)S(1)}, u32[]{:S(2)}, u32[]{:S(2)}) collective-permute-start(bf16[336,128]{1,0:T(8,128)(2,1)} %get-tuple-element.114), channel_id=1, source_target_pairs={{0,16},{4,20},{8,24},{12,28},{16,0},{20,4},{24,8},{28,12},{1,17},{... | collective-permute-start | bytes 258056 | tf_op jit(solution)/shard_map/ppermute | solution.py:936
  13.1 7.6 %collective-permute-start.2 = (bf16[336,128]{1,0:T(8,128)(2,1)}, bf16[336,128]{1,0:T(8,128)(2,1)S(1)}, u32[]{:S(2)}, u32[]{:S(2)}) collective-permute-start(bf16[336,128]{1,0:T(8,128)(2,1)} %get-tuple-element.114), channel_id=1, source_target_pairs={{0,24},{4,28},{8,16},{12,20},{16,8},{20,12},{24,0},{28,4},{1,25},{... | collective-permute-start | bytes 258056 | tf_op jit(solution)/shard_map/ppermute | solution.py:936
  13.1 21.6 %all-to-all-start = ((f32[32,1,2048]{2,1,0:T(1,128)}), f32[32,1,2048]{2,1,0:T(1,128)S(1)}, u32[]{:S(2)}, u32[]{:S(2)}) async-start(f32[32,1,2048]{2,1,0:T(1,128)} %get-tuple-element.120), calls=%async_computation | async-start | bytes 524288 | tf_op jit(solution)/shard_map/all_to_all | solution.py:919
  21.6 16.5 %collective-permute-start.3 = (bf16[4,336,128]{2,1,0:T(8,128)(2,1)S(1)}, bf16[4,336,128]{2,1,0:T(8,128)(2,1)S(1)}, u32[]{:S(2)}, u32[]{:S(2)}) collective-permute-start(bf16[4,336,128]{2,1,0:T(8,128)(2,1)S(1)} %pad_maximum_fusion.mine_near), channel_id=1, source_target_pairs={{0,4},{4,0},{8,12},{12,8},{16,20},{20,16},{24,28},{28,24},{1,5},{5... | collective-permute-start | bytes 1032200 | tf_op jit(solution)/shard_map/ppermute | solution.py:936
  23.4 10.5 %collective-permute-start.5 = (bf16[208,128]{1,0:T(8,128)(2,1)}, bf16[208,128]{1,0:T(8,128)(2,1)S(1)}, u32[]{:S(2)}, u32[]{:S(2)}) collective-permute-start(bf16[208,128]{1,0:T(8,128)(2,1)} %get-tuple-element.116), channel_id=1, source_target_pairs={{0,16},{4,20},{8,24},{12,28},{16,0},{20,4},{24,8},{28,12},{1,17},{... | collective-permute-start | bytes 159752 | tf_op jit(solution)/shard_map/ppermute | solution.py:936
  25.8 8.0 %collective-permute-start.6 = (bf16[208,128]{1,0:T(8,128)(2,1)}, bf16[208,128]{1,0:T(8,128)(2,1)S(1)}, u32[]{:S(2)}, u32[]{:S(2)}) collective-permute-start(bf16[208,128]{1,0:T(8,128)(2,1)} %get-tuple-element.116), channel_id=1, source_target_pairs={{0,24},{4,28},{8,16},{12,20},{16,8},{20,12},{24,0},{28,4},{1,25},{... | collective-permute-start | bytes 159752 | tf_op jit(solution)/shard_map/ppermute | solution.py:936
  27.2 6.7 %collective-permute-start.4 = (bf16[208,128]{1,0:T(8,128)(2,1)}, bf16[208,128]{1,0:T(8,128)(2,1)S(1)}, u32[]{:S(2)}, u32[]{:S(2)}) collective-permute-start(bf16[208,128]{1,0:T(8,128)(2,1)} %get-tuple-element.116), channel_id=1, source_target_pairs={{0,8},{4,12},{8,0},{12,4},{16,24},{20,28},{24,16},{28,20},{1,9},{5... | collective-permute-start | bytes 159752 | tf_op jit(solution)/shard_map/ppermute | solution.py:936
  27.3 13.2 %collective-permute-start.12 = (bf16[4,336,128]{2,1,0:T(8,128)(2,1)S(1)}, bf16[4,336,128]{2,1,0:T(8,128)(2,1)S(1)}, u32[]{:S(2)}, u32[]{:S(2)}) collective-permute-start(bf16[4,336,128]{2,1,0:T(8,128)(2,1)S(1)} %pad_maximum_fusion.mine_near), channel_id=1, source_target_pairs={{0,1},{1,0},{2,3},{3,2},{4,5},{5,4},{6,7},{7,6},{8,9},{9,8},{10,11... | collective-permute-start | bytes 1032200 | tf_op jit(solution)/shard_map/ppermute | solution.py:923
  38.2 15.1 %collective-permute-start.9 = (bf16[4,208,128]{2,1,0:T(8,128)(2,1)S(1)}, bf16[4,208,128]{2,1,0:T(8,128)(2,1)S(1)}, u32[]{:S(2)}, u32[]{:S(2)}) collective-permute-start(bf16[4,208,128]{2,1,0:T(8,128)(2,1)S(1)} %pad_maximum_fusion.1.mine_near), channel_id=1, source_target_pairs={{0,4},{4,0},{8,12},{12,8},{16,20},{20,16},{24,28},{28,24},{1,5},{5... | collective-permute-start | bytes 638984 | tf_op jit(solution)/shard_map/ppermute | solution.py:936
  39.8 18.1 %collective-permute-start.14 = (bf16[4,208,128]{2,1,0:T(8,128)(2,1)S(1)}, bf16[4,208,128]{2,1,0:T(8,128)(2,1)S(1)}, u32[]{:S(2)}, u32[]{:S(2)}) collective-permute-start(bf16[4,208,128]{2,1,0:T(8,128)(2,1)S(1)} %pad_maximum_fusion.1.mine_near), channel_id=1, source_target_pairs={{0,1},{1,0},{2,3},{3,2},{4,5},{5,4},{6,7},{7,6},{8,9},{9,8},{10,11... | collective-permute-start | bytes 638984 | tf_op jit(solution)/shard_map/ppermute | solution.py:923
  39.9 13.4 %collective-permute-start.10 = (bf16[4,192,128]{2,1,0:T(8,128)(2,1)S(1)}, bf16[4,192,128]{2,1,0:T(8,128)(2,1)S(1)}, u32[]{:S(2)}, u32[]{:S(2)}) collective-permute-start(bf16[4,192,128]{2,1,0:T(8,128)(2,1)S(1)} %get-tuple-element.123), channel_id=1, source_target_pairs={{0,4},{4,0},{8,12},{12,8},{16,20},{20,16},{24,28},{28,24},{1,5},{5... | collective-permute-start | bytes 589832 | tf_op jit(solution)/shard_map/ppermute | solution.py:931
  40.5 12.8 %collective-permute-start.11 = (bf16[4,192,128]{2,1,0:T(8,128)(2,1)S(1)}, bf16[4,192,128]{2,1,0:T(8,128)(2,1)S(1)}, u32[]{:S(2)}, u32[]{:S(2)}) collective-permute-start(bf16[4,192,128]{2,1,0:T(8,128)(2,1)S(1)} %get-tuple-element.124), channel_id=1, source_target_pairs={{4,8},{12,16},{20,24},{8,4},{16,12},{24,20},{5,9},{13,17},{21,25},... | collective-permute-start | bytes 589832 | tf_op jit(solution)/shard_map/ppermute | solution.py:931
  53.3 13.9 %all-to-all-start.1 = ((f32[32,1,384]{2,1,0:T(1,128)}), f32[32,1,384]{2,1,0:T(1,128)S(1)}, u32[]{:S(2)}, u32[]{:S(2)}) async-start(f32[32,1,384]{2,1,0:T(1,128)} %get-tuple-element.128), calls=%async_computation.1 | async-start | bytes 98304 | tf_op jit(solution)/shard_map/all_to_all | solution.py:919
  102.8 15.2 %collective-permute-start.19 = (f32[2,2,264,128]{3,2,1,0:T(8,128)S(1)}, f32[2,2,264,128]{3,2,1,0:T(8,128)S(1)}, u32[]{:S(2)}, u32[]{:S(2)}) collective-permute-start(f32[2,2,264,128]{3,2,1,0:T(8,128)S(1)} %get-tuple-element.169), channel_id=1, source_target_pairs={{0,2},{2,0},{1,3},{3,1},{4,6},{6,4},{5,7},{7,5},{8,10},{10,8},{9,1... | collective-permute-start | bytes 1622024 | tf_op jit(solution)/shard_map/ppermute | solution.py:940
  103.3 14.6 %collective-permute-start.20 = (f32[2,2,264,128]{3,2,1,0:T(8,128)S(1)}, f32[2,2,264,128]{3,2,1,0:T(8,128)S(1)}, u32[]{:S(2)}, u32[]{:S(2)}) collective-permute-start(f32[2,2,264,128]{3,2,1,0:T(8,128)S(1)} %get-tuple-element.171), channel_id=1, source_target_pairs={{0,4},{4,0},{8,12},{12,8},{16,20},{20,16},{24,28},{28,24},{1,5},{5... | collective-permute-start | bytes 1622024 | tf_op jit(solution)/shard_map/ppermute | solution.py:936
  112.9 12.7 %all-to-all-start.3 = ((f32[32,1,1664]{2,1,0:T(1,128)}), f32[32,1,1664]{2,1,0:T(1,128)}, u32[]{:S(2)}, u32[]{:S(2)}) async-start(f32[32,1,1664]{2,1,0:T(1,128)} %get-tuple-element.159), calls=%async_computation.3 | async-start | bytes 425984 | tf_op jit(solution)/shard_map/all_to_all | solution.py:919
  118.8 9.6 %collective-permute-start.21 = (f32[2,264,128]{2,1,0:T(8,128)}, f32[2,264,128]{2,1,0:T(8,128)S(1)}, u32[]{:S(2)}, u32[]{:S(2)}) collective-permute-start(f32[2,264,128]{2,1,0:T(8,128)} %get-tuple-element.177), channel_id=1, source_target_pairs={{0,4},{4,0},{8,12},{12,8},{16,20},{20,16},{24,28},{28,24},{1,5},{5... | collective-permute-start | bytes 811016 | tf_op jit(solution)/shard_map/ppermute | solution.py:936
  120.4 8.5 %collective-permute-start.22 = (f32[2,264,128]{2,1,0:T(8,128)S(1)}, f32[2,264,128]{2,1,0:T(8,128)S(1)}, u32[]{:S(2)}, u32[]{:S(2)}) collective-permute-start(f32[2,264,128]{2,1,0:T(8,128)S(1)} %get-tuple-element.179), channel_id=1, source_target_pairs={{0,2},{2,0},{1,3},{3,1},{4,6},{6,4},{5,7},{7,5},{8,10},{10,8},{9,1... | collective-permute-start | bytes 811016 | tf_op jit(solution)/shard_map/ppermute | solution.py:940
  129.0 8.4 %collective-permute-start.23 = (f32[1,264,128]{2,1,0:T(8,128)S(1)}, f32[1,264,128]{2,1,0:T(8,128)S(1)}, u32[]{:S(2)}, u32[]{:S(2)}) collective-permute-start(f32[1,264,128]{2,1,0:T(8,128)S(1)} %get-tuple-element.185), channel_id=1, source_target_pairs={{0,8},{4,12},{8,0},{12,4},{16,24},{20,28},{24,16},{28,20},{1,9},{5... | collective-permute-start | bytes 405512 | tf_op jit(solution)/shard_map/ppermute | solution.py:936
  130.5 12.4 %collective-permute-start.24 = (f32[1,264,128]{2,1,0:T(8,128)S(1)}, f32[1,264,128]{2,1,0:T(8,128)S(1)}, u32[]{:S(2)}, u32[]{:S(2)}) collective-permute-start(f32[1,264,128]{2,1,0:T(8,128)S(1)} %get-tuple-element.186), channel_id=1, source_target_pairs={{0,16},{4,20},{8,24},{12,28},{16,0},{20,4},{24,8},{28,12},{1,17},{... | collective-permute-start | bytes 405512 | tf_op jit(solution)/shard_map/ppermute | solution.py:936
  132.8 10.2 %collective-permute-start.25 = (f32[1,264,128]{2,1,0:T(8,128)S(1)}, f32[1,264,128]{2,1,0:T(8,128)S(1)}, u32[]{:S(2)}, u32[]{:S(2)}) collective-permute-start(f32[1,264,128]{2,1,0:T(8,128)S(1)} %get-tuple-element.187), channel_id=1, source_target_pairs={{0,24},{4,28},{8,16},{12,20},{16,8},{20,12},{24,0},{28,4},{1,25},{... | collective-permute-start | bytes 405512 | tf_op jit(solution)/shard_map/ppermute | solution.py:936
  (38 other events, 661.0 us)

commit v5 on v4

--- a/solution.py
+++ b/solution.py
@@ -1138,7 +1138,7 @@
     )
     blocks = gather_upper(half_one)
     near, far = row_swaps(near, far)
-    (pay,) = tied([pay], [near, far])
+    (pay,) = tied([pay], [near])
     got_one = share(pay)
     acts, proj, stats_one, spec, near_cot, far_cot = run(
         bind(act_kernel, s),

time: 153 us -> 151 us (0.987)
  starting transfers between devices: 43.9 us -> 40.3 us
    ppermute x13, starting transfers between devices: 19.9 us -> 17.8 us  [row_swap(): return lax.ppermute(values, 'rows', [(i, i ^ step) for i in range(devices)])]
  transfers between devices with their start and end apart: 32 -> 32, of which waited for: 9 -> 10; matrix products, arithmetic and copies ran while one was open for 2% -> 2% of each run, Pallas kernels for 25% -> 25%
where the time goes in v5:
time: 151 us; the launch traced here: 150 us
  Pallas kernels  60.9 us (40%)
  starting transfers between devices  40.3 us (27%)
  waiting for transfers between devices  30.8 us (20%)
  blocking collectives  13 us (9%)
  other arithmetic  2.41 us (2%)
    pallas_call x14, Pallas kernels, run(): pl.pallas_call(kernel, out_shape=tuple(outs), in_specs=specs, out_specs=t...  60.9 us
    ppermute x13, starting transfers between devices, row_swap(): return lax.ppermute(values, 'rows', [(i, i ^ step) for i in range(devices)])  17.8 us
    ppermute x13, waiting for transfers between devices, row_swap(): return lax.ppermute(values, 'rows', [(i, i ^ step) for i in range(devices)])  16.2 us
    all_to_all x3, starting transfers between devices, share(): return lax.all_to_all(chunks, ALL, 0, 0, tiled=True)  14 us
    all_to_all x1, blocking collectives, share(): return lax.all_to_all(chunks, ALL, 0, 0, tiled=True)  13 us
    ppermute x4, waiting for transfers between devices, x_swap(): return lax.ppermute(values, 'x', [(0, 1), (1, 0)])  4.83 us
    ppermute x4, starting transfers between devices, row_swaps(): return (lax.ppermute(near, 'rows', pairs), lax.ppermute(far, 'rows', odd))  4.64 us
    all_to_all x3, waiting for transfers between devices, share(): return lax.all_to_all(chunks, ALL, 0, 0, tiled=True)  4.63 us
  transfers between devices with their start and end apart: 32, of which 10 were waited for; matrix products, arithmetic and copies ran while one was open for 2% of the time, Pallas kernels for 25%

profile of v5, /device:TPU:0, one launch (start us, length us, event | category | flops | bytes accessed | tf_op | source)
XLA Modules:
  0.0 150.1 jit_solution(4327687762130990660)
XLA Ops:
  0.7 2.8 %shard_map.323 = (f32[32,1,2048]{2,1,0:T(1,128)}, bf16[336,128]{1,0:T(8,128)(2,1)}, bf16[208,128]{1,0:T(8,128)(2,1)}, bf16[4,96,128]{2,1,0:T(8,128)(2,1)}, bf16[...) custom-call(s32[4]{0:T(128)} %counts.13, bf16[4,4,32,384]{3,2,1,0:T(8,128)(2,1)} %image.11, ...), custom_call_target="tpu_custom_call" | custom-call | bytes 1617392 | tf_op jit(solution)/shard_map/pallas_call | solution.py:42
  3.5 3.1 %collective-permute-start.7 = (bf16[4,96,128]{2,1,0:T(8,128)(2,1)}, bf16[4,96,128]{2,1,0:T(8,128)(2,1)S(1)}, u32[]{:S(2)}, u32[]{:S(2)}) collective-permute-start(bf16[4,96,128]{2,1,0:T(8,128)(2,1)} %get-tuple-element.118), channel_id=1, source_target_pairs={{0,4},{4,0},{8,12},{12,8},{16,20},{20,16},{24,28},{28,24},{1,5},{5... | collective-permute-start | bytes 294920 | tf_op jit(solution)/shard_map/ppermute | solution.py:931
  8.2 2.6 %collective-permute-start.1 = (bf16[336,128]{1,0:T(8,128)(2,1)}, bf16[336,128]{1,0:T(8,128)(2,1)S(1)}, u32[]{:S(2)}, u32[]{:S(2)}) collective-permute-start(bf16[336,128]{1,0:T(8,128)(2,1)} %get-tuple-element.114), channel_id=1, source_target_pairs={{0,16},{4,20},{8,24},{12,28},{16,0},{20,4},{24,8},{28,12},{1,17},{... | collective-permute-start | bytes 258056 | tf_op jit(solution)/shard_map/ppermute | solution.py:936
  11.0 4.9 %all-to-all-start = ((f32[32,1,2048]{2,1,0:T(1,128)}), f32[32,1,2048]{2,1,0:T(1,128)S(1)}, u32[]{:S(2)}, u32[]{:S(2)}) async-start(f32[32,1,2048]{2,1,0:T(1,128)} %get-tuple-element.119), calls=%async_computation | async-start | bytes 524288 | tf_op jit(solution)/shard_map/all_to_all | solution.py:919
  19.1 2.5 %collective-permute-start.5 = (bf16[208,128]{1,0:T(8,128)(2,1)}, bf16[208,128]{1,0:T(8,128)(2,1)S(1)}, u32[]{:S(2)}, u32[]{:S(2)}) collective-permute-start(bf16[208,128]{1,0:T(8,128)(2,1)} %get-tuple-element.116), channel_id=1, source_target_pairs={{0,16},{4,20},{8,24},{12,28},{16,0},{20,4},{24,8},{28,12},{1,17},{... | collective-permute-start | bytes 159752 | tf_op jit(solution)/shard_map/ppermute | solution.py:936
  23.6 5.6 %collective-permute-done.5 = bf16[208,128]{1,0:T(8,128)(2,1)S(1)} collective-permute-done((bf16[208,128]{1,0:T(8,128)(2,1)}, bf16[208,128]{1,0:T(8,128)(2,1)S(1)}, u32[]{:S(2)}, u32[]{:S(2)}) %collective-permute-start.5) | collective-permute-done | bytes 53280 | tf_op jit(solution)/shard_map/ppermute | solution.py:936
  30.5 3.4 %shard_map.324 = (bf16[4,6,32,1536]{3,2,1,0:T(8,128)(2,1)}, f32[4,1152]{1,0:T(4,128)S(1)}, f32[2,384]{1,0:T(2,128)S(1)}, f32[16,256]{1,0:T(8,128)S(1)}, bf16[4,1...) custom-call(s32[4]{0:T(128)S(1)} %copy-done.17, f32[32,1,2048]{2,1,0:T(1,128)S(1)} %all-to-all-done.got, ...), custom_call_target="tpu_custom_call" | custom-call | tf_op jit(solution)/shard_map/pallas_call | solution.py:42
  34.1 2.2 %collective-permute-start.9 = (bf16[4,208,128]{2,1,0:T(8,128)(2,1)S(1)}, bf16[4,208,128]{2,1,0:T(8,128)(2,1)S(1)}, u32[]{:S(2)}, u32[]{:S(2)}) collective-permute-start(bf16[4,208,128]{2,1,0:T(8,128)(2,1)S(1)} %pad_maximum_fusion.1.mine_near), channel_id=1, source_target_pairs={{0,4},{4,0},{8,12},{12,8},{16,20},{20,16},{24,28},{28,24},{1,5},{5... | collective-permute-start | bytes 638984 | tf_op jit(solution)/shard_map/ppermute | solution.py:936
  37.4 8.6 %shard_map.325 = (f32[4,10,2,32,192]{4,3,2,1,0:T(8,128)}, bf16[3456,192]{1,0:T(8,128)(2,1)}, f32[32,1,384]{2,1,0:T(1,128)}) custom-call(s32[4]{0:T(128)S(1)} %copy-done.17, bf16[4,6,32,1536]{3,2,1,0:T(8,128)(2,1)} %get-tuple-element.125.slots.acts_from, bf16[4,336,128]{2,1,0:T(8,128)(2,1)S(1)} %pad_maximum_fusion.mine_near, ...), custom_call_target="tpu_custom_call" | custom-call | flops 3397386240 | bytes 7077904 | tf_op jit(solution)/shard_map/pallas_call | solution.py:42
  46.0 3.8 %collective-permute-done.10.near = bf16[4,192,128]{2,1,0:T(8,128)(2,1)S(1)} collective-permute-done((bf16[4,192,128]{2,1,0:T(8,128)(2,1)S(1)}, bf16[4,192,128]{2,1,0:T(8,128)(2,1)S(1)}, u32[]{:S(2)}, u32[]{:S(2)}) %collective-permute-start.10) | collective-permute-done | bytes 196640 | tf_op jit(solution)/shard_map/ppermute | solution.py:931
  49.8 5.8 %all-to-all-start.1 = ((f32[32,1,384]{2,1,0:T(1,128)}), f32[32,1,384]{2,1,0:T(1,128)S(1)}, u32[]{:S(2)}, u32[]{:S(2)}) async-start(f32[32,1,384]{2,1,0:T(1,128)} %get-tuple-element.128), calls=%async_computation.1 | async-start | bytes 98304 | tf_op jit(solution)/shard_map/all_to_all | solution.py:919
  55.6 8.7 %shard_map.326 = (f32[4,10,2,32,192]{4,3,2,1,0:T(8,128)}, bf16[4,8,2,32,192]{4,3,2,1,0:T(8,128)(2,1)}, bf16[4,8,2,32,192]{4,3,2,1,0:T(8,128)(2,1)}, bf16[4,4,32,...) custom-call(s32[4]{0:T(128)S(1)} %copy-done.17, ...), custom_call_target="tpu_custom_call" | custom-call | flops 1698693120 | bytes 7610384 | tf_op jit(solution)/shard_map/pallas_call | solution.py:42
  65.0 5.4 %shard_map.327 = (f32[2,256]{1,0:T(2,128)S(1)}, f32[8,512]{1,0:T(8,128)S(1)}, f32[32,1,384]{2,1,0:T(1,128)S(1)}, bf16[4,10,32,1024]{3,2,1,0:T(8,128)(2,1)}, f32[4,10,2,32,192]{4,3,2,1,0:T(8,128)}) custom-call(s32[4]{0:T(128)S(1)} %copy-done.17, f32[32,1,384]{2,1,0:T(1,128)S(1)} %all-to-all-done.1.got, f32[16,256]{1,0:T(8,128)S(1)} %get-tuple-element.150.spec, ...), custom_call_target="tpu_custom_call" | custom-call | bytes 151568 | tf_op jit(solution)/shard_map/pallas_call | solution.py:42
  70.5 13.0 %all_to_all.20.got = f32[32,1,384]{2,1,0:T(1,128)S(1)} all-to-all(f32[32,1,384]{2,1,0:T(1,128)S(1)} %get-tuple-element.140), channel_id=1, replica_groups=mesh['rows'=8,'x'=2,'core'=2] {'rows','x','core'}, dimensions={0} | all-to-all | bytes 98304 | tf_op jit(solution)/shard_map/all_to_all | solution.py:919
  83.5 12.4 %shard_map.328 = (f32[8,256]{1,0:T(8,128)S(1)}, f32[16,264,128]{2,1,0:T(8,128)S(1)}, f32[16,264,128]{2,1,0:T(8,128)S(1)}, bf16[4,2,5,32,1024]{4,3,2,1,0:T(8,128)(2,1)}) custom-call(s32[4]{0:T(128)S(1)} %copy-done.17, f32[32,1,384]{2,1,0:T(1,128)S(1)} %all_to_all.20.got, f32[2,256]{1,0:T(2,128)S(1)} %get-tuple-element.141.stats, ...), custom_call_target="tpu_custom_call" | custom-call | flops 2717908992 | bytes 665616 | tf_op jit(solution)/shard_map/pallas_call | solution.py:42
  96.1 4.1 %shard_map.329 = (bf16[4,8,64,192]{3,2,1,0:T(8,128)(2,1)}, f32[8,128]{1,0:T(8,128)S(1)}) custom-call(bf16[4,10,32,1024]{3,2,1,0:T(8,128)(2,1)S(1)} %copy-done.2, bf16[3,768,192]{2,1,0:T(8,128)(2,1)S(1)} %copy-done.24, bf16[4,8,2,32,192]{4,3,2,1,0:T(8,128)(2,1)S(1)} %copy-done.25, f32[4,4,32,192]{3,2,1,0:T(8,128)S(1)} %copy-done.26, ...), custom_call_target="tpu_custom_call" | custom-call | flops 2717908992 | bytes 5492736 | tf_op jit(solution)/shard_map/pallas_call | solution.py:42
  101.8 8.8 %shard_map.330 = (f32[4,4,32,384]{3,2,1,0:T(8,128)}, f32[32,1,1664]{2,1,0:T(1,128)}) custom-call(bf16[4,2,5,32,1024]{4,3,2,1,0:T(8,128)(2,1)} %get-tuple-element.152.slots, bf16[3456,192]{1,0:T(8,128)(2,1)} %get-tuple-element.153.weight, bf16[4,4,32,384]{3,2,1,0:T(8,128)(2,1)} %image.11, f32[2,384]{1,0:T(2,128)} %copy-done.19, f32[4,1152]{1,0:T(4,128)} %copy-done.13, ...), custom_call_target="tpu_custom_call" | custom-call | flops 2717908992 | bytes 5399552 | tf_op jit(solution)/shard_map/pallas_call | solution.py:42
  110.6 3.3 %all-to-all-start.3 = ((f32[32,1,1664]{2,1,0:T(1,128)}), f32[32,1,1664]{2,1,0:T(1,128)}, u32[]{:S(2)}, u32[]{:S(2)}) async-start(f32[32,1,1664]{2,1,0:T(1,128)} %get-tuple-element.159), calls=%async_computation.3 | async-start | bytes 425984 | tf_op jit(solution)/shard_map/all_to_all | solution.py:919
  118.7 4.6 %all-to-all-done.3.got = f32[32,1,1664]{2,1,0:T(1,128)} async-done(((f32[32,1,1664]{2,1,0:T(1,128)}), f32[32,1,1664]{2,1,0:T(1,128)}, u32[]{:S(2)}, u32[]{:S(2)}) %all-to-all-start.3) | async-done | bytes 213024 | tf_op jit(solution)/shard_map/all_to_all | solution.py:919
  123.3 2.8 %collective-permute-done.21.got_a = f32[2,264,128]{2,1,0:T(8,128)S(1)} collective-permute-done((f32[2,264,128]{2,1,0:T(8,128)}, f32[2,264,128]{2,1,0:T(8,128)S(1)}, u32[]{:S(2)}, u32[]{:S(2)}) %collective-permute-start.21) | collective-permute-done | bytes 270368 | tf_op jit(solution)/shard_map/ppermute | solution.py:936
  128.2 2.2 %collective-permute-start.24 = (f32[1,264,128]{2,1,0:T(8,128)S(1)}, f32[1,264,128]{2,1,0:T(8,128)S(1)}, u32[]{:S(2)}, u32[]{:S(2)}) collective-permute-start(f32[1,264,128]{2,1,0:T(8,128)S(1)} %get-tuple-element.186), channel_id=1, source_target_pairs={{0,16},{4,20},{8,24},{12,28},{16,0},{20,4},{24,8},{28,12},{1,17},{... | collective-permute-start | bytes 405512 | tf_op jit(solution)/shard_map/ppermute | solution.py:936
  131.8 3.3 %shard_map.331 = (f32[4,4,32,384]{3,2,1,0:T(8,128)}, f32[144,148]{1,0:T(8,128)}, f32[144,148]{1,0:T(8,128)}, f32[144,148]{1,0:T(8,128)}, f32[1,24]{1,0:T(1,128)}...) custom-call(s32[4]{0:T(128)} %counts.13, f32[32,1,1664]{2,1,0:T(1,128)} %all-to-all-done.3.got, ...), custom_call_target="tpu_custom_call" | custom-call | bytes 3065552 | tf_op jit(solution)/shard_map/pallas_call | solution.py:42
  135.1 5.6 %collective-permute-done.24.refs_2_ = f32[1,264,128]{2,1,0:T(8,128)S(1)} collective-permute-done((f32[1,264,128]{2,1,0:T(8,128)S(1)}, f32[1,264,128]{2,1,0:T(8,128)S(1)}, u32[]{:S(2)}, u32[]{:S(2)}) %collective-permute-start.24) | collective-permute-done | bytes 135200 | tf_op jit(solution)/shard_map/ppermute | solution.py:936
  141.4 4.3 %collective-permute-done.26.beside = f32[1,264,128]{2,1,0:T(8,128)S(1)} collective-permute-done((f32[1,264,128]{2,1,0:T(8,128)S(1)}, f32[1,264,128]{2,1,0:T(8,128)S(1)}, u32[]{:S(2)}, u32[]{:S(2)}) %collective-permute-start.26) | collective-permute-done | bytes 135200 | tf_op jit(solution)/shard_map/ppermute | solution.py:940
  (122 shorter events, 25.1 us)
Async XLA Ops:
  3.5 7.4 %collective-permute-start.7 = (bf16[4,96,128]{2,1,0:T(8,128)(2,1)}, bf16[4,96,128]{2,1,0:T(8,128)(2,1)S(1)}, u32[]{:S(2)}, u32[]{:S(2)}) collective-permute-start(bf16[4,96,128]{2,1,0:T(8,128)(2,1)} %get-tuple-element.118), channel_id=1, source_target_pairs={{0,4},{4,0},{8,12},{12,8},{16,20},{20,16},{24,28},{28,24},{1,5},{5... | collective-permute-start | bytes 294920 | tf_op jit(solution)/shard_map/ppermute | solution.py:931
  6.6 9.3 %collective-permute-start = (bf16[336,128]{1,0:T(8,128)(2,1)}, bf16[336,128]{1,0:T(8,128)(2,1)S(1)}, u32[]{:S(2)}, u32[]{:S(2)}) collective-permute-start(bf16[336,128]{1,0:T(8,128)(2,1)} %get-tuple-element.114), channel_id=1, source_target_pairs={{0,8},{4,12},{8,0},{12,4},{16,24},{20,28},{24,16},{28,20},{1,9},{5... | collective-permute-start | bytes 258056 | tf_op jit(solution)/shard_map/ppermute | solution.py:936
  8.2 9.4 %collective-permute-start.1 = (bf16[336,128]{1,0:T(8,128)(2,1)}, bf16[336,128]{1,0:T(8,128)(2,1)S(1)}, u32[]{:S(2)}, u32[]{:S(2)}) collective-permute-start(bf16[336,128]{1,0:T(8,128)(2,1)} %get-tuple-element.114), channel_id=1, source_target_pairs={{0,16},{4,20},{8,24},{12,28},{16,0},{20,4},{24,8},{28,12},{1,17},{... | collective-permute-start | bytes 258056 | tf_op jit(solution)/shard_map/ppermute | solution.py:936
  10.7 6.9 %collective-permute-start.2 = (bf16[336,128]{1,0:T(8,128)(2,1)}, bf16[336,128]{1,0:T(8,128)(2,1)S(1)}, u32[]{:S(2)}, u32[]{:S(2)}) collective-permute-start(bf16[336,128]{1,0:T(8,128)(2,1)} %get-tuple-element.114), channel_id=1, source_target_pairs={{0,24},{4,28},{8,16},{12,20},{16,8},{20,12},{24,0},{28,4},{1,25},{... | collective-permute-start | bytes 258056 | tf_op jit(solution)/shard_map/ppermute | solution.py:936
  11.0 19.5 %all-to-all-start = ((f32[32,1,2048]{2,1,0:T(1,128)}), f32[32,1,2048]{2,1,0:T(1,128)S(1)}, u32[]{:S(2)}, u32[]{:S(2)}) async-start(f32[32,1,2048]{2,1,0:T(1,128)} %get-tuple-element.119), calls=%async_computation | async-start | bytes 524288 | tf_op jit(solution)/shard_map/all_to_all | solution.py:919
  18.5 15.4 %collective-permute-start.3 = (bf16[4,336,128]{2,1,0:T(8,128)(2,1)S(1)}, bf16[4,336,128]{2,1,0:T(8,128)(2,1)S(1)}, u32[]{:S(2)}, u32[]{:S(2)}) collective-permute-start(bf16[4,336,128]{2,1,0:T(8,128)(2,1)S(1)} %pad_maximum_fusion.mine_near), channel_id=1, source_target_pairs={{0,4},{4,0},{8,12},{12,8},{16,20},{20,16},{24,28},{28,24},{1,5},{5... | collective-permute-start | bytes 1032200 | tf_op jit(solution)/shard_map/ppermute | solution.py:936
  19.1 10.1 %collective-permute-start.5 = (bf16[208,128]{1,0:T(8,128)(2,1)}, bf16[208,128]{1,0:T(8,128)(2,1)S(1)}, u32[]{:S(2)}, u32[]{:S(2)}) collective-permute-start(bf16[208,128]{1,0:T(8,128)(2,1)} %get-tuple-element.116), channel_id=1, source_target_pairs={{0,16},{4,20},{8,24},{12,28},{16,0},{20,4},{24,8},{28,12},{1,17},{... | collective-permute-start | bytes 159752 | tf_op jit(solution)/shard_map/ppermute | solution.py:936
  21.6 7.6 %collective-permute-start.6 = (bf16[208,128]{1,0:T(8,128)(2,1)}, bf16[208,128]{1,0:T(8,128)(2,1)S(1)}, u32[]{:S(2)}, u32[]{:S(2)}) collective-permute-start(bf16[208,128]{1,0:T(8,128)(2,1)} %get-tuple-element.116), channel_id=1, source_target_pairs={{0,24},{4,28},{8,16},{12,20},{16,8},{20,12},{24,0},{28,4},{1,25},{... | collective-permute-start | bytes 159752 | tf_op jit(solution)/shard_map/ppermute | solution.py:936
  22.9 6.7 %collective-permute-start.4 = (bf16[208,128]{1,0:T(8,128)(2,1)}, bf16[208,128]{1,0:T(8,128)(2,1)S(1)}, u32[]{:S(2)}, u32[]{:S(2)}) collective-permute-start(bf16[208,128]{1,0:T(8,128)(2,1)} %get-tuple-element.116), channel_id=1, source_target_pairs={{0,8},{4,12},{8,0},{12,4},{16,24},{20,28},{24,16},{28,20},{1,9},{5... | collective-permute-start | bytes 159752 | tf_op jit(solution)/shard_map/ppermute | solution.py:936
  22.9 7.6 %collective-permute-start.8 = (bf16[4,96,128]{2,1,0:T(8,128)(2,1)}, bf16[4,96,128]{2,1,0:T(8,128)(2,1)S(1)}, u32[]{:S(2)}, u32[]{:S(2)}) collective-permute-start(bf16[4,96,128]{2,1,0:T(8,128)(2,1)} %get-tuple-element.120), channel_id=1, source_target_pairs={{4,8},{12,16},{20,24},{8,4},{16,12},{24,20},{5,9},{13,17},{21,25},... | collective-permute-start | bytes 294920 | tf_op jit(solution)/shard_map/ppermute | solution.py:931
  29.2 7.5 %collective-permute-start.12 = (bf16[4,336,128]{2,1,0:T(8,128)(2,1)S(1)}, bf16[4,336,128]{2,1,0:T(8,128)(2,1)S(1)}, u32[]{:S(2)}, u32[]{:S(2)}) collective-permute-start(bf16[4,336,128]{2,1,0:T(8,128)(2,1)S(1)} %pad_maximum_fusion.mine_near), channel_id=1, source_target_pairs={{0,1},{1,0},{2,3},{3,2},{4,5},{5,4},{6,7},{7,6},{8,9},{9,8},{10,11... | collective-permute-start | bytes 1032200 | tf_op jit(solution)/shard_map/ppermute | solution.py:923
  34.1 15.8 %collective-permute-start.9 = (bf16[4,208,128]{2,1,0:T(8,128)(2,1)S(1)}, bf16[4,208,128]{2,1,0:T(8,128)(2,1)S(1)}, u32[]{:S(2)}, u32[]{:S(2)}) collective-permute-start(bf16[4,208,128]{2,1,0:T(8,128)(2,1)S(1)} %pad_maximum_fusion.1.mine_near), channel_id=1, source_target_pairs={{0,4},{4,0},{8,12},{12,8},{16,20},{20,16},{24,28},{28,24},{1,5},{5... | collective-permute-start | bytes 638984 | tf_op jit(solution)/shard_map/ppermute | solution.py:936
  36.3 19.3 %collective-permute-start.14 = (bf16[4,208,128]{2,1,0:T(8,128)(2,1)S(1)}, bf16[4,208,128]{2,1,0:T(8,128)(2,1)S(1)}, u32[]{:S(2)}, u32[]{:S(2)}) collective-permute-start(bf16[4,208,128]{2,1,0:T(8,128)(2,1)S(1)} %pad_maximum_fusion.1.mine_near), channel_id=1, source_target_pairs={{0,1},{1,0},{2,3},{3,2},{4,5},{5,4},{6,7},{7,6},{8,9},{9,8},{10,11... | collective-permute-start | bytes 638984 | tf_op jit(solution)/shard_map/ppermute | solution.py:923
  36.4 13.4 %collective-permute-start.10 = (bf16[4,192,128]{2,1,0:T(8,128)(2,1)S(1)}, bf16[4,192,128]{2,1,0:T(8,128)(2,1)S(1)}, u32[]{:S(2)}, u32[]{:S(2)}) collective-permute-start(bf16[4,192,128]{2,1,0:T(8,128)(2,1)S(1)} %get-tuple-element.123), channel_id=1, source_target_pairs={{0,4},{4,0},{8,12},{12,8},{16,20},{20,16},{24,28},{28,24},{1,5},{5... | collective-permute-start | bytes 589832 | tf_op jit(solution)/shard_map/ppermute | solution.py:931
  36.7 13.1 %collective-permute-start.11 = (bf16[4,192,128]{2,1,0:T(8,128)(2,1)S(1)}, bf16[4,192,128]{2,1,0:T(8,128)(2,1)S(1)}, u32[]{:S(2)}, u32[]{:S(2)}) collective-permute-start(bf16[4,192,128]{2,1,0:T(8,128)(2,1)S(1)} %get-tuple-element.124), channel_id=1, source_target_pairs={{4,8},{12,16},{20,24},{8,4},{16,12},{24,20},{5,9},{13,17},{21,25},... | collective-permute-start | bytes 589832 | tf_op jit(solution)/shard_map/ppermute | solution.py:931
  49.8 15.2 %all-to-all-start.1 = ((f32[32,1,384]{2,1,0:T(1,128)}), f32[32,1,384]{2,1,0:T(1,128)S(1)}, u32[]{:S(2)}, u32[]{:S(2)}) async-start(f32[32,1,384]{2,1,0:T(1,128)} %get-tuple-element.128), calls=%async_computation.1 | async-start | bytes 98304 | tf_op jit(solution)/shard_map/all_to_all | solution.py:919
  100.5 15.2 %collective-permute-start.19 = (f32[2,2,264,128]{3,2,1,0:T(8,128)S(1)}, f32[2,2,264,128]{3,2,1,0:T(8,128)S(1)}, u32[]{:S(2)}, u32[]{:S(2)}) collective-permute-start(f32[2,2,264,128]{3,2,1,0:T(8,128)S(1)} %get-tuple-element.169), channel_id=1, source_target_pairs={{0,2},{2,0},{1,3},{3,1},{4,6},{6,4},{5,7},{7,5},{8,10},{10,8},{9,1... | collective-permute-start | bytes 1622024 | tf_op jit(solution)/shard_map/ppermute | solution.py:940
  101.0 14.6 %collective-permute-start.20 = (f32[2,2,264,128]{3,2,1,0:T(8,128)S(1)}, f32[2,2,264,128]{3,2,1,0:T(8,128)S(1)}, u32[]{:S(2)}, u32[]{:S(2)}) collective-permute-start(f32[2,2,264,128]{3,2,1,0:T(8,128)S(1)} %get-tuple-element.171), channel_id=1, source_target_pairs={{0,4},{4,0},{8,12},{12,8},{16,20},{20,16},{24,28},{28,24},{1,5},{5... | collective-permute-start | bytes 1622024 | tf_op jit(solution)/shard_map/ppermute | solution.py:936
  110.6 12.7 %all-to-all-start.3 = ((f32[32,1,1664]{2,1,0:T(1,128)}), f32[32,1,1664]{2,1,0:T(1,128)}, u32[]{:S(2)}, u32[]{:S(2)}) async-start(f32[32,1,1664]{2,1,0:T(1,128)} %get-tuple-element.159), calls=%async_computation.3 | async-start | bytes 425984 | tf_op jit(solution)/shard_map/all_to_all | solution.py:919
  116.5 9.6 %collective-permute-start.21 = (f32[2,264,128]{2,1,0:T(8,128)}, f32[2,264,128]{2,1,0:T(8,128)S(1)}, u32[]{:S(2)}, u32[]{:S(2)}) collective-permute-start(f32[2,264,128]{2,1,0:T(8,128)} %get-tuple-element.177), channel_id=1, source_target_pairs={{0,4},{4,0},{8,12},{12,8},{16,20},{20,16},{24,28},{28,24},{1,5},{5... | collective-permute-start | bytes 811016 | tf_op jit(solution)/shard_map/ppermute | solution.py:936
  118.1 8.5 %collective-permute-start.22 = (f32[2,264,128]{2,1,0:T(8,128)S(1)}, f32[2,264,128]{2,1,0:T(8,128)S(1)}, u32[]{:S(2)}, u32[]{:S(2)}) collective-permute-start(f32[2,264,128]{2,1,0:T(8,128)S(1)} %get-tuple-element.179), channel_id=1, source_target_pairs={{0,2},{2,0},{1,3},{3,1},{4,6},{6,4},{5,7},{7,5},{8,10},{10,8},{9,1... | collective-permute-start | bytes 811016 | tf_op jit(solution)/shard_map/ppermute | solution.py:940
  126.7 8.4 %collective-permute-start.23 = (f32[1,264,128]{2,1,0:T(8,128)S(1)}, f32[1,264,128]{2,1,0:T(8,128)S(1)}, u32[]{:S(2)}, u32[]{:S(2)}) collective-permute-start(f32[1,264,128]{2,1,0:T(8,128)S(1)} %get-tuple-element.185), channel_id=1, source_target_pairs={{0,8},{4,12},{8,0},{12,4},{16,24},{20,28},{24,16},{28,20},{1,9},{5... | collective-permute-start | bytes 405512 | tf_op jit(solution)/shard_map/ppermute | solution.py:936
  128.2 12.4 %collective-permute-start.24 = (f32[1,264,128]{2,1,0:T(8,128)S(1)}, f32[1,264,128]{2,1,0:T(8,128)S(1)}, u32[]{:S(2)}, u32[]{:S(2)}) collective-permute-start(f32[1,264,128]{2,1,0:T(8,128)S(1)} %get-tuple-element.186), channel_id=1, source_target_pairs={{0,16},{4,20},{8,24},{12,28},{16,0},{20,4},{24,8},{28,12},{1,17},{... | collective-permute-start | bytes 405512 | tf_op jit(solution)/shard_map/ppermute | solution.py:936
  130.5 10.2 %collective-permute-start.25 = (f32[1,264,128]{2,1,0:T(8,128)S(1)}, f32[1,264,128]{2,1,0:T(8,128)S(1)}, u32[]{:S(2)}, u32[]{:S(2)}) collective-permute-start(f32[1,264,128]{2,1,0:T(8,128)S(1)} %get-tuple-element.187), channel_id=1, source_target_pairs={{0,24},{4,28},{8,16},{12,20},{16,8},{20,12},{24,0},{28,4},{1,25},{... | collective-permute-start | bytes 405512 | tf_op jit(solution)/shard_map/ppermute | solution.py:936
  (38 other events, 656.5 us)

commit v6 on v5

--- a/solution.py
+++ b/solution.py
@@ -1176,7 +1176,7 @@
         flops=2 * n * s.ext * 2 * w * 9 * s.chan * s.out,
         limit=52 * 2**20,
     )
-    far_two, near_cot, far_cot, pay = lax.optimization_barrier((far_two, near_cot, far_cot, pay))
+    far_two, near_cot, pay = lax.optimization_barrier((far_two, near_cot, pay))
     blocks_two = near_two, far_two, core_swap(near_two), core_swap(far_two)
     got_two = share(pay)
     dact, phases, grad_low, grad_skip, skip_part, weight_two, weight_skip, misc = run(

time: 151 us -> 151 us (level)
  waiting for transfers between devices: 30.8 us -> 28 us
  starting transfers between devices: 40.3 us -> 42.1 us
    ppermute x4, waiting for transfers between devices: 3.79 us -> 0.98 us  [row_swaps(): return (lax.ppermute(near, 'rows', pairs), lax.ppermute(far, 'rows', odd))]
    all_to_all x3, starting transfers between devices: 14 us -> 15.8 us  [share(): return lax.all_to_all(chunks, ALL, 0, 0, tiled=True)]
where the time goes in v6:
time: 151 us; the launch traced here: 150 us
  Pallas kernels  60.9 us (40%)
  starting transfers between devices  42.1 us (28%)
  waiting for transfers between devices  28 us (19%)
  blocking collectives  14 us (9%)
  other arithmetic  2.41 us (2%)
    pallas_call x14, Pallas kernels, run(): pl.pallas_call(kernel, out_shape=tuple(outs), in_specs=specs, out_specs=t...  60.9 us
    ppermute x13, starting transfers between devices, row_swap(): return lax.ppermute(values, 'rows', [(i, i ^ step) for i in range(devices)])  17.8 us
    ppermute x13, waiting for transfers between devices, row_swap(): return lax.ppermute(values, 'rows', [(i, i ^ step) for i in range(devices)])  16.2 us
    all_to_all x3, starting transfers between devices, share(): return lax.all_to_all(chunks, ALL, 0, 0, tiled=True)  15.8 us
    all_to_all x1, blocking collectives, share(): return lax.all_to_all(chunks, ALL, 0, 0, tiled=True)  14 us
    ppermute x4, waiting for transfers between devices, x_swap(): return lax.ppermute(values, 'x', [(0, 1), (1, 0)])  4.83 us
    ppermute x4, starting transfers between devices, row_swaps(): return (lax.ppermute(near, 'rows', pairs), lax.ppermute(far, 'rows', odd))  4.64 us
    all_to_all x3, waiting for transfers between devices, share(): return lax.all_to_all(chunks, ALL, 0, 0, tiled=True)  4.63 us
  transfers between devices with their start and end apart: 32, of which 10 were waited for; matrix products, arithmetic and copies ran while one was open for 2% of the time, Pallas kernels for 25%

profile of v6, /device:TPU:0, one launch (start us, length us, event | category | flops | bytes accessed | tf_op | source)
XLA Modules:
  0.0 150.1 jit_solution(2675182434965850445)
XLA Ops:
  0.7 2.8 %shard_map.323 = (f32[32,1,2048]{2,1,0:T(1,128)}, bf16[336,128]{1,0:T(8,128)(2,1)}, bf16[208,128]{1,0:T(8,128)(2,1)}, bf16[4,96,128]{2,1,0:T(8,128)(2,1)}, bf16[...) custom-call(s32[4]{0:T(128)} %counts.13, bf16[4,4,32,384]{3,2,1,0:T(8,128)(2,1)} %image.11, ...), custom_call_target="tpu_custom_call" | custom-call | bytes 1617392 | tf_op jit(solution)/shard_map/pallas_call | solution.py:42
  3.5 3.1 %collective-permute-start.7 = (bf16[4,96,128]{2,1,0:T(8,128)(2,1)}, bf16[4,96,128]{2,1,0:T(8,128)(2,1)S(1)}, u32[]{:S(2)}, u32[]{:S(2)}) collective-permute-start(bf16[4,96,128]{2,1,0:T(8,128)(2,1)} %get-tuple-element.117), channel_id=1, source_target_pairs={{0,4},{4,0},{8,12},{12,8},{16,20},{20,16},{24,28},{28,24},{1,5},{5... | collective-permute-start | bytes 294920 | tf_op jit(solution)/shard_map/ppermute | solution.py:931
  8.2 2.6 %collective-permute-start.1 = (bf16[336,128]{1,0:T(8,128)(2,1)}, bf16[336,128]{1,0:T(8,128)(2,1)S(1)}, u32[]{:S(2)}, u32[]{:S(2)}) collective-permute-start(bf16[336,128]{1,0:T(8,128)(2,1)} %get-tuple-element.113), channel_id=1, source_target_pairs={{0,16},{4,20},{8,24},{12,28},{16,0},{20,4},{24,8},{28,12},{1,17},{... | collective-permute-start | bytes 258056 | tf_op jit(solution)/shard_map/ppermute | solution.py:936
  11.0 4.9 %all-to-all-start = ((f32[32,1,2048]{2,1,0:T(1,128)}), f32[32,1,2048]{2,1,0:T(1,128)S(1)}, u32[]{:S(2)}, u32[]{:S(2)}) async-start(f32[32,1,2048]{2,1,0:T(1,128)} %get-tuple-element.118), calls=%async_computation | async-start | bytes 524288 | tf_op jit(solution)/shard_map/all_to_all | solution.py:919
  19.1 2.5 %collective-permute-start.5 = (bf16[208,128]{1,0:T(8,128)(2,1)}, bf16[208,128]{1,0:T(8,128)(2,1)S(1)}, u32[]{:S(2)}, u32[]{:S(2)}) collective-permute-start(bf16[208,128]{1,0:T(8,128)(2,1)} %get-tuple-element.115), channel_id=1, source_target_pairs={{0,16},{4,20},{8,24},{12,28},{16,0},{20,4},{24,8},{28,12},{1,17},{... | collective-permute-start | bytes 159752 | tf_op jit(solution)/shard_map/ppermute | solution.py:936
  23.6 5.6 %collective-permute-done.5 = bf16[208,128]{1,0:T(8,128)(2,1)S(1)} collective-permute-done((bf16[208,128]{1,0:T(8,128)(2,1)}, bf16[208,128]{1,0:T(8,128)(2,1)S(1)}, u32[]{:S(2)}, u32[]{:S(2)}) %collective-permute-start.5) | collective-permute-done | bytes 53280 | tf_op jit(solution)/shard_map/ppermute | solution.py:936
  30.5 3.4 %shard_map.324 = (bf16[4,6,32,1536]{3,2,1,0:T(8,128)(2,1)}, f32[4,1152]{1,0:T(4,128)S(1)}, f32[2,384]{1,0:T(2,128)S(1)}, f32[16,256]{1,0:T(8,128)S(1)}, bf16[4,1...) custom-call(s32[4]{0:T(128)S(1)} %copy-done.17, f32[32,1,2048]{2,1,0:T(1,128)S(1)} %all-to-all-done.got, ...), custom_call_target="tpu_custom_call" | custom-call | tf_op jit(solution)/shard_map/pallas_call | solution.py:42
  34.1 2.2 %collective-permute-start.9 = (bf16[4,208,128]{2,1,0:T(8,128)(2,1)S(1)}, bf16[4,208,128]{2,1,0:T(8,128)(2,1)S(1)}, u32[]{:S(2)}, u32[]{:S(2)}) collective-permute-start(bf16[4,208,128]{2,1,0:T(8,128)(2,1)S(1)} %pad_maximum_fusion.1.mine_near), channel_id=1, source_target_pairs={{0,4},{4,0},{8,12},{12,8},{16,20},{20,16},{24,28},{28,24},{1,5},{5... | collective-permute-start | bytes 638984 | tf_op jit(solution)/shard_map/ppermute | solution.py:936
  36.7 8.6 %shard_map.325 = (f32[4,10,2,32,192]{4,3,2,1,0:T(8,128)}, bf16[3456,192]{1,0:T(8,128)(2,1)}, f32[32,1,384]{2,1,0:T(1,128)}) custom-call(s32[4]{0:T(128)S(1)} %copy-done.17, bf16[4,6,32,1536]{3,2,1,0:T(8,128)(2,1)} %get-tuple-element.123.slots.acts_from, bf16[4,336,128]{2,1,0:T(8,128)(2,1)S(1)} %pad_maximum_fusion.mine_near, ...), custom_call_target="tpu_custom_call" | custom-call | flops 3397386240 | bytes 7077904 | tf_op jit(solution)/shard_map/pallas_call | solution.py:42
  47.0 7.6 %all-to-all-start.1 = ((f32[32,1,384]{2,1,0:T(1,128)}), f32[32,1,384]{2,1,0:T(1,128)S(1)}, u32[]{:S(2)}, u32[]{:S(2)}) async-start(f32[32,1,384]{2,1,0:T(1,128)} %get-tuple-element.126), calls=%async_computation.1 | async-start | bytes 98304 | tf_op jit(solution)/shard_map/all_to_all | solution.py:919
  54.7 8.7 %shard_map.326 = (f32[4,10,2,32,192]{4,3,2,1,0:T(8,128)}, bf16[4,8,2,32,192]{4,3,2,1,0:T(8,128)(2,1)}, bf16[4,8,2,32,192]{4,3,2,1,0:T(8,128)(2,1)}, bf16[4,4,32,...) custom-call(s32[4]{0:T(128)S(1)} %copy-done.17, ...), custom_call_target="tpu_custom_call" | custom-call | flops 1698693120 | bytes 7610384 | tf_op jit(solution)/shard_map/pallas_call | solution.py:42
  64.1 5.4 %shard_map.327 = (f32[2,256]{1,0:T(2,128)S(1)}, f32[8,512]{1,0:T(8,128)S(1)}, f32[32,1,384]{2,1,0:T(1,128)S(1)}, bf16[4,10,32,1024]{3,2,1,0:T(8,128)(2,1)}, f32[4,10,2,32,192]{4,3,2,1,0:T(8,128)}) custom-call(s32[4]{0:T(128)S(1)} %copy-done.17, f32[32,1,384]{2,1,0:T(1,128)S(1)} %all-to-all-done.1.got, f32[16,256]{1,0:T(8,128)S(1)} %get-tuple-element.148.spec, ...), custom_call_target="tpu_custom_call" | custom-call | bytes 151568 | tf_op jit(solution)/shard_map/pallas_call | solution.py:42
  69.5 14.0 %all_to_all.20.got = f32[32,1,384]{2,1,0:T(1,128)S(1)} all-to-all(f32[32,1,384]{2,1,0:T(1,128)S(1)} %get-tuple-element.138), channel_id=1, replica_groups=mesh['rows'=8,'x'=2,'core'=2] {'rows','x','core'}, dimensions={0} | all-to-all | bytes 98304 | tf_op jit(solution)/shard_map/all_to_all | solution.py:919
  83.5 12.4 %shard_map.328 = (f32[8,256]{1,0:T(8,128)S(1)}, f32[16,264,128]{2,1,0:T(8,128)S(1)}, f32[16,264,128]{2,1,0:T(8,128)S(1)}, bf16[4,2,5,32,1024]{4,3,2,1,0:T(8,128)(2,1)}) custom-call(s32[4]{0:T(128)S(1)} %copy-done.17, f32[32,1,384]{2,1,0:T(1,128)S(1)} %all_to_all.20.got, f32[2,256]{1,0:T(2,128)S(1)} %get-tuple-element.139.stats, ...), custom_call_target="tpu_custom_call" | custom-call | flops 2717908992 | bytes 665616 | tf_op jit(solution)/shard_map/pallas_call | solution.py:42
  96.1 4.1 %shard_map.329 = (bf16[4,8,64,192]{3,2,1,0:T(8,128)(2,1)}, f32[8,128]{1,0:T(8,128)S(1)}) custom-call(bf16[4,10,32,1024]{3,2,1,0:T(8,128)(2,1)S(1)} %copy-done.2, bf16[3,768,192]{2,1,0:T(8,128)(2,1)S(1)} %copy-done.24, bf16[4,8,2,32,192]{4,3,2,1,0:T(8,128)(2,1)S(1)} %copy-done.25, f32[4,4,32,192]{3,2,1,0:T(8,128)S(1)} %copy-done.26, ...), custom_call_target="tpu_custom_call" | custom-call | flops 2717908992 | bytes 5492736 | tf_op jit(solution)/shard_map/pallas_call | solution.py:42
  101.8 8.8 %shard_map.330 = (f32[4,4,32,384]{3,2,1,0:T(8,128)}, f32[32,1,1664]{2,1,0:T(1,128)}) custom-call(bf16[4,2,5,32,1024]{4,3,2,1,0:T(8,128)(2,1)} %get-tuple-element.150.slots, bf16[3456,192]{1,0:T(8,128)(2,1)} %get-tuple-element.151.weight, bf16[4,4,32,384]{3,2,1,0:T(8,128)(2,1)} %image.11, f32[2,384]{1,0:T(2,128)} %copy-done.19, f32[4,1152]{1,0:T(4,128)} %copy-done.13, ...), custom_call_target="tpu_custom_call" | custom-call | flops 2717908992 | bytes 5399552 | tf_op jit(solution)/shard_map/pallas_call | solution.py:42
  110.7 3.3 %all-to-all-start.3 = ((f32[32,1,1664]{2,1,0:T(1,128)}), f32[32,1,1664]{2,1,0:T(1,128)}, u32[]{:S(2)}, u32[]{:S(2)}) async-start(f32[32,1,1664]{2,1,0:T(1,128)} %get-tuple-element.157), calls=%async_computation.3 | async-start | bytes 425984 | tf_op jit(solution)/shard_map/all_to_all | solution.py:919
  118.7 4.6 %all-to-all-done.3.got = f32[32,1,1664]{2,1,0:T(1,128)} async-done(((f32[32,1,1664]{2,1,0:T(1,128)}), f32[32,1,1664]{2,1,0:T(1,128)}, u32[]{:S(2)}, u32[]{:S(2)}) %all-to-all-start.3) | async-done | bytes 213024 | tf_op jit(solution)/shard_map/all_to_all | solution.py:919
  123.4 2.8 %collective-permute-done.21.got_a = f32[2,264,128]{2,1,0:T(8,128)S(1)} collective-permute-done((f32[2,264,128]{2,1,0:T(8,128)}, f32[2,264,128]{2,1,0:T(8,128)S(1)}, u32[]{:S(2)}, u32[]{:S(2)}) %collective-permute-start.21) | collective-permute-done | bytes 270368 | tf_op jit(solution)/shard_map/ppermute | solution.py:936
  128.3 2.2 %collective-permute-start.24 = (f32[1,264,128]{2,1,0:T(8,128)S(1)}, f32[1,264,128]{2,1,0:T(8,128)S(1)}, u32[]{:S(2)}, u32[]{:S(2)}) collective-permute-start(f32[1,264,128]{2,1,0:T(8,128)S(1)} %get-tuple-element.184), channel_id=1, source_target_pairs={{0,16},{4,20},{8,24},{12,28},{16,0},{20,4},{24,8},{28,12},{1,17},{... | collective-permute-start | bytes 405512 | tf_op jit(solution)/shard_map/ppermute | solution.py:936
  131.8 3.3 %shard_map.331 = (f32[4,4,32,384]{3,2,1,0:T(8,128)}, f32[144,148]{1,0:T(8,128)}, f32[144,148]{1,0:T(8,128)}, f32[144,148]{1,0:T(8,128)}, f32[1,24]{1,0:T(1,128)}...) custom-call(s32[4]{0:T(128)} %counts.13, f32[32,1,1664]{2,1,0:T(1,128)} %all-to-all-done.3.got, ...), custom_call_target="tpu_custom_call" | custom-call | bytes 3065552 | tf_op jit(solution)/shard_map/pallas_call | solution.py:42
  135.1 5.6 %collective-permute-done.24.refs_2_ = f32[1,264,128]{2,1,0:T(8,128)S(1)} collective-permute-done((f32[1,264,128]{2,1,0:T(8,128)S(1)}, f32[1,264,128]{2,1,0:T(8,128)S(1)}, u32[]{:S(2)}, u32[]{:S(2)}) %collective-permute-start.24) | collective-permute-done | bytes 135200 | tf_op jit(solution)/shard_map/ppermute | solution.py:936
  141.5 4.3 %collective-permute-done.26.beside = f32[1,264,128]{2,1,0:T(8,128)S(1)} collective-permute-done((f32[1,264,128]{2,1,0:T(8,128)S(1)}, f32[1,264,128]{2,1,0:T(8,128)S(1)}, u32[]{:S(2)}, u32[]{:S(2)}) %collective-permute-start.26) | collective-permute-done | bytes 135200 | tf_op jit(solution)/shard_map/ppermute | solution.py:940
  148.0 2.1 %shard_map.336 = (f32[192,432]{1,0:T(8,128)}, f32[192,432]{1,0:T(8,128)}, f32[192,432]{1,0:T(8,128)}, f32[192,216]{1,0:T(8,128)}, f32[192,216]{1,0:T(8,128)}, /*...) custom-call(f32[1,264,128]{2,1,0:T(8,128)S(1)} %shard_map.335.own, ...), custom_call_target="tpu_custom_call" | custom-call | bytes 3771104 | tf_op jit(solution)/shard_map/pallas_call | solution.py:42
  (122 shorter events, 23.9 us)
Async XLA Ops:
  3.5 7.4 %collective-permute-start.7 = (bf16[4,96,128]{2,1,0:T(8,128)(2,1)}, bf16[4,96,128]{2,1,0:T(8,128)(2,1)S(1)}, u32[]{:S(2)}, u32[]{:S(2)}) collective-permute-start(bf16[4,96,128]{2,1,0:T(8,128)(2,1)} %get-tuple-element.117), channel_id=1, source_target_pairs={{0,4},{4,0},{8,12},{12,8},{16,20},{20,16},{24,28},{28,24},{1,5},{5... | collective-permute-start | bytes 294920 | tf_op jit(solution)/shard_map/ppermute | solution.py:931
  6.6 9.3 %collective-permute-start = (bf16[336,128]{1,0:T(8,128)(2,1)}, bf16[336,128]{1,0:T(8,128)(2,1)S(1)}, u32[]{:S(2)}, u32[]{:S(2)}) collective-permute-start(bf16[336,128]{1,0:T(8,128)(2,1)} %get-tuple-element.113), channel_id=1, source_target_pairs={{0,8},{4,12},{8,0},{12,4},{16,24},{20,28},{24,16},{28,20},{1,9},{5... | collective-permute-start | bytes 258056 | tf_op jit(solution)/shard_map/ppermute | solution.py:936
  8.2 9.4 %collective-permute-start.1 = (bf16[336,128]{1,0:T(8,128)(2,1)}, bf16[336,128]{1,0:T(8,128)(2,1)S(1)}, u32[]{:S(2)}, u32[]{:S(2)}) collective-permute-start(bf16[336,128]{1,0:T(8,128)(2,1)} %get-tuple-element.113), channel_id=1, source_target_pairs={{0,16},{4,20},{8,24},{12,28},{16,0},{20,4},{24,8},{28,12},{1,17},{... | collective-permute-start | bytes 258056 | tf_op jit(solution)/shard_map/ppermute | solution.py:936
  10.7 6.9 %collective-permute-start.2 = (bf16[336,128]{1,0:T(8,128)(2,1)}, bf16[336,128]{1,0:T(8,128)(2,1)S(1)}, u32[]{:S(2)}, u32[]{:S(2)}) collective-permute-start(bf16[336,128]{1,0:T(8,128)(2,1)} %get-tuple-element.113), channel_id=1, source_target_pairs={{0,24},{4,28},{8,16},{12,20},{16,8},{20,12},{24,0},{28,4},{1,25},{... | collective-permute-start | bytes 258056 | tf_op jit(solution)/shard_map/ppermute | solution.py:936
  11.0 19.5 %all-to-all-start = ((f32[32,1,2048]{2,1,0:T(1,128)}), f32[32,1,2048]{2,1,0:T(1,128)S(1)}, u32[]{:S(2)}, u32[]{:S(2)}) async-start(f32[32,1,2048]{2,1,0:T(1,128)} %get-tuple-element.118), calls=%async_computation | async-start | bytes 524288 | tf_op jit(solution)/shard_map/all_to_all | solution.py:919
  18.5 15.4 %collective-permute-start.3 = (bf16[4,336,128]{2,1,0:T(8,128)(2,1)S(1)}, bf16[4,336,128]{2,1,0:T(8,128)(2,1)S(1)}, u32[]{:S(2)}, u32[]{:S(2)}) collective-permute-start(bf16[4,336,128]{2,1,0:T(8,128)(2,1)S(1)} %pad_maximum_fusion.mine_near), channel_id=1, source_target_pairs={{0,4},{4,0},{8,12},{12,8},{16,20},{20,16},{24,28},{28,24},{1,5},{5... | collective-permute-start | bytes 1032200 | tf_op jit(solution)/shard_map/ppermute | solution.py:936
  19.1 10.1 %collective-permute-start.5 = (bf16[208,128]{1,0:T(8,128)(2,1)}, bf16[208,128]{1,0:T(8,128)(2,1)S(1)}, u32[]{:S(2)}, u32[]{:S(2)}) collective-permute-start(bf16[208,128]{1,0:T(8,128)(2,1)} %get-tuple-element.115), channel_id=1, source_target_pairs={{0,16},{4,20},{8,24},{12,28},{16,0},{20,4},{24,8},{28,12},{1,17},{... | collective-permute-start | bytes 159752 | tf_op jit(solution)/shard_map/ppermute | solution.py:936
  21.6 7.6 %collective-permute-start.6 = (bf16[208,128]{1,0:T(8,128)(2,1)}, bf16[208,128]{1,0:T(8,128)(2,1)S(1)}, u32[]{:S(2)}, u32[]{:S(2)}) collective-permute-start(bf16[208,128]{1,0:T(8,128)(2,1)} %get-tuple-element.115), channel_id=1, source_target_pairs={{0,24},{4,28},{8,16},{12,20},{16,8},{20,12},{24,0},{28,4},{1,25},{... | collective-permute-start | bytes 159752 | tf_op jit(solution)/shard_map/ppermute | solution.py:936
  22.9 7.6 %collective-permute-start.8 = (bf16[4,96,128]{2,1,0:T(8,128)(2,1)}, bf16[4,96,128]{2,1,0:T(8,128)(2,1)S(1)}, u32[]{:S(2)}, u32[]{:S(2)}) collective-permute-start(bf16[4,96,128]{2,1,0:T(8,128)(2,1)} %get-tuple-element.119), channel_id=1, source_target_pairs={{4,8},{12,16},{20,24},{8,4},{16,12},{24,20},{5,9},{13,17},{21,25},... | collective-permute-start | bytes 294920 | tf_op jit(solution)/shard_map/ppermute | solution.py:931
  29.2 7.5 %collective-permute-start.11 = (bf16[4,336,128]{2,1,0:T(8,128)(2,1)S(1)}, bf16[4,336,128]{2,1,0:T(8,128)(2,1)S(1)}, u32[]{:S(2)}, u32[]{:S(2)}) collective-permute-start(bf16[4,336,128]{2,1,0:T(8,128)(2,1)S(1)} %pad_maximum_fusion.mine_near), channel_id=1, source_target_pairs={{0,1},{1,0},{2,3},{3,2},{4,5},{5,4},{6,7},{7,6},{8,9},{9,8},{10,11... | collective-permute-start | bytes 1032200 | tf_op jit(solution)/shard_map/ppermute | solution.py:923
  34.1 12.3 %collective-permute-start.9 = (bf16[4,208,128]{2,1,0:T(8,128)(2,1)S(1)}, bf16[4,208,128]{2,1,0:T(8,128)(2,1)S(1)}, u32[]{:S(2)}, u32[]{:S(2)}) collective-permute-start(bf16[4,208,128]{2,1,0:T(8,128)(2,1)S(1)} %pad_maximum_fusion.1.mine_near), channel_id=1, source_target_pairs={{0,4},{4,0},{8,12},{12,8},{16,20},{20,16},{24,28},{28,24},{1,5},{5... | collective-permute-start | bytes 638984 | tf_op jit(solution)/shard_map/ppermute | solution.py:936
  36.3 18.4 %collective-permute-start.14 = (bf16[4,208,128]{2,1,0:T(8,128)(2,1)S(1)}, bf16[4,208,128]{2,1,0:T(8,128)(2,1)S(1)}, u32[]{:S(2)}, u32[]{:S(2)}) collective-permute-start(bf16[4,208,128]{2,1,0:T(8,128)(2,1)S(1)} %pad_maximum_fusion.1.mine_near), channel_id=1, source_target_pairs={{0,1},{1,0},{2,3},{3,2},{4,5},{5,4},{6,7},{7,6},{8,9},{9,8},{10,11... | collective-permute-start | bytes 638984 | tf_op jit(solution)/shard_map/ppermute | solution.py:923
  36.4 9.9 %collective-permute-start.10 = (bf16[4,192,128]{2,1,0:T(8,128)(2,1)S(1)}, bf16[4,192,128]{2,1,0:T(8,128)(2,1)S(1)}, u32[]{:S(2)}, u32[]{:S(2)}) collective-permute-start(bf16[4,192,128]{2,1,0:T(8,128)(2,1)S(1)} %get-tuple-element.122), channel_id=1, source_target_pairs={{0,4},{4,0},{8,12},{12,8},{16,20},{20,16},{24,28},{28,24},{1,5},{5... | collective-permute-start | bytes 589832 | tf_op jit(solution)/shard_map/ppermute | solution.py:931
  46.3 8.3 %collective-permute-start.15 = (bf16[4,208,128]{2,1,0:T(8,128)(2,1)S(1)}, bf16[4,208,128]{2,1,0:T(8,128)(2,1)S(1)}, u32[]{:S(2)}, u32[]{:S(2)}) collective-permute-start(bf16[4,208,128]{2,1,0:T(8,128)(2,1)S(1)} %collective-permute-done.9.mine_far), channel_id=1, source_target_pairs={{0,1},{1,0},{2,3},{3,2},{4,5},{5,4},{6,7},{7,6},{8,9},{9,8},{10,11... | collective-permute-start | bytes 638984 | tf_op jit(solution)/shard_map/ppermute | solution.py:923
  46.3 8.3 %collective-permute-start.13 = (bf16[4,192,128]{2,1,0:T(8,128)(2,1)S(1)}, bf16[4,192,128]{2,1,0:T(8,128)(2,1)S(1)}, u32[]{:S(2)}, u32[]{:S(2)}) collective-permute-start(bf16[4,192,128]{2,1,0:T(8,128)(2,1)S(1)} %get-tuple-element.131), channel_id=1, source_target_pairs={{4,8},{12,16},{20,24},{8,4},{16,12},{24,20},{5,9},{13,17},{21,25},... | collective-permute-start | bytes 589832 | tf_op jit(solution)/shard_map/ppermute | solution.py:931
  47.0 17.0 %all-to-all-start.1 = ((f32[32,1,384]{2,1,0:T(1,128)}), f32[32,1,384]{2,1,0:T(1,128)S(1)}, u32[]{:S(2)}, u32[]{:S(2)}) async-start(f32[32,1,384]{2,1,0:T(1,128)} %get-tuple-element.126), calls=%async_computation.1 | async-start | bytes 98304 | tf_op jit(solution)/shard_map/all_to_all | solution.py:919
  100.5 15.2 %collective-permute-start.19 = (f32[2,2,264,128]{3,2,1,0:T(8,128)S(1)}, f32[2,2,264,128]{3,2,1,0:T(8,128)S(1)}, u32[]{:S(2)}, u32[]{:S(2)}) collective-permute-start(f32[2,2,264,128]{3,2,1,0:T(8,128)S(1)} %get-tuple-element.167), channel_id=1, source_target_pairs={{0,2},{2,0},{1,3},{3,1},{4,6},{6,4},{5,7},{7,5},{8,10},{10,8},{9,1... | collective-permute-start | bytes 1622024 | tf_op jit(solution)/shard_map/ppermute | solution.py:940
  101.0 14.6 %collective-permute-start.20 = (f32[2,2,264,128]{3,2,1,0:T(8,128)S(1)}, f32[2,2,264,128]{3,2,1,0:T(8,128)S(1)}, u32[]{:S(2)}, u32[]{:S(2)}) collective-permute-start(f32[2,2,264,128]{3,2,1,0:T(8,128)S(1)} %get-tuple-element.169), channel_id=1, source_target_pairs={{0,4},{4,0},{8,12},{12,8},{16,20},{20,16},{24,28},{28,24},{1,5},{5... | collective-permute-start | bytes 1622024 | tf_op jit(solution)/shard_map/ppermute | solution.py:936
  110.7 12.7 %all-to-all-start.3 = ((f32[32,1,1664]{2,1,0:T(1,128)}), f32[32,1,1664]{2,1,0:T(1,128)}, u32[]{:S(2)}, u32[]{:S(2)}) async-start(f32[32,1,1664]{2,1,0:T(1,128)} %get-tuple-element.157), calls=%async_computation.3 | async-start | bytes 425984 | tf_op jit(solution)/shard_map/all_to_all | solution.py:919
  116.6 9.6 %collective-permute-start.21 = (f32[2,264,128]{2,1,0:T(8,128)}, f32[2,264,128]{2,1,0:T(8,128)S(1)}, u32[]{:S(2)}, u32[]{:S(2)}) collective-permute-start(f32[2,264,128]{2,1,0:T(8,128)} %get-tuple-element.175), channel_id=1, source_target_pairs={{0,4},{4,0},{8,12},{12,8},{16,20},{20,16},{24,28},{28,24},{1,5},{5... | collective-permute-start | bytes 811016 | tf_op jit(solution)/shard_map/ppermute | solution.py:936
  118.2 8.5 %collective-permute-start.22 = (f32[2,264,128]{2,1,0:T(8,128)S(1)}, f32[2,264,128]{2,1,0:T(8,128)S(1)}, u32[]{:S(2)}, u32[]{:S(2)}) collective-permute-start(f32[2,264,128]{2,1,0:T(8,128)S(1)} %get-tuple-element.177), channel_id=1, source_target_pairs={{0,2},{2,0},{1,3},{3,1},{4,6},{6,4},{5,7},{7,5},{8,10},{10,8},{9,1... | collective-permute-start | bytes 811016 | tf_op jit(solution)/shard_map/ppermute | solution.py:940
  126.8 8.4 %collective-permute-start.23 = (f32[1,264,128]{2,1,0:T(8,128)S(1)}, f32[1,264,128]{2,1,0:T(8,128)S(1)}, u32[]{:S(2)}, u32[]{:S(2)}) collective-permute-start(f32[1,264,128]{2,1,0:T(8,128)S(1)} %get-tuple-element.183), channel_id=1, source_target_pairs={{0,8},{4,12},{8,0},{12,4},{16,24},{20,28},{24,16},{28,20},{1,9},{5... | collective-permute-start | bytes 405512 | tf_op jit(solution)/shard_map/ppermute | solution.py:936
  128.3 12.4 %collective-permute-start.24 = (f32[1,264,128]{2,1,0:T(8,128)S(1)}, f32[1,264,128]{2,1,0:T(8,128)S(1)}, u32[]{:S(2)}, u32[]{:S(2)}) collective-permute-start(f32[1,264,128]{2,1,0:T(8,128)S(1)} %get-tuple-element.184), channel_id=1, source_target_pairs={{0,16},{4,20},{8,24},{12,28},{16,0},{20,4},{24,8},{28,12},{1,17},{... | collective-permute-start | bytes 405512 | tf_op jit(solution)/shard_map/ppermute | solution.py:936
  130.5 10.2 %collective-permute-start.25 = (f32[1,264,128]{2,1,0:T(8,128)S(1)}, f32[1,264,128]{2,1,0:T(8,128)S(1)}, u32[]{:S(2)}, u32[]{:S(2)}) collective-permute-start(f32[1,264,128]{2,1,0:T(8,128)S(1)} %get-tuple-element.185), channel_id=1, source_target_pairs={{0,24},{4,28},{8,16},{12,20},{16,8},{20,12},{24,0},{28,4},{1,25},{... | collective-permute-start | bytes 405512 | tf_op jit(solution)/shard_map/ppermute | solution.py:936
  (38 other events, 659.1 us)
